TPU v7x, 32 devices: a whole 2x2x4 slice. The times are simulated.
32 devices in a mesh: batch: 16 (over z, y, x), tensor: 2 (over core).
Axes of the slice: x: 2, y: 2, z: 4, core: 2. Of those that a mesh axis runs over, the one named last changes fastest.
Arguments:
- hidden_in: bfloat16 [81920, 768], P(('batch', 'tensor')), may hold values from -6 to 6
- lengths: int32 [160, 8], P('batch'), may hold values from 1 to 256, 512 in all within a row
- attn_gain: float32 [768], replicated, may hold values from 0.1 to 1.9
- attn_query: bfloat16 [768, 768], P(None, 'tensor'), may hold values from -0.21875 to 0.21875
- attn_key: bfloat16 [768, 768], P(None, 'tensor'), may hold values from -0.21875 to 0.21875
- attn_value: bfloat16 [768, 768], P(None, 'tensor'), may hold values from -0.21875 to 0.21875
- attn_out: bfloat16 [768, 768], P('tensor'), may hold values from -1.75 to 1.75
- ffn_gain: float32 [768], replicated, may hold values from 0.1 to 1.9
- ffn_in: bfloat16 [768, 3072], P(None, 'tensor'), may hold values from -0.21875 to 0.21875
- ffn_out: bfloat16 [3072, 768], P('tensor'), may hold values from -0.109375 to 0.109375
- side_state: bfloat16 [81920, 96], P(('batch', 'tensor')), may hold values from -6 to 6
- gate_alpha: float32 [96], replicated, may hold values from -0.3 to 0.3
- down_w: bfloat16 [768, 96], replicated, may hold values from -0.21875 to 0.21875
- side_attn_gain: float32 [96], replicated, may hold values from 0.1 to 1.9
- side_query: bfloat16 [96, 96], replicated, may hold values from -0.625 to 0.625
- side_key: bfloat16 [96, 96], replicated, may hold values from -0.625 to 0.625
- side_value: bfloat16 [96, 96], replicated, may hold values from -0.625 to 0.625
- side_proj: bfloat16 [96, 96], replicated, may hold values from -3.5 to 3.5
- side_ffn_gain: float32 [96], replicated, may hold values from 0.1 to 1.9
- side_expand: bfloat16 [96, 384], replicated, may hold values from -0.625 to 0.625
- side_shrink: bfloat16 [384, 96], replicated, may hold values from -0.3125 to 0.3125
- cotangent: bfloat16 [81920, 96], P(('batch', 'tensor')), may hold values from -6 to 6
Outputs:
- backbone_out: bfloat16 [81920, 768], P(('batch', 'tensor'))
- side_out: float32 [81920, 96], P(('batch', 'tensor'))
- state_grad: float32 [81920, 96], P(('batch', 'tensor'))
- down_grad: float32 [768, 96], replicated
- alpha_grad: float32 [96], replicated
- attn_gain_grad: float32 [96], replicated
- query_weight_grad: float32 [96, 96], replicated
- key_weight_grad: float32 [96, 96], replicated
- value_weight_grad: float32 [96, 96], replicated
- proj_grad: float32 [96, 96], replicated
- ffn_gain_grad: float32 [96], replicated
- expand_grad: float32 [96, 384], replicated
- shrink_grad: float32 [384, 96], replicated
Inputs may be any that keep to these rules, and one draw needn't show every extreme that they name: Each row's 8 lengths add up to 512, and the longest of each row is exactly 256.
All inputs are finite; a program needn't handle non-finite values.
Results may differ from a plain program's by a relative error of at most 0.03.
Values may be sent and summed in bfloat16 or wider, within the bound.
No kernel may reach another device: no remote copies, remote signals or barrier semaphores. Data moves between devices by JAX's collectives and lax.ppermute only.
A program may use at most 128 MiB of HBM per device.

v0:
```python
import jax
import jax.numpy as jnp
from jax import lax
from jax.sharding import PartitionSpec as P

HEAD_DIM = 64
DS = 96
SIDE_HEADS = 12
SIDE_HEAD_DIM = 8
ROW_LEN = 512


epsilon = 1e-06


def inverse_rms(features):
    return lax.rsqrt(jnp.mean(features * features, axis=-1, keepdims=True) + epsilon)


def segment_ids(row_lengths):
    segment_ends = jnp.cumsum(row_lengths, axis=1)
    places = lax.broadcasted_iota(jnp.int32, (1, ROW_LEN, 1), 1)
    return jnp.sum((places >= segment_ends[:, None, :]).astype(jnp.int32), axis=2)


def contract_rows(first_operand, second_operand):
    return lax.dot_general(
        first_operand, second_operand, (((0,), (0,)), ((), ())), preferred_element_type=jnp.float32
    )


def times_transpose(first_operand, second_operand):
    return lax.dot_general(
        first_operand, second_operand, (((1,), (1,)), ((), ())), preferred_element_type=jnp.float32
    )


def project(normed, matrix):
    return jnp.dot(normed, matrix, preferred_element_type=jnp.float32).astype(jnp.bfloat16)


def masked_scores(query_row, key_row, segment_row, head_dim):
    scores = jnp.einsum(
        "qhd,khd->hqk", query_row, key_row, preferred_element_type=jnp.float32
    ) * head_dim ** (-0.5)
    same_doc = (segment_row[:, None] == segment_row[None, :])[None]
    return jnp.where(same_doc, scores, -1e30)


def frozen_attention(query_heads, key_heads, value_heads, segment):
    row_count = segment.shape[0]
    columns = query_heads.shape[1]
    split_shape = (row_count, ROW_LEN, columns // HEAD_DIM, HEAD_DIM)

    def one_row(element):
        scores = masked_scores(element[0], element[1], element[3], HEAD_DIM)
        raised = jnp.exp(scores - jnp.max(scores, axis=-1, keepdims=True))
        weights = (raised / jnp.sum(raised, axis=-1, keepdims=True)).astype(jnp.bfloat16)
        mixed = jnp.einsum("hqk,khd->qhd", weights, element[2], preferred_element_type=jnp.float32)
        return mixed.astype(jnp.bfloat16).reshape(ROW_LEN, columns)

    stacked = lax.map(
        one_row,
        (
            query_heads.reshape(split_shape),
            key_heads.reshape(split_shape),
            value_heads.reshape(split_shape),
            segment,
        ),
    )
    return stacked.reshape(row_count * ROW_LEN, columns)


def side_attention(query_heads, key_heads, value_heads, segment):
    row_count = segment.shape[0]
    split_shape = (row_count, ROW_LEN, SIDE_HEADS, SIDE_HEAD_DIM)

    def one_row(element):
        scores = masked_scores(element[0], element[1], element[3], SIDE_HEAD_DIM)
        row_max = jnp.max(scores, axis=-1, keepdims=True)
        raised = jnp.exp(scores - row_max)
        row_total = jnp.sum(raised, axis=-1, keepdims=True)
        weights = (raised / row_total).astype(jnp.bfloat16)
        mixed = jnp.einsum("hqk,khd->qhd", weights, element[2], preferred_element_type=jnp.float32)
        return (mixed.reshape(ROW_LEN, DS), (row_max + jnp.log(row_total))[:, :, 0])

    context, log_sums = lax.map(
        one_row,
        (
            query_heads.reshape(split_shape),
            key_heads.reshape(split_shape),
            value_heads.reshape(split_shape),
            segment,
        ),
    )
    return (context.reshape(row_count * ROW_LEN, DS), log_sums)


def side_attention_back(query_heads, key_heads, value_heads, segment, log_sums, context_grad):
    row_count = segment.shape[0]
    split_shape = (row_count, ROW_LEN, SIDE_HEADS, SIDE_HEAD_DIM)
    score_scale = SIDE_HEAD_DIM ** (-0.5)

    def one_row(element):
        query_row, key_row, value_row, segment_row, log_row, grad_row = element
        probability = jnp.exp(
            masked_scores(query_row, key_row, segment_row, SIDE_HEAD_DIM) - log_row[:, :, None]
        )
        value_grad = jnp.einsum(
            "hqk,qhd->khd",
            probability.astype(jnp.bfloat16),
            grad_row,
            preferred_element_type=jnp.float32,
        )
        prob_grad = jnp.einsum(
            "qhd,khd->hqk", grad_row, value_row, preferred_element_type=jnp.float32
        )
        centre = jnp.sum(probability * prob_grad, axis=-1, keepdims=True)
        score_grad = (probability * (prob_grad - centre)).astype(jnp.bfloat16)
        query_grad = (
            jnp.einsum("hqk,khd->qhd", score_grad, key_row, preferred_element_type=jnp.float32)
            * score_scale
        )
        key_grad = (
            jnp.einsum("hqk,qhd->khd", score_grad, query_row, preferred_element_type=jnp.float32)
            * score_scale
        )
        return tuple(
            (
                member.astype(jnp.bfloat16).reshape(ROW_LEN, DS)
                for member in (query_grad, key_grad, value_grad)
            )
        )

    results = lax.map(
        one_row,
        (
            query_heads.reshape(split_shape),
            key_heads.reshape(split_shape),
            value_heads.reshape(split_shape),
            segment,
            log_sums,
            context_grad.reshape(split_shape),
        ),
    )
    return tuple((member.reshape(row_count * ROW_LEN, DS) for member in results))


def body(
    hidden_in,
    lengths,
    attn_gain,
    attn_query,
    attn_key,
    attn_value,
    attn_out,
    ffn_gain,
    ffn_in,
    ffn_out,
    side_state,
    gate_alpha,
    down_w,
    side_attn_gain,
    side_query,
    side_key,
    side_value,
    side_proj,
    side_ffn_gain,
    side_expand,
    side_shrink,
    cotangent,
):
    residual = hidden_in.astype(jnp.float32)
    local_rows = residual.shape[0]
    own_count = local_rows // ROW_LEN
    group_segment = segment_ids(lengths)
    own_segment = lax.dynamic_slice_in_dim(
        group_segment, lax.axis_index("tensor") * own_count, own_count, 0
    )
    normed = (residual * inverse_rms(residual) * attn_gain).astype(jnp.bfloat16)
    local_cols = attn_query.shape[1]
    shard_rows = lax.all_gather(normed, "tensor", axis=0, tiled=True)
    projected = jnp.concatenate(
        (
            project(shard_rows, attn_query),
            project(shard_rows, attn_key),
            project(shard_rows, attn_value),
        ),
        axis=1,
    )
    context = frozen_attention(
        projected[:, :local_cols],
        projected[:, local_cols : 2 * local_cols],
        projected[:, 2 * local_cols :],
        group_segment,
    )
    middle = residual + lax.psum_scatter(
        jnp.dot(context, attn_out, preferred_element_type=jnp.float32).astype(jnp.bfloat16),
        "tensor",
        scatter_dimension=0,
        tiled=True,
    ).astype(jnp.float32)
    normed = (middle * inverse_rms(middle) * ffn_gain).astype(jnp.bfloat16)
    hidden = jax.nn.gelu(
        jnp.dot(
            lax.all_gather(normed, "tensor", axis=0, tiled=True),
            ffn_in,
            preferred_element_type=jnp.float32,
        )
    ).astype(jnp.bfloat16)
    backbone = (
        middle
        + lax.psum_scatter(
            jnp.dot(hidden, ffn_out, preferred_element_type=jnp.float32).astype(jnp.bfloat16),
            "tensor",
            scatter_dimension=0,
            tiled=True,
        ).astype(jnp.float32)
    ).astype(jnp.bfloat16)
    mixing = jax.nn.sigmoid(gate_alpha / 0.1)
    lowered = jnp.dot(backbone, down_w, preferred_element_type=jnp.float32)
    side_input = side_state.astype(jnp.float32)
    inputs = mixing * lowered + (1.0 - mixing) * side_input
    first_scale = inverse_rms(inputs)
    first_normed = (inputs * first_scale * side_attn_gain).astype(jnp.bfloat16)
    side_queries = project(first_normed, side_query)
    side_keys = project(first_normed, side_key)
    side_values = project(first_normed, side_value)
    side_context, log_sums = side_attention(side_queries, side_keys, side_values, own_segment)
    context_low = side_context.astype(jnp.bfloat16)
    middle_side = inputs + jnp.dot(context_low, side_proj, preferred_element_type=jnp.float32)
    second_scale = inverse_rms(middle_side)
    second_normed = (middle_side * second_scale * side_ffn_gain).astype(jnp.bfloat16)
    expanded = jnp.dot(second_normed, side_expand, preferred_element_type=jnp.float32)
    activated, gelu_back = jax.vjp(jax.nn.gelu, expanded)
    activated_low = activated.astype(jnp.bfloat16)
    side_out = middle_side + jnp.dot(activated_low, side_shrink, preferred_element_type=jnp.float32)
    upstream = cotangent.astype(jnp.float32)
    shrink_grad = contract_rows(activated_low, cotangent)
    activated_grad = times_transpose(cotangent, side_shrink)
    expanded_grad = gelu_back(activated_grad)[0].astype(jnp.bfloat16)
    expand_grad = contract_rows(second_normed, expanded_grad)
    second_grad = times_transpose(expanded_grad, side_expand)
    weighted = second_grad * side_ffn_gain
    ffn_gain_grad = jnp.sum(second_grad * middle_side * second_scale, axis=0)
    middle_grad = (
        upstream
        + second_scale * weighted
        - middle_side * second_scale**3 * jnp.mean(weighted * middle_side, axis=-1, keepdims=True)
    )
    branch_grad = middle_grad.astype(jnp.bfloat16)
    proj_grad = contract_rows(context_low, branch_grad)
    context_grad = times_transpose(branch_grad, side_proj).astype(jnp.bfloat16)
    query_grad, key_grad, value_grad = side_attention_back(
        side_queries, side_keys, side_values, own_segment, log_sums, context_grad
    )
    query_weight_grad = contract_rows(first_normed, query_grad)
    key_weight_grad = contract_rows(first_normed, key_grad)
    value_weight_grad = contract_rows(first_normed, value_grad)
    first_grad = (
        times_transpose(query_grad, side_query)
        + times_transpose(key_grad, side_key)
        + times_transpose(value_grad, side_value)
    )
    weighted = first_grad * side_attn_gain
    attn_gain_grad = jnp.sum(first_grad * inputs * first_scale, axis=0)
    input_grad = (
        middle_grad
        + first_scale * weighted
        - inputs * first_scale**3 * jnp.mean(weighted * inputs, axis=-1, keepdims=True)
    )
    state_grad = (1.0 - mixing) * input_grad
    down_grad = contract_rows(backbone, (mixing * input_grad).astype(jnp.bfloat16))
    alpha_grad = (
        jnp.sum(input_grad * (lowered - side_input), axis=0) * mixing * (1.0 - mixing) / 0.1
    )
    summed = lax.psum(
        (
            down_grad,
            alpha_grad,
            attn_gain_grad,
            query_weight_grad,
            key_weight_grad,
            value_weight_grad,
            proj_grad,
            ffn_gain_grad,
            expand_grad,
            shrink_grad,
        ),
        ("batch", "tensor"),
    )
    return (
        backbone,
        side_out,
        state_grad,
        summed[0],
        summed[1],
        summed[2],
        summed[3],
        summed[4],
        summed[5],
        summed[6],
        summed[7],
        summed[8],
        summed[9],
    )


def solution(mesh):
    return jax.shard_map(
        body,
        mesh=mesh,
        in_specs=(
            P(("batch", "tensor"), None),
            P("batch", None),
            P(),
            P(None, "tensor"),
            P(None, "tensor"),
            P(None, "tensor"),
            P("tensor", None),
            P(),
            P(None, "tensor"),
            P("tensor", None),
            P(("batch", "tensor"), None),
            P(),
            P(),
            P(),
            P(),
            P(),
            P(),
            P(),
            P(),
            P(),
            P(),
            P(("batch", "tensor"), None),
        ),
        out_specs=(
            P(("batch", "tensor"), None),
            P(("batch", "tensor"), None),
            P(("batch", "tensor"), None),
            P(),
            P(),
            P(),
            P(),
            P(),
            P(),
            P(),
            P(),
            P(),
            P(),
        ),
        check_vma=False,
    )
```

profile of v0, /device:TPU:0, one launch (start us, length us, event | category | flops | bytes accessed | tf_op | source)
XLA Modules:
  0.0 864.0 jit_solution(8512598113446087915)
XLA Ops:
  14.3 21.6 %all-gather.3.cloned.1.call-done = bf16[5120,768]{1,0:T(8,128)(2,1)} async-done(((bf16[2560,768]{1,0:T(8,128)(2,1)}), bf16[5120,768]{1,0:T(8,128)(2,1)}) %all-gather.3.cloned.1.call-update) | async-done | bytes 7864336 | tf_op jit(solution)/shard_map/all_gather | solution.py:182
  35.9 9.4 %convolution_convert_fusion.4 = bf16[5120,384]{1,0:T(8,128)(2,1)} fusion(bf16[5120,768]{1,0:T(8,128)(2,1)} %all-gather.3.cloned.1.call-done, bf16[768,384]{1,0:T(8,128)(2,1)S(1)} %copy-done.44), kind=kOutput, calls=%fused_computation.117 | convolution fusion | flops 3021864960 | bytes 12386304 | tf_op jit(solution)/shard_map/dot_general | solution.py:39
  45.3 13.3 %reshape.267 = bf16[10,512,6,64]{3,2,1,0:T(8,128)(2,1)} reshape(bf16[5120,384]{1,0:T(8,128)(2,1)} %convolution_convert_fusion.4) | data formatting | bytes 7864320 | tf_op jit(solution)/shard_map/reshape | solution.py:67
  58.6 11.2 %copy.84 = bf16[10,512,6,64]{1,3,2,0:T(8,128)(2,1)} copy(bf16[10,512,6,64]{3,2,1,0:T(8,128)(2,1)} %reshape.267) | data formatting | bytes 7864320 | tf_op jit(solution)/shard_map/while | solution.py:62
  69.8 9.5 %convolution_convert_fusion.3 = bf16[5120,384]{1,0:T(8,128)(2,1)} fusion(bf16[5120,768]{1,0:T(8,128)(2,1)} %all-gather.3.cloned.1.call-done, bf16[768,384]{1,0:T(8,128)(2,1)S(1)} %copy-done.45), kind=kOutput, calls=%fused_computation.116 | convolution fusion | flops 3021864960 | bytes 12386304 | tf_op jit(solution)/shard_map/dot_general | solution.py:39
  79.3 12.9 %reshape.268 = bf16[10,512,6,64]{3,2,1,0:T(8,128)(2,1)} reshape(bf16[5120,384]{1,0:T(8,128)(2,1)} %convolution_convert_fusion.3) | data formatting | bytes 7864320 | tf_op jit(solution)/shard_map/reshape | solution.py:65
  92.2 11.2 %copy.85 = bf16[10,512,6,64]{1,3,2,0:T(8,128)(2,1)} copy(bf16[10,512,6,64]{3,2,1,0:T(8,128)(2,1)} %reshape.268) | data formatting | bytes 7864320 | tf_op jit(solution)/shard_map/while | solution.py:62
  103.3 9.5 %convolution_convert_fusion.2 = bf16[5120,384]{1,0:T(8,128)(2,1)} fusion(bf16[5120,768]{1,0:T(8,128)(2,1)} %all-gather.3.cloned.1.call-done, bf16[768,384]{1,0:T(8,128)(2,1)S(1)} %copy-done.46), kind=kOutput, calls=%fused_computation.115 | convolution fusion | flops 3021864960 | bytes 12386304 | tf_op jit(solution)/shard_map/dot_general | solution.py:39
  112.8 12.9 %reshape.269 = bf16[10,512,6,64]{3,2,1,0:T(8,128)(2,1)} reshape(bf16[5120,384]{1,0:T(8,128)(2,1)} %convolution_convert_fusion.2) | data formatting | bytes 7864320 | tf_op jit(solution)/shard_map/reshape | solution.py:66
  125.7 11.1 %copy.86 = bf16[10,512,6,64]{1,3,2,0:T(8,128)(2,1)} copy(bf16[10,512,6,64]{3,2,1,0:T(8,128)(2,1)} %reshape.269) | data formatting | bytes 7864320 | tf_op jit(solution)/shard_map/while | solution.py:62
  136.7 110.5 %while.36 = (s32[]{:T(128)}, bf16[10,512,384]{2,1,0:T(8,128)(2,1)}, bf16[10,512,6,64]{1,3,2,0:T(8,128)(2,1)}, s32[10,512]{1,0:T(8,128)S(1)}, bf16[10,512,6,64]{1...) while((s32[]{:T(128)}, bf16[10,512,384]{2,1,0:T(8,128)(2,1)}, ...), condition=%wide.region_6.7_spmd, body=%wide.region_3.6_spmd.sunk | while | flops 412549632 | bytes 16284769 | solution.py:62
  159.2 6.2 fusion.214
  192.3 6.2 fusion.214
  247.3 9.6 %convolution_convert_fusion.1 = bf16[5120,768]{1,0:T(8,128)(2,1)} fusion(bf16[5120,384]{1,0:T(8,128)(2,1)} %bitcast.221, bf16[384,768]{1,0:T(8,128)(2,1)} %param.34), kind=kOutput, calls=%fused_computation.108 | convolution fusion | flops 3023831040 | bytes 12386304 | tf_op jit(solution)/shard_map/dot_general | solution.py:198
  256.9 17.8 %reduce-scatter.3.cloned.1.call-done = bf16[2560,768]{1,0:T(8,128)(2,1)} async-done(((bf16[5120,768]{1,0:T(8,128)(2,1)}), bf16[2560,768]{1,0:T(8,128)(2,1)}) %reduce-scatter.3.cloned.1.call-update) | async-done | bytes 3932176 | tf_op jit(solution)/shard_map/reduce_scatter | solution.py:197
  283.4 20.4 %all-gather.5.cloned.1.call-done = bf16[5120,768]{1,0:T(8,128)(2,1)} async-done(((bf16[2560,768]{1,0:T(8,128)(2,1)}), bf16[5120,768]{1,0:T(8,128)(2,1)}) %all-gather.5.cloned.1.call-update) | async-done | bytes 7864336 | tf_op jit(solution)/shard_map/all_gather | solution.py:206
  303.8 31.7 %convolution_convert_fusion = bf16[5120,768]{1,0:T(8,128)(2,1)} fusion(bf16[1536,768]{1,0:T(8,128)(2,1)S(1)} %copy-done, bf16[5120,768]{1,0:T(8,128)(2,1)} %all-gather.5.cloned.1.call-done, bf16[768,1536]{1,0:T(8,128)(2,1)} %param.36), kind=kOutput, calls=%fused_computation.107 | convolution fusion | flops 24233902080 | bytes 20447232 | tf_op jit(solution)/shard_map/dot_general | solution.py:214
  336.2 17.1 %reduce-scatter.5.cloned.1.call-done = bf16[2560,768]{1,0:T(8,128)(2,1)} async-done(((bf16[5120,768]{1,0:T(8,128)(2,1)}), bf16[2560,768]{1,0:T(8,128)(2,1)}) %reduce-scatter.5.cloned.1.call-update) | async-done | bytes 3932176 | tf_op jit(solution)/shard_map/reduce_scatter | solution.py:213
  363.6 45.9 %while.37 = (s32[]{:T(128)}, bf16[5,512,96]{1,2,0:T(8,128)(2,1)}, f32[5,12,512]{2,1,0:T(8,128)S(1)}, bf16[5,512,12,8]{1,3,2,0:T(8,128)(2,1)S(1)}, s32[5,512]{1,0...) while((s32[]{:T(128)}, bf16[5,512,96]{1,2,0:T(8,128)(2,1)}, ...), condition=%wide.region_14.15_spmd, body=%wide.region_11.14_spmd.sunk | while | flops 138668032 | bytes 39534692 | solution.py:87
  423.7 136.6 %while.38 = (s32[]{:T(128)}, bf16[5,512,96]{1,2,0:T(8,128)(2,1)}, bf16[5,512,96]{1,2,0:T(8,128)(2,1)}, bf16[5,512,96]{1,2,0:T(8,128)(2,1)}, bf16[5,512,12,8]{1,3...) while((s32[]{:T(128)}, bf16[5,512,96]{1,2,0:T(8,128)(2,1)}, ...), condition=%wide.region_19.20_spmd, body=%wide.region_17.19_spmd.sunk | while | flops 299345920 | bytes 96603264 | solution.py:135
  430.8 7.7 multiply_reduce_fusion.9
  438.5 7.0 multiply_convert_fusion.10
  458.1 7.7 multiply_reduce_fusion.9
  465.7 7.0 multiply_convert_fusion.10
  485.3 7.7 multiply_reduce_fusion.9
  493.0 7.0 multiply_convert_fusion.10
  512.6 7.7 multiply_reduce_fusion.9
  520.3 7.0 multiply_convert_fusion.10
  539.9 7.7 multiply_reduce_fusion.9
  547.6 7.0 multiply_convert_fusion.10
  583.9 121.4 %all-reduce.5.cloned.1.call-done = (f32[96]{0:T(128)}, f32[96]{0:T(128)}, f32[96,96]{1,0:T(8,128)}, f32[96,96]{1,0:T(8,128)}, f32[96,96]{1,0:T(8,128)}, /*index=5*/f32[96,96]{1,0:T(8,128)}, f32[96]{0:T(128)}) async-done(((f32[96]{0:T(128)}, f32[96]{0:T(128)}, f32[96,96]{1,0:T(8,128)}, f32[96,96]{1,0:T(8,128)}, f32[96,96]{1,0:T(8,128)}, /*index=5*/f32[96,96]{1,0:T(8,128)}, f32[96]{0:T(128)}), (f32[96]{0:T(128)}, ...) | async-done | bytes 148624 | tf_op jit(solution)/shard_map/psum | solution.py:277
  705.4 137.6 %all-reduce.7.cloned.1.call-done = (f32[768,96]{0,1:T(8,128)}, f32[96,384]{1,0:T(8,128)}, f32[384,96]{0,1:T(8,128)}) async-done(((f32[768,96]{0,1:T(8,128)}, f32[96,384]{1,0:T(8,128)}, f32[384,96]{0,1:T(8,128)}), (f32[768,96]{0,1:T(8,128)}, f32[96,384]{1,0:T(8,128)}, f32[384,96]{0,1:T(8,128)})) %all-reduce.7.cloned.1.call-update) | async-done | bytes 589840 | tf_op jit(solution)/shard_map/psum | solution.py:277
  (295 shorter events, 283.8 us)
Async XLA Ops:
  7.2 296.6 %copy-start = (bf16[1536,768]{1,0:T(8,128)(2,1)S(1)}, bf16[1536,768]{1,0:T(8,128)(2,1)}, u32[]{:S(2)}) copy-start(bf16[1536,768]{1,0:T(8,128)(2,1)} %param.37) | copy-start | bytes 7077892
  7.2 28.7 %all-gather.3.cloned.1.call-start = ((), (), s32[]{:S(2)}) async-start(), calls=%async_computation.2 | async-start | bytes 11796480 | tf_op jit(solution)/shard_map/all_gather | solution.py:182
  10.4 25.5 %copy-start.44 = (bf16[768,384]{1,0:T(8,128)(2,1)S(1)}, bf16[768,384]{1,0:T(8,128)(2,1)}, u32[]{:S(2)}) copy-start(bf16[768,384]{1,0:T(8,128)(2,1)} %param.33) | copy-start | bytes 1769476
  14.0 260.7 %reduce-scatter.3.cloned.1.call-start = ((), (), s32[]{:S(2)}) async-start(), calls=%async_computation.3 | async-start | bytes 11796480 | tf_op jit(solution)/shard_map/reduce_scatter | solution.py:197
  58.6 11.2 %copy-start.45 = (bf16[768,384]{1,0:T(8,128)(2,1)S(1)}, bf16[768,384]{1,0:T(8,128)(2,1)}, u32[]{:S(2)}) copy-start(bf16[768,384]{1,0:T(8,128)(2,1)} %param.31) | copy-start | bytes 1769476
  92.2 11.2 %copy-start.46 = (bf16[768,384]{1,0:T(8,128)(2,1)S(1)}, bf16[768,384]{1,0:T(8,128)(2,1)}, u32[]{:S(2)}) copy-start(bf16[768,384]{1,0:T(8,128)(2,1)} %param.32) | copy-start | bytes 1769476
  256.8 22.7 %copy-start.42 = (f32[768]{0:T(1024)S(1)}, f32[768]{0:T(1024)}, u32[]{:S(2)}) copy-start(f32[768]{0:T(1024)} %param.35) | copy-start | bytes 9220
  256.9 47.0 %all-gather.5.cloned.1.call-start = ((), (), s32[]{:S(2)}) async-start(), calls=%async_computation.4 | async-start | bytes 11796480 | tf_op jit(solution)/shard_map/all_gather | solution.py:206
  283.4 70.0 %reduce-scatter.5.cloned.1.call-start = ((), (), s32[]{:S(2)}) async-start(), calls=%async_computation.5 | async-start | bytes 11796480 | tf_op jit(solution)/shard_map/reduce_scatter | solution.py:213
  335.5 369.8 %all-reduce.5.cloned.1.call-start = ((), (), s32[]{:S(2)}) async-start(), calls=%async_computation.6 | async-start | bytes 396288 | tf_op jit(solution)/shard_map/psum | solution.py:277
  336.2 23.0 %copy-start.38 = (f32[96]{0:T(128)}, f32[96]{0:T(128)S(1)}, u32[]{:S(2)}) copy-start(f32[96]{0:T(128)S(1)} %get-tuple-element.276) | copy-start | bytes 1156
  336.2 23.1 %copy-start.40 = (f32[96]{0:T(128)}, f32[96]{0:T(128)S(1)}, u32[]{:S(2)}) copy-start(f32[96]{0:T(128)S(1)} %get-tuple-element.277) | copy-start | bytes 1156
  336.2 23.1 %copy-start.17 = (bf16[2560,96]{0,1:T(8,128)(2,1)S(1)}, bf16[2560,96]{0,1:T(8,128)(2,1)}, u32[]{:S(2)}) copy-start(bf16[2560,96]{0,1:T(8,128)(2,1)} %param.38) | copy-start | bytes 1474564
  336.2 23.0 %copy-start.23 = (bf16[768,96]{0,1:T(8,128)(2,1)S(1)}, bf16[768,96]{0,1:T(8,128)(2,1)}, u32[]{:S(2)}) copy-start(bf16[768,96]{0,1:T(8,128)(2,1)} %param.40) | copy-start | bytes 442372
  361.6 50.5 %copy-start.7 = (f32[2560,96]{0,1:T(8,128)}, f32[2560,96]{0,1:T(8,128)S(1)}, u32[]{:S(2)}) copy-start(f32[2560,96]{0,1:T(8,128)S(1)} %get-tuple-element.275) | copy-start | bytes 2949124
  363.6 48.5 %copy-start.30 = (bf16[96,96]{1,0:T(8,128)(2,1)S(1)}, bf16[96,96]{1,0:T(8,128)(2,1)}, u32[]{:S(2)}) copy-start(bf16[96,96]{1,0:T(8,128)(2,1)} %param.45) | copy-start | bytes 55300
  363.6 50.0 %copy-start.31 = (bf16[96,384]{1,0:T(8,128)(2,1)S(1)}, bf16[96,384]{1,0:T(8,128)(2,1)}, u32[]{:S(2)}) copy-start(bf16[96,384]{1,0:T(8,128)(2,1)} %param.47) | copy-start | bytes 221188
  363.6 50.0 %copy-start.35 = (f32[96]{0:T(128)S(1)}, f32[96]{0:T(128)}, u32[]{:S(2)}) copy-start(f32[96]{0:T(128)} %param.46) | copy-start | bytes 1156
  409.5 6.9 copy-start.12
  423.7 138.1 %copy-start.10 = (bf16[2560,96]{0,1:T(8,128)(2,1)S(1)}, bf16[2560,96]{0,1:T(8,128)(2,1)}, u32[]{:S(2)}) copy-start(bf16[2560,96]{0,1:T(8,128)(2,1)} %copy-done.9) | copy-start | bytes 1474564
  423.7 139.0 %copy-start.29 = (bf16[96,96]{1,0:T(8,128)(2,1)S(1)}, bf16[96,96]{1,0:T(8,128)(2,1)}, u32[]{:S(2)}) copy-start(bf16[96,96]{1,0:T(8,128)(2,1)} %param.42) | copy-start | bytes 55300
  560.3 8.3 copy-start.25
  560.3 10.4 %copy-start.8 = (f32[2560,96]{0,1:T(8,128)S(1)}, f32[2560,96]{0,1:T(8,128)}, u32[]{:S(2)}) copy-start(f32[2560,96]{0,1:T(8,128)} %copy-done.7) | copy-start | bytes 2949124
  560.3 10.4 %copy-start.22 = (f32[2560]{0:T(1024)S(1)}, f32[2560]{0:T(1024)}, u32[]{:S(2)}) copy-start(f32[2560]{0:T(1024)} %copy-done.21) | copy-start | bytes 30724
  560.3 10.4 %copy-start.27 = (bf16[96,96]{1,0:T(8,128)(2,1)S(1)}, bf16[96,96]{1,0:T(8,128)(2,1)}, u32[]{:S(2)}) copy-start(bf16[96,96]{1,0:T(8,128)(2,1)} %param.44) | copy-start | bytes 55300
  560.3 10.4 %copy-start.37 = (f32[96]{0:T(128)S(1)}, f32[96]{0:T(128)}, u32[]{:S(2)}) copy-start(f32[96]{0:T(128)} %param.41) | copy-start | bytes 1156
  562.7 10.2 %copy-start.34 = (f32[2560]{0:T(1024)S(1)}, f32[2560]{0:T(1024)}, u32[]{:S(2)}) copy-start(f32[2560]{0:T(1024)} %get-tuple-element.284) | copy-start | bytes 30724
  567.7 6.9 copy-start.5
  567.7 6.9 copy-start.41
  574.6 6.1 copy-start.33
  574.6 282.3 %copy-start.1 = (bf16[1536,768]{1,0:T(8,128)(2,1)S(1)}, bf16[1536,768]{1,0:T(8,128)(2,1)}, u32[]{:S(2)}) copy-start(bf16[1536,768]{1,0:T(8,128)(2,1)} %param.37) | copy-start | bytes 7077892
  577.8 265.2 %all-reduce.7.cloned.1.call-start = ((), (), s32[]{:S(2)}) async-start(), calls=%async_computation.7 | async-start | bytes 1179648 | tf_op jit(solution)/shard_map/psum | solution.py:277
  (22 other events, 69.9 us)
Sparse Core Ops, SparseCore 0:
  14.1 21.7 all-gather.2
  257.0 17.6 reduce-scatter.2
  283.5 20.2 all-gather.4
  335.7 17.6 reduce-scatter.4
  577.9 127.4 all-reduce.4
  712.9 130.0 all-reduce.6
where the time goes:
time: 872 us; the launch traced here: 864 us
  waiting for transfers between devices  336 us (39%)
  matrix products  329 us (38%)
  local copies, waits for them, and re-layouts  105 us (12%)
  other arithmetic  77.1 us (9%)
  between operations  15 us (2%)
    psum x2, waiting for transfers between devices, body(): lax.psum((down_grad, alpha_grad, attn_gain_grad, query_weight_grad, key_w...  259 us
    sub x10, matrix products, one_row(): raised = jnp.exp(scores - jnp.max(scores, axis=-1, keepdims=True))  61.9 us
    dot_general x15, matrix products, one_row(): jnp.einsum('hqk,khd->qhd', weights, element[2], preferred_element_type=jn...  55.7 us
    dot_general x5, matrix products, one_row(): jnp.einsum('qhd,khd->hqk', grad_row, value_row, preferred_element_type=jn...  38.3 us
    convert_element_type x5, other arithmetic, one_row(): score_grad = (probability * (prob_grad - centre)).astype(jnp.bfloat16)  34.9 us
    while x3, local copies, waits for them, and re-layouts, frozen_attention(): lax.map(one_row, (query_heads.reshape(split_shape), key_heads.reshape(spl...  33.4 us
    dot_general x1, matrix products, body(): jnp.dot(hidden, ffn_out, preferred_element_type=jnp.float32)  31.7 us
    dot_general x6, matrix products, project(): jnp.dot(normed, matrix, preferred_element_type=jnp.float32)  29.3 us
  transfers between devices with their start and end apart: 6, of which 6 were waited for; matrix products, arithmetic and copies ran while one was open for 1% of the time, Pallas kernels for 0%

commit v1 on v0

v1 whole, which is shorter than its diff:
```python
import jax
import jax.numpy as jnp
from jax import lax
from jax.experimental import pallas as pl
from jax.experimental.pallas import tpu as pltpu
from jax.sharding import PartitionSpec as P

BF = jnp.bfloat16
F32 = jnp.float32
D = 768
HEAD_DIM = 64
DS = 96
SIDE_HEADS = 12
SIDE_HEAD_DIM = 8
SFF = 384
ROW_LEN = 512
SEGS = 8
HALF = 256
GRAD_LANES = 2048
LOG2E = 1.4426950408889634
EPS = 1e-06
VMEM_LIMIT = 63 * 1024 * 1024


def dot(a, b, ca=1, cb=0):
    return lax.dot_general(a, b, (((ca,), (cb,)), ((), ())), preferred_element_type=F32)


def gelu(x):
    x2 = x * x
    u = x * (x2 * (0.7978845608028654 * 0.044715) + 0.7978845608028654)
    h = 0.5 * x
    return h + h * jnp.tanh(u)


def gelu_and_slope(x):
    x2 = x * x
    u = x * (x2 * (0.7978845608028654 * 0.044715) + 0.7978845608028654)
    t = jnp.tanh(u)
    h = 0.5 * x
    du = 0.7978845608028654 * 3.0 * 0.044715 * x2 + 0.7978845608028654
    return h + h * t, 0.5 + 0.5 * t + h * (1.0 - t * t) * du


def row_starts(lens_ref, r):
    starts, begin = [], jnp.int32(0)
    long_start = jnp.int32(0)
    for j in range(SEGS):
        n = lens_ref[r * SEGS + j]
        starts.append((begin, n))
        long_start = jnp.where(n == HALF, begin, long_start)
        begin = begin + n
    return long_start, [((b - long_start) & (ROW_LEN - 1), n) for b, n in starts]


def fill_bias(bias_ref, docs):
    q = lax.broadcasted_iota(jnp.int32, (1, HALF), 1) + HALF
    low = jnp.zeros((1, HALF), jnp.int32)
    high = jnp.zeros((1, HALF), jnp.int32)
    for b, n in docs:
        inside = (q >= b) & (q < b + n)
        low = jnp.where(inside, b, low)
        high = jnp.where(inside, b + n, high)
    k = lax.broadcasted_iota(jnp.int32, (HALF, HALF), 0) + HALF
    bias_ref[...] = jnp.where((k >= low) & (k < high), 0.0, -1e30)


def turn_rows(src_ref, shift):
    n = src_ref.shape[1]
    part = shift & 7
    first = lax.shift_right_logical(shift, 3)
    groups = []
    for g in range(ROW_LEN // 8 + 1):
        start = pl.multiple_of(((first + g) & (ROW_LEN // 8 - 1)) * 8, 8)
        groups.append(src_ref[pl.ds(start, 8), :])
    wide = jnp.concatenate(groups, axis=0).reshape(ROW_LEN // 8 + 1, 8, n)
    back = (8 - part) & 7
    wide = pltpu.roll(wide, back, 1)
    place = lax.broadcasted_iota(jnp.int32, (ROW_LEN // 8, 8, n), 1)
    turned = jnp.where(place < 8 - part, wide[:-1], wide[1:])
    return turned.reshape(ROW_LEN, n)


def frozen_heads(normed, wqkv_ref, qkv_ref, vt_ref, ctxt_ref, bias_ref, wo):
    cols = wqkv_ref.shape[1] // 3
    pairs = cols // 128
    qkv_ref[...] = dot(normed, wqkv_ref[...]).astype(BF)
    vt_ref[...] = qkv_ref[:, 2 * cols :].T
    lane = lax.broadcasted_iota(jnp.int32, (1, 128), 1)
    keep = [(lane < 64).astype(F32).astype(BF), (lane >= 64).astype(F32).astype(BF)]
    for half in range(2):
        rows = slice(half * HALF, (half + 1) * HALF)
        for p in range(pairs):
            q2 = qkv_ref[rows, p * 128 : (p + 1) * 128]
            k2 = qkv_ref[rows, cols + p * 128 : cols + (p + 1) * 128]
            for j in range(2):
                s = dot(k2 * keep[j], q2, 1, 1) * (LOG2E / 8.0)
                if half:
                    s = s + bias_ref[...]
                e = jnp.exp2(s - jnp.max(s, axis=0, keepdims=True))
                inv = 1.0 / jnp.sum(e, axis=0, keepdims=True)
                hrow = slice(p * 128 + j * 64, p * 128 + (j + 1) * 64)
                mixed = dot(vt_ref[hrow, rows], e.astype(BF)) * inv
                ctxt_ref[hrow, rows] = mixed.astype(BF)
    return dot(ctxt_ref[...].T, wo)


def first_kernel(lens_ref, x_ref, gain_ref, wq_ref, wk_ref, wv_ref, wo_ref, normed_ref, mid_ref, wqkv_ref, qkv_ref, vt_ref, ctxt_ref, bias_ref, xf_ref):
    r = pl.program_id(0)
    cols = wq_ref.shape[1]

    @pl.when(r == 0)
    def _():
        wqkv_ref[:, :cols] = wq_ref[...]
        wqkv_ref[:, cols : 2 * cols] = wk_ref[...]
        wqkv_ref[:, 2 * cols :] = wv_ref[...]

    shift, docs = row_starts(lens_ref, r)
    fill_bias(bias_ref, docs)
    xf_ref[...] = x_ref[...].astype(F32)
    x = turn_rows(xf_ref, shift)
    xf_ref[...] = x
    normed = (x * lax.rsqrt(jnp.mean(x * x, axis=1, keepdims=True) + EPS) * gain_ref[...]).astype(BF)
    normed_ref[...] = normed
    mid_ref[...] = xf_ref[...] + frozen_heads(normed, wqkv_ref, qkv_ref, vt_ref, ctxt_ref, bias_ref, wo_ref[...])


def second_kernel(lens_ref, normed_ref, part_ref, wq_ref, wk_ref, wv_ref, wo_ref, mid_ref, wqkv_ref, qkv_ref, vt_ref, ctxt_ref, bias_ref):
    r = pl.program_id(0)
    cols = wq_ref.shape[1]

    @pl.when(r == 0)
    def _():
        wqkv_ref[:, :cols] = wq_ref[...]
        wqkv_ref[:, cols : 2 * cols] = wk_ref[...]
        wqkv_ref[:, 2 * cols :] = wv_ref[...]

    _, docs = row_starts(lens_ref, r)
    fill_bias(bias_ref, docs)
    mid_ref[...] = part_ref[...] + frozen_heads(normed_ref[...], wqkv_ref, qkv_ref, vt_ref, ctxt_ref, bias_ref, wo_ref[...])


def third_kernel(
    lens_ref,
    mid_ref,
    fgain_ref,
    w1a_ref,
    w1b_ref,
    w2a_ref,
    w2b_ref,
    side_ref,
    cot_ref,
    vecs_ref,
    downt_ref,
    sq_ref,
    sk_ref,
    sv_ref,
    proj_ref,
    expand_ref,
    shrinkt_ref,
    bb_ref,
    out_ref,
    state_ref,
    grads_ref,
    hid_ref,
    bias_ref,
    f_ref,
    cols_ref,
    wqkvt_ref,
    e_ref,
    ds_ref,
    inv_ref,
    ctxt_ref,
    dq_ref,
    qm_ref,
    acc_ref,
):
    r = pl.program_id(0)

    @pl.when(r == 0)
    def _():
        grads_ref[...] = jnp.zeros_like(grads_ref)
        acc_ref[...] = jnp.zeros_like(acc_ref)
        vt = vecs_ref[...].T
        for i in range(3):
            cols_ref[i] = jnp.broadcast_to(vt[:DS, i : i + 1], (DS, ROW_LEN))
        wqkvt_ref[:DS] = sq_ref[...].T
        wqkvt_ref[DS : 2 * DS] = sk_ref[...].T
        wqkvt_ref[2 * DS :] = sv_ref[...].T

    shift, docs = row_starts(lens_ref, r)
    fill_bias(bias_ref, docs)

    middle = mid_ref[...]
    normed = (middle * lax.rsqrt(jnp.mean(middle * middle, axis=1, keepdims=True) + EPS) * fgain_ref[...]).astype(BF)
    units = w1a_ref.shape[1]
    for i, w in enumerate((w1a_ref, w1b_ref)):
        for c in range(units // 256):
            hid_ref[:, i * units + c * 256 : i * units + (c + 1) * 256] = gelu(dot(normed, w[:, c * 256 : (c + 1) * 256])).astype(BF)
    f_ref[...] = mid_ref[...] + dot(hid_ref[:, :units], w2a_ref[...]) + dot(hid_ref[:, units:], w2b_ref[...])
    bb = f_ref[...].astype(BF)
    bb_ref[...] = turn_rows(f_ref, (ROW_LEN - shift) & (ROW_LEN - 1)).astype(BF)

    alpha = cols_ref[0]
    gain1 = cols_ref[1]
    gain2 = cols_ref[2]
    mixing = 1.0 / (1.0 + jnp.exp(alpha * -10.0))
    forward = (ROW_LEN - shift) & (ROW_LEN - 1)
    side = pltpu.roll(side_ref[...].astype(F32), forward, 1)
    cot = pltpu.roll(cot_ref[...].astype(F32), forward, 1)
    cotb = cot.astype(BF)
    lowered = dot(downt_ref[...], bb, 1, 1)
    inputs = mixing * lowered + (1.0 - mixing) * side
    scale1 = lax.rsqrt(jnp.mean(inputs * inputs, axis=0, keepdims=True) + EPS)
    fnt = (inputs * scale1 * gain1).astype(BF)
    qkvt = dot(wqkvt_ref[...], fnt).astype(BF)
    qt, kt, vt = qkvt[:DS], qkvt[DS : 2 * DS], qkvt[2 * DS :]
    lane = lax.broadcasted_iota(jnp.int32, (1, DS), 1)
    masks = [((lane >= 8 * h) & (lane < 8 * h + 8)).astype(F32).astype(BF) for h in range(SIDE_HEADS)]
    lane2 = lax.broadcasted_iota(jnp.int32, (1, 128), 1)
    masks2 = [
        (((lane2 >= 8 * h) & (lane2 < 8 * h + 8)) | (lane2 == DS + h) | (lane2 == DS + 16 + h)).astype(F32).astype(BF)
        for h in range(SIDE_HEADS)
    ]
    q, k, v = qt.T, kt.T, vt.T
    for half in range(2):
        rows = slice(half * HALF, (half + 1) * HALF)
        kh, qh = k[rows], qt[:, rows]
        for h in range(SIDE_HEADS):
            s = dot(kh * masks[h], qh) * (LOG2E * SIDE_HEAD_DIM**-0.5)
            if half:
                s = s + bias_ref[...]
            e = jnp.exp2(s - jnp.max(s, axis=0, keepdims=True))
            inv = 1.0 / jnp.sum(e, axis=0, keepdims=True)
            eb = e.astype(BF)
            e_ref[rows, h * HALF : (h + 1) * HALF] = eb
            mixed = dot(vt[16 * (h // 2) : 16 * (h // 2 + 1), rows], eb)
            low = 8 * (h % 2)
            ctxt_ref[8 * h : 8 * h + 8, rows] = mixed[low : low + 8] * inv
            inv_ref[8 * h : 8 * h + 8, rows] = jnp.broadcast_to(inv, (8, HALF))
    ctx = ctxt_ref[...]
    ctxb = ctx.astype(BF)
    middle_side = inputs + dot(proj_ref[...], ctxb, 0, 0)
    scale2 = lax.rsqrt(jnp.mean(middle_side * middle_side, axis=0, keepdims=True) + EPS)
    snt = (middle_side * scale2 * gain2).astype(BF)
    expanded = dot(expand_ref[...], snt, 0, 0)
    activated, slope = gelu_and_slope(expanded)
    activated = activated.astype(BF)
    side_out = middle_side + dot(shrinkt_ref[...], activated)
    out_ref[...] = pltpu.roll(side_out, shift, 1)

    activated_grad = dot(shrinkt_ref[...], cotb, 0, 0)
    expanded_grad = (activated_grad * slope).astype(BF)
    second_grad = dot(expand_ref[...], expanded_grad)
    w2 = second_grad * gain2
    ms = middle_side * scale2
    mean2 = jnp.mean(w2 * middle_side, axis=0, keepdims=True)
    middle_grad = cot + scale2 * w2 - ms * (scale2 * scale2) * mean2
    acc_ref[0] += second_grad * ms
    branch = middle_grad.astype(BF)
    context_grad = dot(proj_ref[...], branch).astype(BF).astype(F32)
    dop = (context_grad * inv_ref[...]).astype(BF)
    centre = jnp.sum((dop.astype(F32) * ctx).reshape(SIDE_HEADS, 8, ROW_LEN), axis=1)
    centre = jnp.concatenate([centre, jnp.zeros((4, ROW_LEN), F32)], axis=0)
    chigh = centre.astype(BF)
    clow = (centre - chigh.astype(F32)).astype(BF)
    dstack = jnp.concatenate([dop, -chigh, -clow], axis=0)
    vones = jnp.concatenate([v, jnp.ones((ROW_LEN, 32), BF)], axis=1)
    dopt = dop.T
    dks, dvs = [], []
    for half in range(2):
        rows = slice(half * HALF, (half + 1) * HALF)
        for h in range(SIDE_HEADS):
            cut = slice(h * HALF, (h + 1) * HALF)
            dp = dot(vones[rows] * masks2[h], dstack[:, rows])
            dsb = (e_ref[rows, cut].astype(F32) * dp).astype(BF)
            ds_ref[:, cut] = dsb
            mixed = dot(kt[16 * (h // 2) : 16 * (h // 2 + 1), rows], dsb)
            low = 8 * (h % 2)
            dq_ref[8 * h : 8 * h + 8, rows] = mixed[low : low + 8]
            qm_ref[0, cut, :] = q[rows] * masks[h]
            qm_ref[1, cut, :] = dopt[rows] * masks[h]
        dks.append(dot(ds_ref[...], qm_ref[0]))
        dvs.append(dot(e_ref[rows, :], qm_ref[1]))
    dqt = (dq_ref[...] * SIDE_HEAD_DIM**-0.5).astype(BF)
    dkt = (jnp.concatenate(dks, axis=0) * SIDE_HEAD_DIM**-0.5).astype(BF).T
    dvt = jnp.concatenate(dvs, axis=0).astype(BF).T
    dqkvt = jnp.concatenate([dqt, dkt, dvt], axis=0)
    first_grad = dot(wqkvt_ref[...], dqkvt, 0, 0)
    w1 = first_grad * gain1
    ins = inputs * scale1
    mean1 = jnp.mean(w1 * inputs, axis=0, keepdims=True)
    input_grad = middle_grad + scale1 * w1 - ins * (scale1 * scale1) * mean1
    acc_ref[1] += first_grad * ins
    acc_ref[2] += input_grad * (lowered - side)
    state_ref[...] = pltpu.roll((1.0 - mixing) * input_grad, shift, 1)
    grads_ref[:, 0:D] += dot((mixing * input_grad).astype(BF), bb)
    grads_ref[:, D : D + SFF] += dot(snt, expanded_grad, 1, 1)
    grads_ref[:, D + SFF : D + 2 * SFF] += dot(cotb, activated, 1, 1)
    low = D + 2 * SFF
    grads_ref[:, low : low + 3 * DS] += dot(fnt, dqkvt, 1, 1)
    grads_ref[:, low + 3 * DS : low + 4 * DS] += dot(ctxb, branch, 1, 1)

    @pl.when(r == pl.num_programs(0) - 1)
    def _():
        total = [jnp.sum(acc_ref[i], axis=1, keepdims=True) for i in range(3)]
        total[2] = total[2] * (mixing * (1.0 - mixing))[:, 0:1] * 10.0
        lane = lax.broadcasted_iota(jnp.int32, (DS, 128), 1)
        grads_ref[:, low + 4 * DS :] = jnp.where(lane == 0, total[0], jnp.where(lane == 1, total[1], jnp.where(lane == 2, total[2], 0.0)))


def whole(shape):
    return pl.BlockSpec(shape, lambda r, lens: (0,) * len(shape), pipeline_mode=pl.Buffered(1))


def params():
    return pltpu.CompilerParams(vmem_limit_bytes=VMEM_LIMIT, dimension_semantics=("arbitrary",))


def swap(x):
    return lax.ppermute(x, "tensor", [(0, 1), (1, 0)])


def sum_over(x, batch):
    t = lax.axis_index("tensor")
    h = x.shape[0] // 2
    x = x.astype(BF)
    mine = lax.dynamic_slice_in_dim(x, t * h, h, 0)
    other = lax.dynamic_slice_in_dim(x, (1 - t) * h, h, 0)
    part = mine.astype(F32) + swap(other).astype(F32)
    bit = 1
    while bit < batch:
        sent = part.astype(BF)
        got = lax.ppermute(sent, "batch", [(i, i ^ bit) for i in range(batch)])
        part = sent.astype(F32) + got.astype(F32)
        bit *= 2
    sent = part.astype(BF)
    got = swap(sent)
    return jnp.where(t == 0, jnp.concatenate([sent, got]), jnp.concatenate([got, sent])).astype(F32)


def make_body(batch):
    def body(
        hidden_in,
        lengths,
        attn_gain,
        attn_query,
        attn_key,
        attn_value,
        attn_out,
        ffn_gain,
        ffn_in,
        ffn_out,
        side_state,
        gate_alpha,
        down_w,
        side_attn_gain,
        side_query,
        side_key,
        side_value,
        side_proj,
        side_ffn_gain,
        side_expand,
        side_shrink,
        cotangent,
    ):
        tokens = hidden_in.shape[0]
        rows = tokens // ROW_LEN
        cols = attn_query.shape[1]
        units = ffn_in.shape[1]
        t = lax.axis_index("tensor")
        lens = lax.dynamic_slice_in_dim(lengths, t * rows, rows, 0).reshape(-1)
        far = [swap(w) for w in (attn_query, attn_key, attn_value, attn_out, ffn_in, ffn_out)]
        tile = pl.BlockSpec((ROW_LEN, D), lambda r, lens: (r, 0))
        scratch = [
            pltpu.VMEM((D, 3 * cols), BF),
            pltpu.VMEM((ROW_LEN, 3 * cols), BF),
            pltpu.VMEM((cols, ROW_LEN), BF),
            pltpu.VMEM((cols, ROW_LEN), BF),
            pltpu.VMEM((HALF, HALF), F32),
        ]
        attn_specs = [whole((D, cols))] * 3 + [whole((cols, D))]
        normed, mid = pl.pallas_call(
            first_kernel,
            grid_spec=pltpu.PrefetchScalarGridSpec(
                num_scalar_prefetch=1,
                grid=(rows,),
                in_specs=[tile, whole((1, D))] + attn_specs,
                out_specs=[tile, tile],
                scratch_shapes=scratch + [pltpu.VMEM((ROW_LEN, D), F32)],
            ),
            out_shape=[jax.ShapeDtypeStruct((tokens, D), BF), jax.ShapeDtypeStruct((tokens, D), F32)],
            compiler_params=params(),
            name="own_heads",
        )(lens, hidden_in, attn_gain.reshape(1, D), attn_query, attn_key, attn_value, attn_out)
        mid = pl.pallas_call(
            second_kernel,
            grid_spec=pltpu.PrefetchScalarGridSpec(
                num_scalar_prefetch=1,
                grid=(rows,),
                in_specs=[tile, tile] + attn_specs,
                out_specs=tile,
                scratch_shapes=scratch,
            ),
            out_shape=jax.ShapeDtypeStruct((tokens, D), F32),
            compiler_params=params(),
            name="far_heads",
        )(lens, normed, mid, *far[:4])
        vecs = jnp.zeros((8, 128), F32)
        vecs = vecs.at[0, :DS].set(gate_alpha).at[1, :DS].set(side_attn_gain).at[2, :DS].set(side_ffn_gain)
        side_tile = pl.BlockSpec((DS, ROW_LEN), lambda r, lens: (0, r))
        backbone, side_out, state_grad, grads = pl.pallas_call(
            third_kernel,
            grid_spec=pltpu.PrefetchScalarGridSpec(
                num_scalar_prefetch=1,
                grid=(rows,),
                in_specs=[
                    tile,
                    whole((1, D)),
                    whole((D, units)),
                    whole((D, units)),
                    whole((units, D)),
                    whole((units, D)),
                    side_tile,
                    side_tile,
                    whole((8, 128)),
                    whole((DS, D)),
                    whole((DS, DS)),
                    whole((DS, DS)),
                    whole((DS, DS)),
                    whole((DS, DS)),
                    whole((DS, SFF)),
                    whole((DS, SFF)),
                ],
                out_specs=[tile, side_tile, side_tile, pl.BlockSpec((DS, GRAD_LANES), lambda r, lens: (0, 0))],
                scratch_shapes=[
                    pltpu.VMEM((ROW_LEN, 2 * units), BF),
                    pltpu.VMEM((HALF, HALF), F32),
                    pltpu.VMEM((ROW_LEN, D), F32),
                    pltpu.VMEM((3, DS, ROW_LEN), F32),
                    pltpu.VMEM((3 * DS, DS), BF),
                    pltpu.VMEM((ROW_LEN, SIDE_HEADS * HALF), BF),
                    pltpu.VMEM((HALF, SIDE_HEADS * HALF), BF),
                    pltpu.VMEM((DS, ROW_LEN), F32),
                    pltpu.VMEM((DS, ROW_LEN), F32),
                    pltpu.VMEM((DS, ROW_LEN), F32),
                    pltpu.VMEM((2, SIDE_HEADS * HALF, DS), BF),
                    pltpu.VMEM((3, DS, ROW_LEN), F32),
                ],
            ),
            out_shape=[
                jax.ShapeDtypeStruct((tokens, D), BF),
                jax.ShapeDtypeStruct((DS, tokens), F32),
                jax.ShapeDtypeStruct((DS, tokens), F32),
                jax.ShapeDtypeStruct((DS, GRAD_LANES), F32),
            ],
            compiler_params=params(),
            name="forward_and_back",
        )(
            lens,
            mid,
            ffn_gain.reshape(1, D),
            ffn_in,
            far[4],
            ffn_out,
            far[5],
            side_state.T,
            cotangent.T,
            vecs,
            down_w.T,
            side_query,
            side_key,
            side_value,
            side_proj,
            side_expand,
            side_shrink.T,
        )
        g = sum_over(grads, batch)
        low = D + 2 * SFF
        return (
            backbone,
            side_out.T,
            state_grad.T,
            g[:, :D].T,
            g[:, low + 4 * DS + 2],
            g[:, low + 4 * DS + 1],
            g[:, low : low + DS],
            g[:, low + DS : low + 2 * DS],
            g[:, low + 2 * DS : low + 3 * DS],
            g[:, low + 3 * DS : low + 4 * DS],
            g[:, low + 4 * DS],
            g[:, D : D + SFF],
            g[:, D + SFF : low].T,
        )

    return body


def solution(mesh):
    split = P(("batch", "tensor"), None)
    return jax.shard_map(
        make_body(mesh.shape["batch"]),
        mesh=mesh,
        in_specs=(
            split,
            P("batch", None),
            P(),
            P(None, "tensor"),
            P(None, "tensor"),
            P(None, "tensor"),
            P("tensor", None),
            P(),
            P(None, "tensor"),
            P("tensor", None),
            split,
            P(),
            P(),
            P(),
            P(),
            P(),
            P(),
            P(),
            P(),
            P(),
            P(),
            split,
        ),
        out_specs=(split, split, split) + (P(),) * 10,
        check_vma=False,
    )
```

time: 872 us -> 225 us (0.26)
  matrix products: 329 us -> 0 us
  waiting for transfers between devices: 336 us -> 29.4 us
  Pallas kernels: 0 us -> 174 us
  local copies, waits for them, and re-layouts: 105 us -> 7.8 us
  other arithmetic: 77.1 us -> 1.49 us
  between operations: 15 us -> 0.8 us
  starting transfers between devices: 0.25 us -> 10.9 us
    dot_general x70 -> x0, matrix products: 267 us -> none  [the longest x15 55.7 us: one_row(): jnp.einsum('hqk,khd->qhd', weights, element[2], preferred_element_type=jn...]
    psum x2 -> x0, waiting for transfers between devices: 259 us -> none  [body(): lax.psum((down_grad, alpha_grad, attn_gain_grad, query_weight_grad, key_w...]
    pallas_call x0 -> x3, Pallas kernels: none -> 174 us  [the longest x1 114 us: body(): pl.pallas_call(third_kernel, grid_spec=pltpu.PrefetchScalarGridSpec(num_s...]
    sub x10 -> x0, matrix products: 61.9 us -> none  [one_row(): raised = jnp.exp(scores - jnp.max(scores, axis=-1, keepdims=True))]
    convert_element_type x9 -> x7, other arithmetic: 47.2 us -> 1.49 us  [the longest x1 1.18 us: sum_over(): x = x.astype(BF)]
    all_gather x2 -> x0, waiting for transfers between devices: 42 us -> none  [the longest x1 21.6 us: body(): shard_rows = lax.all_gather(normed, 'tensor', axis=0, tiled=True)]
    while x9 -> x0, local copies, waits for them, and re-layouts: 37.6 us -> none  [the longest x3 33.4 us: frozen_attention(): lax.map(one_row, (query_heads.reshape(split_shape), key_heads.reshape(spl...]
    reshape x3, local copies, waits for them, and re-layouts: 39.1 us -> 3.12 us  [the longest x1 1.27 us: body(): attn_gain.reshape(1, D)]
  transfers between devices with their start and end apart: 6 -> 12, of which waited for: 6 -> 7; matrix products, arithmetic and copies ran while one was open for 1% -> 2% of each run, Pallas kernels for 0% -> 27%
where the time goes in v1:
time: 225 us; the launch traced here: 224 us
  Pallas kernels  174 us (77%)
  waiting for transfers between devices  29.4 us (13%)
  starting transfers between devices  10.9 us (5%)
  local copies, waits for them, and re-layouts  7.8 us (3%)
    pallas_call x1, Pallas kernels, body(): pl.pallas_call(third_kernel, grid_spec=pltpu.PrefetchScalarGridSpec(num_s...  114 us
    pallas_call x1, Pallas kernels, body(): pl.pallas_call(first_kernel, grid_spec=pltpu.PrefetchScalarGridSpec(num_s...  30.8 us
    pallas_call x1, Pallas kernels, body(): pl.pallas_call(second_kernel, grid_spec=pltpu.PrefetchScalarGridSpec(num_...  29.4 us
    ppermute x4, waiting for transfers between devices, sum_over(): got = lax.ppermute(sent, 'batch', [(i, i ^ bit) for i in range(batch)])  21.6 us
    ppermute x4, starting transfers between devices, sum_over(): got = lax.ppermute(sent, 'batch', [(i, i ^ bit) for i in range(batch)])  8.71 us
    ppermute x8, waiting for transfers between devices, swap(): return lax.ppermute(x, 'tensor', [(0, 1), (1, 0)])  7.78 us
  transfers between devices with their start and end apart: 12, of which 7 were waited for; matrix products, arithmetic and copies ran while one was open for 2% of the time, Pallas kernels for 27%

profile of v1, /device:TPU:0, one launch (start us, length us, event | category | flops | bytes accessed | tf_op | source)
XLA Modules:
  0.0 224.5 jit_solution(15869451103879434255)
XLA Ops:
  0.7 0.5 collective-permute-start.4
  1.2 0.1 collective-permute-start.5
  1.3 0.4 collective-permute-start
  1.8 0.4 collective-permute-start.2
  2.2 5.0 %collective-permute-done.wq_ref = bf16[768,384]{1,0:T(8,128)(2,1)S(1)} collective-permute-done((bf16[768,384]{1,0:T(8,128)(2,1)}, bf16[768,384]{1,0:T(8,128)(2,1)S(1)}, u32[]{:S(2)}, u32[]{:S(2)}) %collective-permute-start) | collective-permute-done | bytes 589856 | tf_op jit(solution)/shard_map/ppermute | solution.py:321
  7.2 0.4 collective-permute-start.3
  7.7 0.1 copy.36
  7.8 0.6 reshape.123.lens_ref
  8.4 1.3 reshape.124.gain_ref
  9.6 1.3 reshape.125.fgain_ref
  10.9 0.7 scatter.10
  11.6 0.7 scatter.11
  12.3 30.8 %own_heads.1 = (bf16[2560,768]{1,0:T(8,128)(2,1)}, f32[2560,768]{1,0:T(8,128)}) custom-call(s32[40]{0:T(128)} %reshape.123.lens_ref, bf16[2560,768]{1,0:T(8,128)(2,1)} %x_ref.1, f32[1,768]{1,0:T(1,128)} %reshape.124.gain_ref, bf16[768,384]{1,0:T(8,128)(2,1)} %wq_ref.1, bf16[768,384]{1,0:T(8,128)(2,1)} %wk_ref.1, bf16[768,384]{1,0:T(8,128)(2,1)} %wv_ref.1, ...), custom_call_target="tpu_custom_call" | custom-call | tf_op jit(solution)/shard_map/own_heads/pallas_call | solution.py:383
  43.1 0.2 scatter.14.vecs_ref
  43.3 29.4 %far_heads.1.mid_ref = f32[2560,768]{1,0:T(8,128)} custom-call(s32[40]{0:T(128)} %reshape.123.lens_ref, bf16[2560,768]{1,0:T(8,128)(2,1)} %get-tuple-element.55.normed_ref, f32[2560,768]{1,0:T(8,128)} %get-tuple-element.56.part_ref, bf16[768,384]{1,0:T(8,128)(2,1)} %copy-done.1, bf16[768,384]{1,0:T(8,128)(2,1)} %collective-permute-done.1.wk_ref, ...), custom_call_target="tpu_custom_call" | custom-call | tf_op jit(solution)/shard_map/far_heads/pallas_call | solution.py:396
  72.7 113.9 %forward_and_back.1 = (bf16[2560,768]{1,0:T(8,128)(2,1)}, f32[96,2560]{1,0:T(8,128)}, f32[96,2560]{1,0:T(8,128)}, f32[96,2048]{1,0:T(8,128)}) custom-call(s32[40]{0:T(128)} %reshape.123.lens_ref, f32[2560,768]{1,0:T(8,128)} %far_heads.1.mid_ref, f32[1,768]{1,0:T(1,128)} %reshape.125.fgain_ref, bf16[768,1536]{1,0:T(8,128)(2,1)} %w1a_ref.1, ...), custom_call_target="tpu_custom_call" | custom-call | tf_op jit(solution)/shard_map/forward_and_back/pallas_call | solution.py:412
  186.7 1.2 convert_element_type.51
  187.9 0.2 collective-permute-start.6
  188.1 1.3 collective-permute-done.6
  189.5 2.7 %collective-permute-start.7 = (bf16[48,2048]{1,0:T(8,128)(2,1)S(1)}, bf16[48,2048]{1,0:T(8,128)(2,1)S(1)}, u32[]{:S(2)}, u32[]{:S(2)}) collective-permute-start(bf16[48,2048]{1,0:T(8,128)(2,1)S(1)} %add_convert_fusion.4), channel_id=1, source_target_pairs={{0,2},{2,0},{4,6},{6,4},{8,10},{10,8},{12,14},{14,12},{16,18},{18,... | collective-permute-start | bytes 589832 | tf_op jit(solution)/shard_map/ppermute | solution.py:334
  192.2 5.4 %collective-permute-done.7 = bf16[48,2048]{1,0:T(8,128)(2,1)S(1)} collective-permute-done((bf16[48,2048]{1,0:T(8,128)(2,1)S(1)}, bf16[48,2048]{1,0:T(8,128)(2,1)S(1)}, u32[]{:S(2)}, u32[]{:S(2)}) %collective-permute-start.7) | collective-permute-done | bytes 196640 | tf_op jit(solution)/shard_map/ppermute | solution.py:334
  197.7 1.8 collective-permute-start.8
  199.5 4.9 %collective-permute-done.8 = bf16[48,2048]{1,0:T(8,128)(2,1)S(1)} collective-permute-done((bf16[48,2048]{1,0:T(8,128)(2,1)S(1)}, bf16[48,2048]{1,0:T(8,128)(2,1)S(1)}, u32[]{:S(2)}, u32[]{:S(2)}) %collective-permute-start.8) | collective-permute-done | bytes 196640 | tf_op jit(solution)/shard_map/ppermute | solution.py:334
  204.4 1.6 collective-permute-start.9
  206.0 4.2 %collective-permute-done.9 = bf16[48,2048]{1,0:T(8,128)(2,1)S(1)} collective-permute-done((bf16[48,2048]{1,0:T(8,128)(2,1)S(1)}, bf16[48,2048]{1,0:T(8,128)(2,1)S(1)}, u32[]{:S(2)}, u32[]{:S(2)}) %collective-permute-start.9) | collective-permute-done | bytes 196640 | tf_op jit(solution)/shard_map/ppermute | solution.py:334
  210.2 2.6 %collective-permute-start.10 = (bf16[48,2048]{1,0:T(8,128)(2,1)S(1)}, bf16[48,2048]{1,0:T(8,128)(2,1)S(1)}, u32[]{:S(2)}, u32[]{:S(2)}) collective-permute-start(bf16[48,2048]{1,0:T(8,128)(2,1)S(1)} %add_convert_fusion.1), channel_id=1, source_target_pairs={{0,16},{2,18},{4,20},{6,22},{8,24},{10,26},{12,28},{14,30},{16,0},... | collective-permute-start | bytes 589832 | tf_op jit(solution)/shard_map/ppermute | solution.py:334
  212.8 7.1 %collective-permute-done.10 = bf16[48,2048]{1,0:T(8,128)(2,1)S(1)} collective-permute-done((bf16[48,2048]{1,0:T(8,128)(2,1)S(1)}, bf16[48,2048]{1,0:T(8,128)(2,1)S(1)}, u32[]{:S(2)}, u32[]{:S(2)}) %collective-permute-start.10) | collective-permute-done | bytes 196640 | tf_op jit(solution)/shard_map/ppermute | solution.py:334
  220.0 1.4 collective-permute-done.11
  221.5 0.7 slice_bitcast_fusion.1
  222.3 0.7 slice_bitcast_fusion
  223.0 0.7 fusion.1
  223.8 0.7 slice_reduce_fusion
  (23 shorter events, 0.6 us)
Async XLA Ops:
  0.6 7.0 %copy-start = (s32[10,8]{0,1:T(8,128)S(1)}, s32[10,8]{0,1:T(8,128)}, u32[]{:S(2)}) copy-start(s32[10,8]{0,1:T(8,128)} %param.29) | copy-start | bytes 964
  0.7 42.5 %copy-start.3 = (f32[96]{0:T(128)S(1)}, f32[96]{0:T(128)}, u32[]{:S(2)}) copy-start(f32[96]{0:T(128)} %param.46) | copy-start | bytes 1156
  0.7 72.0 %collective-permute-start.4 = (bf16[768,1536]{1,0:T(8,128)(2,1)}, bf16[768,1536]{1,0:T(8,128)(2,1)}, u32[]{:S(2)}, u32[]{:S(2)}) collective-permute-start(bf16[768,1536]{1,0:T(8,128)(2,1)} %w1a_ref.1), channel_id=1, source_target_pairs={{0,1},{1,0},{2,3},{3,2},{4,5},{5,4},{6,7},{7,6},{8,9},{9,8},{10,11... | collective-permute-start | bytes 7077896 | tf_op jit(solution)/shard_map/ppermute | solution.py:321
  1.2 71.5 %collective-permute-start.5 = (bf16[1536,768]{1,0:T(8,128)(2,1)}, bf16[1536,768]{1,0:T(8,128)(2,1)}, u32[]{:S(2)}, u32[]{:S(2)}) collective-permute-start(bf16[1536,768]{1,0:T(8,128)(2,1)} %w2a_ref.1), channel_id=1, source_target_pairs={{0,1},{1,0},{2,3},{3,2},{4,5},{5,4},{6,7},{7,6},{8,9},{9,8},{10,11... | collective-permute-start | bytes 7077896 | tf_op jit(solution)/shard_map/ppermute | solution.py:321
  1.3 6.0 %collective-permute-start = (bf16[768,384]{1,0:T(8,128)(2,1)}, bf16[768,384]{1,0:T(8,128)(2,1)S(1)}, u32[]{:S(2)}, u32[]{:S(2)}) collective-permute-start(bf16[768,384]{1,0:T(8,128)(2,1)} %wq_ref.1), channel_id=1, source_target_pairs={{0,1},{1,0},{2,3},{3,2},{4,5},{5,4},{6,7},{7,6},{8,9},{9,8},{10,11... | collective-permute-start | bytes 1769480 | tf_op jit(solution)/shard_map/ppermute | solution.py:321
  1.7 41.6 %collective-permute-start.1 = (bf16[768,384]{1,0:T(8,128)(2,1)}, bf16[768,384]{1,0:T(8,128)(2,1)}, u32[]{:S(2)}, u32[]{:S(2)}) collective-permute-start(bf16[768,384]{1,0:T(8,128)(2,1)} %wk_ref.1), channel_id=1, source_target_pairs={{0,1},{1,0},{2,3},{3,2},{4,5},{5,4},{6,7},{7,6},{8,9},{9,8},{10,11... | collective-permute-start | bytes 1769480 | tf_op jit(solution)/shard_map/ppermute | solution.py:321
  1.8 41.5 %collective-permute-start.2 = (bf16[768,384]{1,0:T(8,128)(2,1)}, bf16[768,384]{1,0:T(8,128)(2,1)}, u32[]{:S(2)}, u32[]{:S(2)}) collective-permute-start(bf16[768,384]{1,0:T(8,128)(2,1)} %wv_ref.1), channel_id=1, source_target_pairs={{0,1},{1,0},{2,3},{3,2},{4,5},{5,4},{6,7},{7,6},{8,9},{9,8},{10,11... | collective-permute-start | bytes 1769480 | tf_op jit(solution)/shard_map/ppermute | solution.py:321
  7.2 36.1 %copy-start.1 = (bf16[768,384]{1,0:T(8,128)(2,1)}, bf16[768,384]{1,0:T(8,128)(2,1)S(1)}, u32[]{:S(2)}) copy-start(bf16[768,384]{1,0:T(8,128)(2,1)S(1)} %collective-permute-done.wq_ref) | copy-start | bytes 1769476
  7.2 36.1 %collective-permute-start.3 = (bf16[384,768]{1,0:T(8,128)(2,1)}, bf16[384,768]{1,0:T(8,128)(2,1)}, u32[]{:S(2)}, u32[]{:S(2)}) collective-permute-start(bf16[384,768]{1,0:T(8,128)(2,1)} %wo_ref.1), channel_id=1, source_target_pairs={{0,1},{1,0},{2,3},{3,2},{4,5},{5,4},{6,7},{7,6},{8,9},{9,8},{10,11... | collective-permute-start | bytes 1769480 | tf_op jit(solution)/shard_map/ppermute | solution.py:321
  43.3 29.4 %copy-start.2 = (f32[8,128]{1,0:T(8,128)}, f32[8,128]{1,0:T(8,128)S(1)}, u32[]{:S(2)}) copy-start(f32[8,128]{1,0:T(8,128)S(1)} %scatter.14.vecs_ref) | copy-start | bytes 12292
  187.9 1.5 collective-permute-start.6
  189.5 8.1 %collective-permute-start.7 = (bf16[48,2048]{1,0:T(8,128)(2,1)S(1)}, bf16[48,2048]{1,0:T(8,128)(2,1)S(1)}, u32[]{:S(2)}, u32[]{:S(2)}) collective-permute-start(bf16[48,2048]{1,0:T(8,128)(2,1)S(1)} %add_convert_fusion.4), channel_id=1, source_target_pairs={{0,2},{2,0},{4,6},{6,4},{8,10},{10,8},{12,14},{14,12},{16,18},{18,... | collective-permute-start | bytes 589832 | tf_op jit(solution)/shard_map/ppermute | solution.py:334
  197.7 6.7 %collective-permute-start.8 = (bf16[48,2048]{1,0:T(8,128)(2,1)S(1)}, bf16[48,2048]{1,0:T(8,128)(2,1)S(1)}, u32[]{:S(2)}, u32[]{:S(2)}) collective-permute-start(bf16[48,2048]{1,0:T(8,128)(2,1)S(1)} %add_convert_fusion.3), channel_id=1, source_target_pairs={{0,4},{2,6},{4,0},{6,2},{8,12},{10,14},{12,8},{14,10},{16,20},{18,... | collective-permute-start | bytes 589832 | tf_op jit(solution)/shard_map/ppermute | solution.py:334
  204.4 5.8 %collective-permute-start.9 = (bf16[48,2048]{1,0:T(8,128)(2,1)S(1)}, bf16[48,2048]{1,0:T(8,128)(2,1)S(1)}, u32[]{:S(2)}, u32[]{:S(2)}) collective-permute-start(bf16[48,2048]{1,0:T(8,128)(2,1)S(1)} %add_convert_fusion.2), channel_id=1, source_target_pairs={{0,8},{2,10},{4,12},{6,14},{8,0},{10,2},{12,4},{14,6},{16,24},{18,... | collective-permute-start | bytes 589832 | tf_op jit(solution)/shard_map/ppermute | solution.py:334
  210.2 9.7 %collective-permute-start.10 = (bf16[48,2048]{1,0:T(8,128)(2,1)S(1)}, bf16[48,2048]{1,0:T(8,128)(2,1)S(1)}, u32[]{:S(2)}, u32[]{:S(2)}) collective-permute-start(bf16[48,2048]{1,0:T(8,128)(2,1)S(1)} %add_convert_fusion.1), channel_id=1, source_target_pairs={{0,16},{2,18},{4,20},{6,22},{8,24},{10,26},{12,28},{14,30},{16,0},... | collective-permute-start | bytes 589832 | tf_op jit(solution)/shard_map/ppermute | solution.py:334
  220.0 1.5 collective-permute-start.11

commit v2 on v1

v2 whole, which is shorter than its diff:
```python
import jax
import jax.numpy as jnp
from jax import lax
from jax.experimental import pallas as pl
from jax.experimental.pallas import tpu as pltpu
from jax.sharding import PartitionSpec as P

BF = jnp.bfloat16
F32 = jnp.float32
D = 768
HEAD_DIM = 64
DS = 96
SIDE_HEADS = 12
SIDE_HEAD_DIM = 8
SFF = 384
ROW_LEN = 512
SEGS = 8
HALF = 256
GRAD_LANES = 2048
LOG2E = 1.4426950408889634
EPS = 1e-06


def dot(a, b, ca=1, cb=0):
    return lax.dot_general(a, b, (((ca,), (cb,)), ((), ())), preferred_element_type=F32)


def gelu(x):
    x2 = x * x
    u = x * (x2 * (0.7978845608028654 * 0.044715) + 0.7978845608028654)
    h = 0.5 * x
    return h + h * jnp.tanh(u)


def gelu_and_slope(x):
    x2 = x * x
    u = x * (x2 * (0.7978845608028654 * 0.044715) + 0.7978845608028654)
    t = jnp.tanh(u)
    h = 0.5 * x
    du = 0.7978845608028654 * 3.0 * 0.044715 * x2 + 0.7978845608028654
    return h + h * t, 0.5 + 0.5 * t + h * (1.0 - t * t) * du


def row_starts(first_ref, lens_ref, r):
    starts, begin = [], jnp.int32(0)
    long_start = jnp.int32(0)
    for j in range(SEGS):
        n = lens_ref[j, first_ref[0] + r]
        starts.append((begin, n))
        long_start = jnp.where(n == HALF, begin, long_start)
        begin = begin + n
    return long_start, [((b - long_start) & (ROW_LEN - 1), n) for b, n in starts]


def fill_bias(bias_ref, docs):
    q = lax.broadcasted_iota(jnp.int32, (1, HALF), 1) + HALF
    low = jnp.zeros((1, HALF), jnp.int32)
    high = jnp.zeros((1, HALF), jnp.int32)
    for b, n in docs:
        inside = (q >= b) & (q < b + n)
        low = jnp.where(inside, b, low)
        high = jnp.where(inside, b + n, high)
    k = lax.broadcasted_iota(jnp.int32, (HALF, HALF), 0) + HALF
    bias_ref[...] = jnp.where((k >= low) & (k < high), 0.0, -1e30)


def turn_rows(src_ref, shift):
    n = src_ref.shape[1]
    part = shift & 7
    first = lax.shift_right_logical(shift, 3)
    groups = []
    for g in range(ROW_LEN // 8 + 1):
        start = pl.multiple_of(((first + g) & (ROW_LEN // 8 - 1)) * 8, 8)
        groups.append(src_ref[pl.ds(start, 8), :])
    wide = jnp.concatenate(groups, axis=0).reshape(ROW_LEN // 8 + 1, 8, n)
    back = (8 - part) & 7
    wide = pltpu.roll(wide, back, 1)
    place = lax.broadcasted_iota(jnp.int32, (ROW_LEN // 8, 8, n), 1)
    turned = jnp.where(place < 8 - part, wide[:-1], wide[1:])
    return turned.reshape(ROW_LEN, n)


def exponentials(s, half, bias_ref, safe):
    if half:
        s = s + bias_ref[...]
    if safe:
        s = s - jnp.max(s, axis=0, keepdims=True)
    e = jnp.exp2(s)
    return e.astype(BF), jnp.sum(e, axis=0, keepdims=True)


def out_of_range(sums):
    low, high = sums[0], sums[0]
    for one in sums[1:]:
        low, high = jnp.minimum(low, one), jnp.maximum(high, one)
    fine = (jnp.min(low) > 1e-20) & (jnp.max(high) < 1e20)
    return jnp.logical_not(fine)


def frozen_attention(qkv_ref, vt_ref, e_ref, ctxt_ref, bias_ref, safe):
    cols = qkv_ref.shape[1] // 3
    lane = lax.broadcasted_iota(jnp.int32, (1, 128), 1)
    keep = [(lane < 64).astype(F32).astype(BF), (lane >= 64).astype(F32).astype(BF)]
    blocks = [(half, p, j) for half in range(2) for p in range(cols // 128) for j in range(2)]
    sums = []
    for n, (half, p, j) in enumerate(blocks):
        rows = slice(half * HALF, (half + 1) * HALF)
        q2 = qkv_ref[rows, p * 128 : (p + 1) * 128]
        k2 = qkv_ref[rows, cols + p * 128 : cols + (p + 1) * 128]
        s = dot(k2 * keep[j], q2, 1, 1) * (LOG2E / 8.0)
        e_ref[n], total = exponentials(s, half, bias_ref, safe)
        sums.append(total)
    for n, (half, p, j) in enumerate(blocks):
        rows = slice(half * HALF, (half + 1) * HALF)
        head = slice(p * 128 + j * 64, p * 128 + (j + 1) * 64)
        ctxt_ref[head, rows] = (dot(vt_ref[head, rows], e_ref[n]) * (1.0 / sums[n])).astype(BF)
    return sums


def add_heads(mid_ref, wo_ref, qkv_ref, vt_ref, e_ref, ctxt_ref, bias_ref):
    sums = frozen_attention(qkv_ref, vt_ref, e_ref, ctxt_ref, bias_ref, False)
    bad = out_of_range(sums)

    @pl.when(bad)
    def _():
        frozen_attention(qkv_ref, vt_ref, e_ref, ctxt_ref, bias_ref, True)

    mid_ref[...] += dot(ctxt_ref[...].T, wo_ref[...])


def join_weights(wqkv_ref, parts):
    cols = parts[0].shape[1]
    for i, part in enumerate(parts):
        wqkv_ref[:, i * cols : (i + 1) * cols] = part[...]


def turn_and_norm(first_ref, lens_ref, r, x_ref, gain_ref, raw_ref, xf_ref, normed_ref):
    shift, _ = row_starts(first_ref, lens_ref, r)
    raw_ref[...] = x_ref[...].astype(F32)
    x = turn_rows(raw_ref, shift)
    xf_ref[...] = x
    normed_ref[...] = (x * lax.rsqrt(jnp.mean(x * x, axis=1, keepdims=True) + EPS) * gain_ref[...].reshape(1, D)).astype(BF)


def first_kernel(first_ref, lens_ref, x_ref, next_ref, gain_ref, wq_ref, wk_ref, wv_ref, wo_ref, normed_ref, mid_ref, wqkv_ref, qkv_ref, vt_ref, e_ref, ctxt_ref, bias_ref, raw_ref, xf_ref, nb_ref):
    r = pl.program_id(0)
    rows = pl.num_programs(0)

    @pl.when(r == 0)
    def _():
        join_weights(wqkv_ref, (wq_ref, wk_ref, wv_ref))
        turn_and_norm(first_ref, lens_ref, 0, x_ref, gain_ref, raw_ref, xf_ref, nb_ref)

    _, docs = row_starts(first_ref, lens_ref, r)
    fill_bias(bias_ref, docs)
    mid_ref[...] = xf_ref[...]
    normed_ref[...] = nb_ref[...]
    qkv_ref[...] = dot(nb_ref[...], wqkv_ref[...]).astype(BF)
    vt_ref[...] = qkv_ref[:, 2 * wq_ref.shape[1] :].T
    turn_and_norm(first_ref, lens_ref, jnp.minimum(r + 1, rows - 1), next_ref, gain_ref, raw_ref, xf_ref, nb_ref)
    add_heads(mid_ref, wo_ref, qkv_ref, vt_ref, e_ref, ctxt_ref, bias_ref)


def second_kernel(first_ref, lens_ref, normed_ref, part_ref, wq_ref, wk_ref, wv_ref, wo_ref, mid_ref, wqkv_ref, qkv_ref, vt_ref, e_ref, ctxt_ref, bias_ref):
    r = pl.program_id(0)

    @pl.when(r == 0)
    def _():
        join_weights(wqkv_ref, (wq_ref, wk_ref, wv_ref))

    _, docs = row_starts(first_ref, lens_ref, r)
    fill_bias(bias_ref, docs)
    mid_ref[...] = part_ref[...]
    qkv_ref[...] = dot(normed_ref[...], wqkv_ref[...]).astype(BF)
    vt_ref[...] = qkv_ref[:, 2 * wq_ref.shape[1] :].T
    add_heads(mid_ref, wo_ref, qkv_ref, vt_ref, e_ref, ctxt_ref, bias_ref)


def side_blocks():
    return [(half, h) for half in range(2) for h in range(SIDE_HEADS)]


def head_rows(product, h):
    low = SIDE_HEAD_DIM * (h % 2)
    return product[low : low + SIDE_HEAD_DIM]


def pair(h):
    return slice(2 * SIDE_HEAD_DIM * (h // 2), 2 * SIDE_HEAD_DIM * (h // 2 + 1))


def side_forward(k, qt, vt, masks, bias_ref, e_ref, inv_ref, ctxt_ref, safe):
    sums = []
    for n, (half, h) in enumerate(side_blocks()):
        rows = slice(half * HALF, (half + 1) * HALF)
        s = dot(k[rows] * masks[h], qt[:, rows]) * (LOG2E * SIDE_HEAD_DIM**-0.5)
        e_ref[n], total = exponentials(s, half, bias_ref, safe)
        sums.append(total)
    for n, (half, h) in enumerate(side_blocks()):
        rows = slice(half * HALF, (half + 1) * HALF)
        own = slice(SIDE_HEAD_DIM * h, SIDE_HEAD_DIM * (h + 1))
        inv = 1.0 / sums[n]
        ctxt_ref[own, rows] = head_rows(dot(vt[pair(h), rows], e_ref[n]), h) * inv
        inv_ref[own, rows] = jnp.broadcast_to(inv, (SIDE_HEAD_DIM, HALF))
    return sums


def third_kernel(
    first_ref,
    lens_ref,
    mid_ref,
    fgain_ref,
    w1a_ref,
    w1b_ref,
    w2a_ref,
    w2b_ref,
    side_ref,
    cot_ref,
    alpha_ref,
    gain1_ref,
    gain2_ref,
    downt_ref,
    sq_ref,
    sk_ref,
    sv_ref,
    proj_ref,
    expand_ref,
    shrinkt_ref,
    bb_ref,
    out_ref,
    state_ref,
    mine_ref,
    other_ref,
    grads_ref,
    hid_ref,
    bias_ref,
    f_ref,
    cols_ref,
    wqkvt_ref,
    e_ref,
    et_ref,
    ds_ref,
    dst_ref,
    inv_ref,
    ctxt_ref,
    qkvt_ref,
    dq_ref,
    acc_ref,
):
    r = pl.program_id(0)

    @pl.when(r == 0)
    def _():
        grads_ref[...] = jnp.zeros_like(grads_ref)
        acc_ref[...] = jnp.zeros_like(acc_ref)
        for i, ref in enumerate((alpha_ref, gain1_ref, gain2_ref)):
            cols_ref[i] = jnp.broadcast_to(jnp.broadcast_to(ref[...].reshape(1, DS), (8, DS)).T[:, 0:1], (DS, ROW_LEN))
        wqkvt_ref[:DS] = sq_ref[...].T
        wqkvt_ref[DS : 2 * DS] = sk_ref[...].T
        wqkvt_ref[2 * DS :] = sv_ref[...].T

    shift, docs = row_starts(first_ref, lens_ref, r)
    fill_bias(bias_ref, docs)

    middle = mid_ref[...]
    normed = (middle * lax.rsqrt(jnp.mean(middle * middle, axis=1, keepdims=True) + EPS) * fgain_ref[...].reshape(1, D)).astype(BF)
    units = w1a_ref.shape[1]
    for i, w in enumerate((w1a_ref, w1b_ref)):
        for c in range(units // 256):
            hid_ref[:, i * units + c * 256 : i * units + (c + 1) * 256] = gelu(dot(normed, w[:, c * 256 : (c + 1) * 256])).astype(BF)
    f_ref[...] = mid_ref[...] + dot(hid_ref[:, :units], w2a_ref[...]) + dot(hid_ref[:, units:], w2b_ref[...])
    bb = f_ref[...].astype(BF)
    bb_ref[...] = turn_rows(f_ref, (ROW_LEN - shift) & (ROW_LEN - 1)).astype(BF)

    alpha = cols_ref[0]
    gain1 = cols_ref[1]
    gain2 = cols_ref[2]
    mixing = 1.0 / (1.0 + jnp.exp(alpha * -10.0))
    forward = (ROW_LEN - shift) & (ROW_LEN - 1)
    side = pltpu.roll(side_ref[...].astype(F32), forward, 1)
    cot = pltpu.roll(cot_ref[...].astype(F32), forward, 1)
    cotb = cot.astype(BF)
    lowered = dot(downt_ref[...], bb, 1, 1)
    inputs = mixing * lowered + (1.0 - mixing) * side
    scale1 = lax.rsqrt(jnp.mean(inputs * inputs, axis=0, keepdims=True) + EPS)
    fnt = (inputs * scale1 * gain1).astype(BF)
    qkvt_ref[...] = dot(wqkvt_ref[...], fnt).astype(BF)
    qt, kt, vt = qkvt_ref[:DS], qkvt_ref[DS : 2 * DS], qkvt_ref[2 * DS :]
    lane = lax.broadcasted_iota(jnp.int32, (1, DS), 1)
    masks = [((lane >= 8 * h) & (lane < 8 * h + 8)).astype(F32).astype(BF) for h in range(SIDE_HEADS)]
    lane2 = lax.broadcasted_iota(jnp.int32, (1, 128), 1)
    masks2 = [
        (((lane2 >= 8 * h) & (lane2 < 8 * h + 8)) | (lane2 == DS + h) | (lane2 == DS + 16 + h)).astype(F32).astype(BF)
        for h in range(SIDE_HEADS)
    ]
    k, v = kt.T, vt.T
    sums = side_forward(k, qt, vt, masks, bias_ref, e_ref, inv_ref, ctxt_ref, False)
    bad = out_of_range(sums)

    @pl.when(bad)
    def _():
        qt, kt, vt = qkvt_ref[:DS], qkvt_ref[DS : 2 * DS], qkvt_ref[2 * DS :]
        side_forward(kt.T, qt, vt, masks, bias_ref, e_ref, inv_ref, ctxt_ref, True)

    ctx = ctxt_ref[...]
    ctxb = ctx.astype(BF)
    middle_side = inputs + dot(proj_ref[...], ctxb, 0, 0)
    scale2 = lax.rsqrt(jnp.mean(middle_side * middle_side, axis=0, keepdims=True) + EPS)
    snt = (middle_side * scale2 * gain2).astype(BF)
    expanded = dot(expand_ref[...], snt, 0, 0)
    activated, slope = gelu_and_slope(expanded)
    activated = activated.astype(BF)
    side_out = middle_side + dot(shrinkt_ref[...], activated)
    out_ref[...] = pltpu.roll(side_out, shift, 1)

    activated_grad = dot(shrinkt_ref[...], cotb, 0, 0)
    expanded_grad = (activated_grad * slope).astype(BF)
    second_grad = dot(expand_ref[...], expanded_grad)
    w2 = second_grad * gain2
    ms = middle_side * scale2
    mean2 = jnp.mean(w2 * middle_side, axis=0, keepdims=True)
    middle_grad = cot + scale2 * w2 - ms * (scale2 * scale2) * mean2
    acc_ref[0] += second_grad * ms
    branch = middle_grad.astype(BF)
    context_grad = dot(proj_ref[...], branch).astype(BF).astype(F32)
    dop = (context_grad * inv_ref[...]).astype(BF)
    centre = jnp.sum((dop.astype(F32) * ctx).reshape(SIDE_HEADS, 8, ROW_LEN), axis=1)
    centre = jnp.concatenate([centre, jnp.zeros((4, ROW_LEN), F32)], axis=0)
    chigh = centre.astype(BF)
    clow = (centre - chigh.astype(F32)).astype(BF)
    dstack = jnp.concatenate([dop, -chigh, -clow], axis=0)
    vones = jnp.concatenate([v, jnp.ones((ROW_LEN, 32), BF)], axis=1)
    for n, (half, h) in enumerate(side_blocks()):
        rows = slice(half * HALF, (half + 1) * HALF)
        dp = dot(vones[rows] * masks2[h], dstack[:, rows])
        ds_ref[n] = (e_ref[n].astype(F32) * dp).astype(BF)
        et_ref[n] = e_ref[n].T
    for n, (half, h) in enumerate(side_blocks()):
        rows = slice(half * HALF, (half + 1) * HALF)
        dq_ref[8 * h : 8 * h + 8, rows] = head_rows(dot(kt[pair(h), rows], ds_ref[n]), h) * SIDE_HEAD_DIM**-0.5
        dst_ref[n] = ds_ref[n].T
    for n, (half, h) in enumerate(side_blocks()):
        rows = slice(half * HALF, (half + 1) * HALF)
        low = 2 * DS + 8 * h
        dq_ref[low : low + 8, rows] = head_rows(dot(dop[pair(h), rows], et_ref[n]), h)
    for n, (half, h) in enumerate(side_blocks()):
        rows = slice(half * HALF, (half + 1) * HALF)
        low = DS + 8 * h
        dq_ref[low : low + 8, rows] = head_rows(dot(qt[pair(h), rows], dst_ref[n]), h) * SIDE_HEAD_DIM**-0.5
    dqkvt = dq_ref[...].astype(BF)
    first_grad = dot(wqkvt_ref[...], dqkvt, 0, 0)
    w1 = first_grad * gain1
    ins = inputs * scale1
    mean1 = jnp.mean(w1 * inputs, axis=0, keepdims=True)
    input_grad = middle_grad + scale1 * w1 - ins * (scale1 * scale1) * mean1
    acc_ref[1] += first_grad * ins
    acc_ref[2] += input_grad * (lowered - side)
    state_ref[...] = pltpu.roll((1.0 - mixing) * input_grad, shift, 1)
    grads_ref[:, 0:D] += dot((mixing * input_grad).astype(BF), bb)
    grads_ref[:, D : D + SFF] += dot(snt, expanded_grad, 1, 1)
    grads_ref[:, D + SFF : D + 2 * SFF] += dot(cotb, activated, 1, 1)
    low = D + 2 * SFF
    grads_ref[:, low : low + 3 * DS] += dot(fnt, dqkvt, 1, 1)
    grads_ref[:, low + 3 * DS : low + 4 * DS] += dot(ctxb, branch, 1, 1)

    @pl.when(r == pl.num_programs(0) - 1)
    def _():
        total = [jnp.sum(acc_ref[i], axis=1, keepdims=True) for i in range(3)]
        total[2] = total[2] * (mixing * (1.0 - mixing))[:, 0:1] * 10.0
        lane = lax.broadcasted_iota(jnp.int32, (DS, 128), 1)
        grads_ref[:, low + 4 * DS :] = jnp.where(lane == 0, total[0], jnp.where(lane == 1, total[1], jnp.where(lane == 2, total[2], 0.0)))
        half = DS // 2
        tensor = (first_ref[0] != 0).astype(jnp.int32)
        mine_ref[...] = grads_ref[pl.ds(pl.multiple_of(tensor * half, 8), half), :].astype(BF)
        other_ref[...] = grads_ref[pl.ds(pl.multiple_of((1 - tensor) * half, 8), half), :].astype(BF)


def whole(shape):
    return pl.BlockSpec(shape, lambda r, *_: (0,) * len(shape), pipeline_mode=pl.Buffered(1))


def params(limit):
    return pltpu.CompilerParams(vmem_limit_bytes=limit * 1024 * 1024, dimension_semantics=("arbitrary",))


def swap(x):
    return lax.ppermute(x, "tensor", [(0, 1), (1, 0)])


def sum_over(mine, other, batch):
    def trade(x, bit):
        return lax.ppermute(x, "batch", [(i, i ^ bit) for i in range(batch)])

    place = lax.axis_index("batch")
    part = mine.astype(F32) + swap(other).astype(F32)
    bits = [1 << i for i in range(batch.bit_length() - 1)]
    split = bits[:2]
    for bit in split:
        low, high = jnp.split(part.astype(BF), 2, axis=1)
        upper = (place & bit) != 0
        got = trade(jnp.where(upper, low, high), bit)
        part = jnp.where(upper, high, low).astype(F32) + got.astype(F32)
    for bit in bits[2:]:
        sent = part.astype(BF)
        part = sent.astype(F32) + trade(sent, bit).astype(F32)
    sent = part.astype(BF)
    for bit in reversed(split):
        got = trade(sent, bit)
        upper = (place & bit) != 0
        sent = jnp.concatenate([jnp.where(upper, got, sent), jnp.where(upper, sent, got)], axis=1)
    got = swap(sent)
    upper = lax.axis_index("tensor") != 0
    return jnp.concatenate([jnp.where(upper, got, sent), jnp.where(upper, sent, got)], axis=0).astype(F32)


def make_body(batch):
    def body(
        hidden_in,
        lengths,
        attn_gain,
        attn_query,
        attn_key,
        attn_value,
        attn_out,
        ffn_gain,
        ffn_in,
        ffn_out,
        side_state,
        gate_alpha,
        down_w,
        side_attn_gain,
        side_query,
        side_key,
        side_value,
        side_proj,
        side_ffn_gain,
        side_expand,
        side_shrink,
        cotangent,
    ):
        tokens = hidden_in.shape[0]
        rows = tokens // ROW_LEN
        cols = attn_query.shape[1]
        units = ffn_in.shape[1]
        t = lax.axis_index("tensor")
        first = (t * rows).astype(jnp.int32).reshape(1)
        far = [swap(w) for w in (attn_query, attn_key, attn_value, attn_out, ffn_in, ffn_out)]
        tile = pl.BlockSpec((ROW_LEN, D), lambda r, *_: (r, 0))
        scratch = [
            pltpu.VMEM((D, 3 * cols), BF),
            pltpu.VMEM((ROW_LEN, 3 * cols), BF),
            pltpu.VMEM((cols, ROW_LEN), BF),
            pltpu.VMEM((2 * cols // HEAD_DIM, HALF, HALF), BF),
            pltpu.VMEM((cols, ROW_LEN), BF),
            pltpu.VMEM((HALF, HALF), F32),
        ]
        attn_specs = [whole((D, cols))] * 3 + [whole((cols, D))]
        normed, mid = pl.pallas_call(
            first_kernel,
            grid_spec=pltpu.PrefetchScalarGridSpec(
                num_scalar_prefetch=2,
                grid=(rows,),
                in_specs=[
                    whole((ROW_LEN, D)),
                    pl.BlockSpec((ROW_LEN, D), lambda r, *_: (jnp.minimum(r + 1, rows - 1), 0)),
                    whole((D,)),
                ]
                + attn_specs,
                out_specs=[tile, tile],
                scratch_shapes=scratch + [pltpu.VMEM((ROW_LEN, D), F32)] * 2 + [pltpu.VMEM((ROW_LEN, D), BF)],
            ),
            out_shape=[jax.ShapeDtypeStruct((tokens, D), BF), jax.ShapeDtypeStruct((tokens, D), F32)],
            compiler_params=params(60),
            name="own_heads",
        )(first, lengths.T, hidden_in, hidden_in, attn_gain, attn_query, attn_key, attn_value, attn_out)
        mid = pl.pallas_call(
            second_kernel,
            grid_spec=pltpu.PrefetchScalarGridSpec(
                num_scalar_prefetch=2,
                grid=(rows,),
                in_specs=[tile, tile] + attn_specs,
                out_specs=tile,
                scratch_shapes=scratch,
            ),
            out_shape=jax.ShapeDtypeStruct((tokens, D), F32),
            compiler_params=params(60),
            name="far_heads",
        )(first, lengths.T, normed, mid, *far[:4])
        side_tile = pl.BlockSpec((DS, ROW_LEN), lambda r, *_: (0, r))
        backbone, side_out, state_grad, mine, other = pl.pallas_call(
            third_kernel,
            grid_spec=pltpu.PrefetchScalarGridSpec(
                num_scalar_prefetch=2,
                grid=(rows,),
                in_specs=[
                    tile,
                    whole((D,)),
                    whole((D, units)),
                    whole((D, units)),
                    whole((units, D)),
                    whole((units, D)),
                    side_tile,
                    side_tile,
                    whole((DS,)),
                    whole((DS,)),
                    whole((DS,)),
                    whole((DS, D)),
                    whole((DS, DS)),
                    whole((DS, DS)),
                    whole((DS, DS)),
                    whole((DS, DS)),
                    whole((DS, SFF)),
                    whole((DS, SFF)),
                ],
                out_specs=[tile, side_tile, side_tile] + [pl.BlockSpec((DS // 2, GRAD_LANES), lambda r, *_: (0, 0))] * 2,
                scratch_shapes=[
                    pltpu.VMEM((DS, GRAD_LANES), F32),
                    pltpu.VMEM((ROW_LEN, 2 * units), BF),
                    pltpu.VMEM((HALF, HALF), F32),
                    pltpu.VMEM((ROW_LEN, D), F32),
                    pltpu.VMEM((3, DS, ROW_LEN), F32),
                    pltpu.VMEM((3 * DS, DS), BF),
                    pltpu.VMEM((2 * SIDE_HEADS, HALF, HALF), BF),
                    pltpu.VMEM((2 * SIDE_HEADS, HALF, HALF), BF),
                    pltpu.VMEM((2 * SIDE_HEADS, HALF, HALF), BF),
                    pltpu.VMEM((2 * SIDE_HEADS, HALF, HALF), BF),
                    pltpu.VMEM((DS, ROW_LEN), F32),
                    pltpu.VMEM((DS, ROW_LEN), F32),
                    pltpu.VMEM((3 * DS, ROW_LEN), BF),
                    pltpu.VMEM((3 * DS, ROW_LEN), F32),
                    pltpu.VMEM((3, DS, ROW_LEN), F32),
                ],
            ),
            out_shape=[
                jax.ShapeDtypeStruct((tokens, D), BF),
                jax.ShapeDtypeStruct((DS, tokens), F32),
                jax.ShapeDtypeStruct((DS, tokens), F32),
                jax.ShapeDtypeStruct((DS // 2, GRAD_LANES), BF),
                jax.ShapeDtypeStruct((DS // 2, GRAD_LANES), BF),
            ],
            compiler_params=params(60),
            name="forward_and_back",
        )(
            first,
            lengths.T,
            mid,
            ffn_gain,
            ffn_in,
            far[4],
            ffn_out,
            far[5],
            side_state.T,
            cotangent.T,
            gate_alpha,
            side_attn_gain,
            side_ffn_gain,
            down_w.T,
            side_query,
            side_key,
            side_value,
            side_proj,
            side_expand,
            side_shrink.T,
        )
        g = sum_over(mine, other, batch)
        low = D + 2 * SFF
        return (
            backbone,
            side_out.T,
            state_grad.T,
            g[:, :D].T,
            g[:, low + 4 * DS + 2],
            g[:, low + 4 * DS + 1],
            g[:, low : low + DS],
            g[:, low + DS : low + 2 * DS],
            g[:, low + 2 * DS : low + 3 * DS],
            g[:, low + 3 * DS : low + 4 * DS],
            g[:, low + 4 * DS],
            g[:, D : D + SFF],
            g[:, D + SFF : low].T,
        )

    return body


def solution(mesh):
    split = P(("batch", "tensor"), None)
    return jax.shard_map(
        make_body(mesh.shape["batch"]),
        mesh=mesh,
        in_specs=(
            split,
            P("batch", None),
            P(),
            P(None, "tensor"),
            P(None, "tensor"),
            P(None, "tensor"),
            P("tensor", None),
            P(),
            P(None, "tensor"),
            P("tensor", None),
            split,
            P(),
            P(),
            P(),
            P(),
            P(),
            P(),
            P(),
            P(),
            P(),
            P(),
            split,
        ),
        out_specs=(split, split, split) + (P(),) * 10,
        check_vma=False,
    )
```

time: 225 us -> 160 us (0.71)
  Pallas kernels: 174 us -> 111 us
  local copies, waits for them, and re-layouts: 7.8 us -> 2.99 us
  starting transfers between devices: 10.9 us -> 15.1 us
  waiting for transfers between devices: 29.4 us -> 25.9 us
    pallas_call x1, Pallas kernels: 114 us -> 73.3 us  [body(): pl.pallas_call(third_kernel, grid_spec=pltpu.PrefetchScalarGridSpec(num_s...]
    pallas_call x1, Pallas kernels: 29.4 us -> 17.8 us  [body(): pl.pallas_call(second_kernel, grid_spec=pltpu.PrefetchScalarGridSpec(num_...]
    pallas_call x1, Pallas kernels: 30.8 us -> 19.9 us  [body(): pl.pallas_call(first_kernel, grid_spec=pltpu.PrefetchScalarGridSpec(num_s...]
    ppermute x4 -> x6, waiting for transfers between devices: 21.6 us -> 15.4 us  [trade(): return lax.ppermute(x, 'batch', [(i, i ^ bit) for i in range(batch)])]
    ppermute x4 -> x6, starting transfers between devices: 8.71 us -> 13 us  [trade(): return lax.ppermute(x, 'batch', [(i, i ^ bit) for i in range(batch)])]
    reshape x3 -> x0, local copies, waits for them, and re-layouts: 3.12 us -> none  [the longest x1 1.27 us: body(): attn_gain.reshape(1, D)]
    ppermute x8, waiting for transfers between devices: 7.78 us -> 10.6 us  [swap(): return lax.ppermute(x, 'tensor', [(0, 1), (1, 0)])]
  transfers between devices with their start and end apart: 12 -> 14, of which waited for: 7 -> 9; matrix products, arithmetic and copies ran while one was open for 2% -> 0% of each run, Pallas kernels for 27% -> 24%
where the time goes in v2:
time: 160 us; the launch traced here: 159 us
  Pallas kernels  111 us (69%)
  waiting for transfers between devices  25.9 us (16%)
  starting transfers between devices  15.1 us (9%)
  other arithmetic  3.46 us (2%)
  local copies, waits for them, and re-layouts  2.99 us (2%)
    pallas_call x1, Pallas kernels, body(): pl.pallas_call(third_kernel, grid_spec=pltpu.PrefetchScalarGridSpec(num_s...  73.3 us
    pallas_call x1, Pallas kernels, body(): pl.pallas_call(first_kernel, grid_spec=pltpu.PrefetchScalarGridSpec(num_s...  19.9 us
    pallas_call x1, Pallas kernels, body(): pl.pallas_call(second_kernel, grid_spec=pltpu.PrefetchScalarGridSpec(num_...  17.8 us
    ppermute x6, waiting for transfers between devices, trade(): return lax.ppermute(x, 'batch', [(i, i ^ bit) for i in range(batch)])  15.4 us
    ppermute x6, starting transfers between devices, trade(): return lax.ppermute(x, 'batch', [(i, i ^ bit) for i in range(batch)])  13 us
    ppermute x8, waiting for transfers between devices, swap(): return lax.ppermute(x, 'tensor', [(0, 1), (1, 0)])  10.6 us
  transfers between devices with their start and end apart: 14, of which 9 were waited for; matrix products, arithmetic and copies ran while one was open for 0% of the time, Pallas kernels for 24%

profile of v2, /device:TPU:0, one launch (start us, length us, event | category | flops | bytes accessed | tf_op | source)
XLA Modules:
  0.0 159.4 jit_solution(10216154761281849743)
XLA Ops:
  0.6 0.5 collective-permute-start.4
  1.2 0.1 collective-permute-start.5
  1.2 0.4 collective-permute-start
  1.7 0.1 collective-permute-start.1
  1.8 0.4 collective-permute-start.2
  2.2 7.6 %collective-permute-done.wq_ref = bf16[768,384]{1,0:T(8,128)(2,1)S(1)} collective-permute-done((bf16[768,384]{1,0:T(8,128)(2,1)}, bf16[768,384]{1,0:T(8,128)(2,1)S(1)}, u32[]{:S(2)}, u32[]{:S(2)}) %collective-permute-start) | collective-permute-done | bytes 589856 | tf_op jit(solution)/shard_map/ppermute | solution.py:387
  9.8 0.4 collective-permute-start.3
  10.2 19.9 %own_heads.1 = (bf16[2560,768]{1,0:T(8,128)(2,1)}, f32[2560,768]{1,0:T(8,128)}) custom-call(s32[1]{0:T(128)} %bitcast.first_ref, s32[8,10]{1,0:T(8,128)} %bitcast.16, bf16[2560,768]{1,0:T(8,128)(2,1)} %next_ref.1, bf16[2560,768]{1,0:T(8,128)(2,1)} %next_ref.1, f32[768]{0:T(1024)} %gain_ref.1, bf16[768,384]{1,0:T(8,128)(2,1)} %wq_ref.1, ...), custom_call_target="tpu_custom_call" | custom-call | tf_op jit(solution)/shard_map/own_heads/pallas_call | solution.py:458
  30.2 0.8 copy-done.2
  30.9 17.8 %far_heads.1.mid_ref = f32[2560,768]{1,0:T(8,128)} custom-call(s32[1]{0:T(128)} %bitcast.first_ref, s32[8,10]{1,0:T(8,128)} %bitcast.17, bf16[2560,768]{1,0:T(8,128)(2,1)} %get-tuple-element.20.normed_ref, f32[2560,768]{1,0:T(8,128)} %get-tuple-element.21.part_ref, bf16[768,384]{1,0:T(8,128)(2,1)} %copy-done.1, bf16[768,384]{1,0:T(8,128)(2,1)} %copy-done.2, ...), custom_call_target="tpu_custom_call" | custom-call | tf_op jit(solution)/shard_map/far_heads/pallas_call | solution.py:476
  48.8 1.5 copy-done
  50.3 73.3 %forward_and_back.1 = (bf16[2560,768]{1,0:T(8,128)(2,1)}, f32[96,2560]{1,0:T(8,128)}, f32[96,2560]{1,0:T(8,128)}, bf16[48,2048]{1,0:T(8,128)(2,1)}, bf16[48,2048]{1,0:T(8,128)(2,1)}) custom-call(s32[1]{0:T(128)} %bitcast.first_ref, s32[8,10]{1,0:T(8,128)} %bitcast.18, f32[2560,768]{1,0:T(8,128)} %far_heads.1.mid_ref, f32[768]{0:T(1024)} %fgain_ref.1, ...), custom_call_target="tpu_custom_call" | custom-call | tf_op jit(solution)/shard_map/forward_and_back/pallas_call | solution.py:490
  123.6 0.2 collective-permute-start.6
  123.8 1.5 collective-permute-done.6
  125.3 1.0 add_convert_fusion
  126.3 2.7 %collective-permute-start.7 = (bf16[48,1024]{1,0:T(8,128)(2,1)S(1)}, bf16[48,1024]{1,0:T(8,128)(2,1)S(1)}, u32[]{:S(2)}, u32[]{:S(2)}) collective-permute-start(bf16[48,1024]{1,0:T(8,128)(2,1)S(1)} %broadcast_select_fusion.4), channel_id=1, source_target_pairs={{0,2},{2,0},{4,6},{6,4},{8,10},{10,8},{12,14},{14,12},{16,18},{18,... | collective-permute-start | bytes 294920 | tf_op jit(solution)/shard_map/ppermute | solution.py:392
  129.0 3.3 %collective-permute-done.7 = bf16[48,1024]{1,0:T(8,128)(2,1)S(1)} collective-permute-done((bf16[48,1024]{1,0:T(8,128)(2,1)S(1)}, bf16[48,1024]{1,0:T(8,128)(2,1)S(1)}, u32[]{:S(2)}, u32[]{:S(2)}) %collective-permute-start.7) | collective-permute-done | bytes 98336 | tf_op jit(solution)/shard_map/ppermute | solution.py:392
  132.4 1.8 %collective-permute-start.8 = (bf16[48,512]{1,0:T(8,128)(2,1)S(1)}, bf16[48,512]{1,0:T(8,128)(2,1)S(1)}, u32[]{:S(2)}, u32[]{:S(2)}) collective-permute-start(bf16[48,512]{1,0:T(8,128)(2,1)S(1)} %broadcast_select_fusion.7), channel_id=1, source_target_pairs={{0,4},{2,6},{4,0},{6,2},{8,12},{10,14},{12,8},{14,10},{16,20},{18,... | collective-permute-start | bytes 147464 | tf_op jit(solution)/shard_map/ppermute | solution.py:392
  134.3 2.3 %collective-permute-done.8 = bf16[48,512]{1,0:T(8,128)(2,1)S(1)} collective-permute-done((bf16[48,512]{1,0:T(8,128)(2,1)S(1)}, bf16[48,512]{1,0:T(8,128)(2,1)S(1)}, u32[]{:S(2)}, u32[]{:S(2)}) %collective-permute-start.8) | collective-permute-done | bytes 49184 | tf_op jit(solution)/shard_map/ppermute | solution.py:392
  136.6 1.9 %collective-permute-start.9 = (bf16[48,512]{1,0:T(8,128)(2,1)S(1)}, bf16[48,512]{1,0:T(8,128)(2,1)S(1)}, u32[]{:S(2)}, u32[]{:S(2)}) collective-permute-start(bf16[48,512]{1,0:T(8,128)(2,1)S(1)} %add_convert_fusion.4), channel_id=1, source_target_pairs={{0,8},{2,10},{4,12},{6,14},{8,0},{10,2},{12,4},{14,6},{16,24},{18,... | collective-permute-start | bytes 147464 | tf_op jit(solution)/shard_map/ppermute | solution.py:392
  138.5 2.3 %collective-permute-done.9 = bf16[48,512]{1,0:T(8,128)(2,1)S(1)} collective-permute-done((bf16[48,512]{1,0:T(8,128)(2,1)S(1)}, bf16[48,512]{1,0:T(8,128)(2,1)S(1)}, u32[]{:S(2)}, u32[]{:S(2)}) %collective-permute-start.9) | collective-permute-done | bytes 49184 | tf_op jit(solution)/shard_map/ppermute | solution.py:392
  140.8 3.1 %collective-permute-start.10 = (bf16[48,512]{1,0:T(8,128)(2,1)S(1)}, bf16[48,512]{1,0:T(8,128)(2,1)S(1)}, u32[]{:S(2)}, u32[]{:S(2)}) collective-permute-start(bf16[48,512]{1,0:T(8,128)(2,1)S(1)} %add_convert_fusion.3), channel_id=1, source_target_pairs={{0,16},{2,18},{4,20},{6,22},{8,24},{10,26},{12,28},{14,30},{16,0},... | collective-permute-start | bytes 147464 | tf_op jit(solution)/shard_map/ppermute | solution.py:392
  143.9 2.1 %collective-permute-done.10 = bf16[48,512]{1,0:T(8,128)(2,1)S(1)} collective-permute-done((bf16[48,512]{1,0:T(8,128)(2,1)S(1)}, bf16[48,512]{1,0:T(8,128)(2,1)S(1)}, u32[]{:S(2)}, u32[]{:S(2)}) %collective-permute-start.10) | collective-permute-done | bytes 49184 | tf_op jit(solution)/shard_map/ppermute | solution.py:392
  145.9 1.7 %collective-permute-start.11 = (bf16[48,512]{1,0:T(8,128)(2,1)S(1)}, bf16[48,512]{1,0:T(8,128)(2,1)S(1)}, u32[]{:S(2)}, u32[]{:S(2)}) collective-permute-start(bf16[48,512]{1,0:T(8,128)(2,1)S(1)} %add_convert_fusion.2), channel_id=1, source_target_pairs={{0,4},{2,6},{4,0},{6,2},{8,12},{10,14},{12,8},{14,10},{16,20},{18,... | collective-permute-start | bytes 147464 | tf_op jit(solution)/shard_map/ppermute | solution.py:392
  147.7 2.4 %collective-permute-done.11 = bf16[48,512]{1,0:T(8,128)(2,1)S(1)} collective-permute-done((bf16[48,512]{1,0:T(8,128)(2,1)S(1)}, bf16[48,512]{1,0:T(8,128)(2,1)S(1)}, u32[]{:S(2)}, u32[]{:S(2)}) %collective-permute-start.11) | collective-permute-done | bytes 49184 | tf_op jit(solution)/shard_map/ppermute | solution.py:392
  150.1 1.7 %collective-permute-start.12 = (bf16[48,1024]{1,0:T(8,128)(2,1)S(1)}, bf16[48,1024]{1,0:T(8,128)(2,1)S(1)}, u32[]{:S(2)}, u32[]{:S(2)}) collective-permute-start(bf16[48,1024]{1,0:T(8,128)(2,1)S(1)} %pad_maximum_fusion.1), channel_id=1, source_target_pairs={{0,2},{2,0},{4,6},{6,4},{8,10},{10,8},{12,14},{14,12},{16,18},{18,... | collective-permute-start | bytes 294920 | tf_op jit(solution)/shard_map/ppermute | solution.py:392
  151.8 3.0 %collective-permute-done.12 = bf16[48,1024]{1,0:T(8,128)(2,1)S(1)} collective-permute-done((bf16[48,1024]{1,0:T(8,128)(2,1)S(1)}, bf16[48,1024]{1,0:T(8,128)(2,1)S(1)}, u32[]{:S(2)}, u32[]{:S(2)}) %collective-permute-start.12) | collective-permute-done | bytes 98336 | tf_op jit(solution)/shard_map/ppermute | solution.py:392
  155.0 1.4 collective-permute-done.13
  156.5 0.7 convert_bitcast_fusion
  157.2 0.7 maximum_convert_fusion.2
  157.9 0.7 convert_reduce_fusion
  158.7 0.7 slice_bitcast_fusion
  (22 shorter events, 0.4 us)
Async XLA Ops:
  0.6 48.1 %collective-permute-start.4 = (bf16[768,1536]{1,0:T(8,128)(2,1)}, bf16[768,1536]{1,0:T(8,128)(2,1)S(1)}, u32[]{:S(2)}, u32[]{:S(2)}) collective-permute-start(bf16[768,1536]{1,0:T(8,128)(2,1)} %w1a_ref.1), channel_id=1, source_target_pairs={{0,1},{1,0},{2,3},{3,2},{4,5},{5,4},{6,7},{7,6},{8,9},{9,8},{10,11... | collective-permute-start | bytes 7077896 | tf_op jit(solution)/shard_map/ppermute | solution.py:387
  1.2 47.6 %collective-permute-start.5 = (bf16[1536,768]{1,0:T(8,128)(2,1)}, bf16[1536,768]{1,0:T(8,128)(2,1)}, u32[]{:S(2)}, u32[]{:S(2)}) collective-permute-start(bf16[1536,768]{1,0:T(8,128)(2,1)} %w2a_ref.1), channel_id=1, source_target_pairs={{0,1},{1,0},{2,3},{3,2},{4,5},{5,4},{6,7},{7,6},{8,9},{9,8},{10,11... | collective-permute-start | bytes 7077896 | tf_op jit(solution)/shard_map/ppermute | solution.py:387
  1.2 8.5 %collective-permute-start = (bf16[768,384]{1,0:T(8,128)(2,1)}, bf16[768,384]{1,0:T(8,128)(2,1)S(1)}, u32[]{:S(2)}, u32[]{:S(2)}) collective-permute-start(bf16[768,384]{1,0:T(8,128)(2,1)} %wq_ref.1), channel_id=1, source_target_pairs={{0,1},{1,0},{2,3},{3,2},{4,5},{5,4},{6,7},{7,6},{8,9},{9,8},{10,11... | collective-permute-start | bytes 1769480 | tf_op jit(solution)/shard_map/ppermute | solution.py:387
  1.7 28.4 %collective-permute-start.1 = (bf16[768,384]{1,0:T(8,128)(2,1)}, bf16[768,384]{1,0:T(8,128)(2,1)S(1)}, u32[]{:S(2)}, u32[]{:S(2)}) collective-permute-start(bf16[768,384]{1,0:T(8,128)(2,1)} %wk_ref.1), channel_id=1, source_target_pairs={{0,1},{1,0},{2,3},{3,2},{4,5},{5,4},{6,7},{7,6},{8,9},{9,8},{10,11... | collective-permute-start | bytes 1769480 | tf_op jit(solution)/shard_map/ppermute | solution.py:387
  1.8 28.4 %collective-permute-start.2 = (bf16[768,384]{1,0:T(8,128)(2,1)}, bf16[768,384]{1,0:T(8,128)(2,1)}, u32[]{:S(2)}, u32[]{:S(2)}) collective-permute-start(bf16[768,384]{1,0:T(8,128)(2,1)} %wv_ref.1), channel_id=1, source_target_pairs={{0,1},{1,0},{2,3},{3,2},{4,5},{5,4},{6,7},{7,6},{8,9},{9,8},{10,11... | collective-permute-start | bytes 1769480 | tf_op jit(solution)/shard_map/ppermute | solution.py:387
  9.8 20.3 %copy-start.1 = (bf16[768,384]{1,0:T(8,128)(2,1)}, bf16[768,384]{1,0:T(8,128)(2,1)S(1)}, u32[]{:S(2)}) copy-start(bf16[768,384]{1,0:T(8,128)(2,1)S(1)} %collective-permute-done.wq_ref) | copy-start | bytes 1769476
  9.8 20.4 %collective-permute-start.3 = (bf16[384,768]{1,0:T(8,128)(2,1)}, bf16[384,768]{1,0:T(8,128)(2,1)}, u32[]{:S(2)}, u32[]{:S(2)}) collective-permute-start(bf16[384,768]{1,0:T(8,128)(2,1)} %wo_ref.1), channel_id=1, source_target_pairs={{0,1},{1,0},{2,3},{3,2},{4,5},{5,4},{6,7},{7,6},{8,9},{9,8},{10,11... | collective-permute-start | bytes 1769480 | tf_op jit(solution)/shard_map/ppermute | solution.py:387
  30.1 0.8 copy-start.2
  48.8 1.5 copy-start
  123.6 1.7 %collective-permute-start.6 = (bf16[48,2048]{1,0:T(8,128)(2,1)}, bf16[48,2048]{1,0:T(8,128)(2,1)S(1)}, u32[]{:S(2)}, u32[]{:S(2)}) collective-permute-start(bf16[48,2048]{1,0:T(8,128)(2,1)} %get-tuple-element.26), channel_id=1, source_target_pairs={{0,1},{1,0},{2,3},{3,2},{4,5},{5,4},{6,7},{7,6},{8,9},{9,8},{10,11... | collective-permute-start | bytes 589832 | tf_op jit(solution)/shard_map/ppermute | solution.py:387
  126.3 6.0 %collective-permute-start.7 = (bf16[48,1024]{1,0:T(8,128)(2,1)S(1)}, bf16[48,1024]{1,0:T(8,128)(2,1)S(1)}, u32[]{:S(2)}, u32[]{:S(2)}) collective-permute-start(bf16[48,1024]{1,0:T(8,128)(2,1)S(1)} %broadcast_select_fusion.4), channel_id=1, source_target_pairs={{0,2},{2,0},{4,6},{6,4},{8,10},{10,8},{12,14},{14,12},{16,18},{18,... | collective-permute-start | bytes 294920 | tf_op jit(solution)/shard_map/ppermute | solution.py:392
  132.4 4.2 %collective-permute-start.8 = (bf16[48,512]{1,0:T(8,128)(2,1)S(1)}, bf16[48,512]{1,0:T(8,128)(2,1)S(1)}, u32[]{:S(2)}, u32[]{:S(2)}) collective-permute-start(bf16[48,512]{1,0:T(8,128)(2,1)S(1)} %broadcast_select_fusion.7), channel_id=1, source_target_pairs={{0,4},{2,6},{4,0},{6,2},{8,12},{10,14},{12,8},{14,10},{16,20},{18,... | collective-permute-start | bytes 147464 | tf_op jit(solution)/shard_map/ppermute | solution.py:392
  136.6 4.2 %collective-permute-start.9 = (bf16[48,512]{1,0:T(8,128)(2,1)S(1)}, bf16[48,512]{1,0:T(8,128)(2,1)S(1)}, u32[]{:S(2)}, u32[]{:S(2)}) collective-permute-start(bf16[48,512]{1,0:T(8,128)(2,1)S(1)} %add_convert_fusion.4), channel_id=1, source_target_pairs={{0,8},{2,10},{4,12},{6,14},{8,0},{10,2},{12,4},{14,6},{16,24},{18,... | collective-permute-start | bytes 147464 | tf_op jit(solution)/shard_map/ppermute | solution.py:392
  140.8 5.2 %collective-permute-start.10 = (bf16[48,512]{1,0:T(8,128)(2,1)S(1)}, bf16[48,512]{1,0:T(8,128)(2,1)S(1)}, u32[]{:S(2)}, u32[]{:S(2)}) collective-permute-start(bf16[48,512]{1,0:T(8,128)(2,1)S(1)} %add_convert_fusion.3), channel_id=1, source_target_pairs={{0,16},{2,18},{4,20},{6,22},{8,24},{10,26},{12,28},{14,30},{16,0},... | collective-permute-start | bytes 147464 | tf_op jit(solution)/shard_map/ppermute | solution.py:392
  145.9 4.2 %collective-permute-start.11 = (bf16[48,512]{1,0:T(8,128)(2,1)S(1)}, bf16[48,512]{1,0:T(8,128)(2,1)S(1)}, u32[]{:S(2)}, u32[]{:S(2)}) collective-permute-start(bf16[48,512]{1,0:T(8,128)(2,1)S(1)} %add_convert_fusion.2), channel_id=1, source_target_pairs={{0,4},{2,6},{4,0},{6,2},{8,12},{10,14},{12,8},{14,10},{16,20},{18,... | collective-permute-start | bytes 147464 | tf_op jit(solution)/shard_map/ppermute | solution.py:392
  150.1 4.7 %collective-permute-start.12 = (bf16[48,1024]{1,0:T(8,128)(2,1)S(1)}, bf16[48,1024]{1,0:T(8,128)(2,1)S(1)}, u32[]{:S(2)}, u32[]{:S(2)}) collective-permute-start(bf16[48,1024]{1,0:T(8,128)(2,1)S(1)} %pad_maximum_fusion.1), channel_id=1, source_target_pairs={{0,2},{2,0},{4,6},{6,4},{8,10},{10,8},{12,14},{14,12},{16,18},{18,... | collective-permute-start | bytes 294920 | tf_op jit(solution)/shard_map/ppermute | solution.py:392
  154.9 1.5 collective-permute-start.13

commit v3 on v2

v3 whole, which is shorter than its diff:
```python
import jax
import jax.numpy as jnp
from jax import lax
from jax.experimental import pallas as pl
from jax.experimental.pallas import tpu as pltpu
from jax.sharding import PartitionSpec as P

BF = jnp.bfloat16
F32 = jnp.float32
D = 768
HEADS = 12
HEAD_DIM = 64
DS = 96
SIDE_HEADS = 12
SIDE_HEAD_DIM = 8
SFF = 384
ROW_LEN = 512
SEGS = 8
HALF = 256
GRAD_LANES = 2048
LOG2E = 1.4426950408889634
EPS = 1e-06


def dot(a, b, ca=1, cb=0):
    return lax.dot_general(a, b, (((ca,), (cb,)), ((), ())), preferred_element_type=F32)


def gelu(x):
    x2 = x * x
    u = x * (x2 * (0.7978845608028654 * 0.044715) + 0.7978845608028654)
    h = 0.5 * x
    return h + h * jnp.tanh(u)


def gelu_and_slope(x):
    x2 = x * x
    u = x * (x2 * (0.7978845608028654 * 0.044715) + 0.7978845608028654)
    t = jnp.tanh(u)
    h = 0.5 * x
    du = 0.7978845608028654 * 3.0 * 0.044715 * x2 + 0.7978845608028654
    return h + h * t, 0.5 + 0.5 * t + h * (1.0 - t * t) * du


def row_starts(first_ref, lens_ref, r):
    starts, begin = [], jnp.int32(0)
    long_start = jnp.int32(0)
    for j in range(SEGS):
        n = lens_ref[j, first_ref[0] + r]
        starts.append((begin, n))
        long_start = jnp.where(n == HALF, begin, long_start)
        begin = begin + n
    return long_start, [((b - long_start) & (ROW_LEN - 1), n) for b, n in starts]


def fill_bias(bias_ref, docs):
    q = lax.broadcasted_iota(jnp.int32, (1, HALF), 1) + HALF
    low = jnp.zeros((1, HALF), jnp.int32)
    high = jnp.zeros((1, HALF), jnp.int32)
    for b, n in docs:
        inside = (q >= b) & (q < b + n)
        low = jnp.where(inside, b, low)
        high = jnp.where(inside, b + n, high)
    k = lax.broadcasted_iota(jnp.int32, (HALF, HALF), 0) + HALF
    bias_ref[...] = jnp.where((k >= low) & (k < high), 0.0, -1e30)


def turn_rows(src_ref, shift):
    n = src_ref.shape[1]
    part = shift & 7
    first = lax.shift_right_logical(shift, 3)
    groups = []
    for g in range(ROW_LEN // 8 + 1):
        start = pl.multiple_of(((first + g) & (ROW_LEN // 8 - 1)) * 8, 8)
        groups.append(src_ref[pl.ds(start, 8), :])
    wide = jnp.concatenate(groups, axis=0).reshape(ROW_LEN // 8 + 1, 8, n)
    back = (8 - part) & 7
    wide = pltpu.roll(wide, back, 1)
    place = lax.broadcasted_iota(jnp.int32, (ROW_LEN // 8, 8, n), 1)
    turned = jnp.where(place < 8 - part, wide[:-1], wide[1:])
    return turned.reshape(ROW_LEN, n)


def exponentials(s, half, bias_ref, safe):
    if half:
        s = s + bias_ref[...]
    if safe:
        s = s - jnp.max(s, axis=0, keepdims=True)
    e = jnp.exp2(s)
    return e.astype(BF), jnp.sum(e, axis=0, keepdims=True)


def out_of_range(sums):
    low, high = sums[0], sums[0]
    for one in sums[1:]:
        low, high = jnp.minimum(low, one), jnp.maximum(high, one)
    fine = (jnp.min(low) > 1e-20) & (jnp.max(high) < 1e20)
    return jnp.logical_not(fine)


def at(start, size, step):
    return pl.ds(start if isinstance(start, int) else pl.multiple_of(start, step), size)


def frozen_scores(half, h, qkv_ref, e_ref, bias_ref, safe):
    p, j = h // 2, h % 2
    lane = lax.broadcasted_iota(jnp.int32, (1, 128), 1)
    keep = (lane >= 64 * j) & (lane < 64 * (j + 1))
    rows = slice(half * HALF, (half + 1) * HALF)
    q2 = qkv_ref[rows, at(p * 128, 128, 128)]
    k2 = qkv_ref[rows, at(D + p * 128, 128, 128)]
    s = dot(k2 * keep.astype(F32).astype(BF), q2, 1, 1) * (LOG2E / 8.0)
    e_ref[half * HEADS + h], total = exponentials(s, half, bias_ref, safe)
    return total


def frozen_values(half, h, vt_ref, e_ref, ctxt_ref, total):
    rows = slice(half * HALF, (half + 1) * HALF)
    head = at(h * HEAD_DIM, HEAD_DIM, HEAD_DIM)
    ctxt_ref[head, rows] = (dot(vt_ref[head, rows], e_ref[half * HEADS + h]) * (1.0 / total)).astype(BF)


def start_copies(pairs, sems):
    for i, (src, dst) in enumerate(pairs):
        pltpu.make_async_copy(src, dst, sems.at[i]).start()


def wait_copies(pairs, sems, first, last):
    for i in range(first, last):
        src, dst = pairs[i]
        pltpu.make_async_copy(src, dst, sems.at[i]).wait()


def turn_kernel(first_ref, lens_ref, x_ref, gain_ref, turned_ref, normed_ref, raw_ref):
    shift, _ = row_starts(first_ref, lens_ref, pl.program_id(0))
    raw_ref[...] = x_ref[...].astype(F32)
    x = turn_rows(raw_ref, shift)
    turned_ref[...] = x.astype(BF)
    normed_ref[...] = (x * lax.rsqrt(jnp.mean(x * x, axis=1, keepdims=True) + EPS) * gain_ref[...].reshape(1, D)).astype(BF)


def attention_kernel(
    first_ref,
    lens_ref,
    turned_ref,
    normed_ref,
    wqa_ref,
    wqb_ref,
    wka_ref,
    wkb_ref,
    wva_ref,
    wvb_ref,
    woa_ref,
    wob_ref,
    mid_ref,
    wqkv_ref,
    wo_ref,
    qkv_ref,
    vt_ref,
    e_ref,
    ctxt_ref,
    bias_ref,
    sems,
):
    r = pl.program_id(0)
    cols = woa_ref.shape[0]
    copies = [(w, wqkv_ref.at[:, i * cols : (i + 1) * cols]) for i, w in enumerate((wqa_ref, wqb_ref, wka_ref, wkb_ref, wva_ref, wvb_ref))]
    copies += [(woa_ref, wo_ref.at[:cols]), (wob_ref, wo_ref.at[cols:])]

    @pl.when(r == 0)
    def _():
        start_copies(copies, sems)
        wait_copies(copies, sems, 0, 8)

    _, docs = row_starts(first_ref, lens_ref, r)
    fill_bias(bias_ref, docs)
    qkv_ref[...] = dot(normed_ref[...], wqkv_ref[...]).astype(BF)
    vt_ref[...] = qkv_ref[:, 2 * D :].T
    blocks = [(half, h) for half in range(2) for h in range(HEADS)]
    sums = [frozen_scores(half, h, qkv_ref, e_ref, bias_ref, False) for half, h in blocks]
    for (half, h), total in zip(blocks, sums):
        frozen_values(half, h, vt_ref, e_ref, ctxt_ref, total)

    @pl.when(out_of_range(sums))
    def _():
        for half in range(2):

            def again(h, carry):
                frozen_values(half, h, vt_ref, e_ref, ctxt_ref, frozen_scores(half, h, qkv_ref, e_ref, bias_ref, True))
                return carry

            lax.fori_loop(0, HEADS, again, 0)

    mid_ref[...] = turned_ref[...].astype(F32) + dot(ctxt_ref[...].T, wo_ref[...])


def head_mask(h, width):
    lane = lax.broadcasted_iota(jnp.int32, (1, width), 1)
    own = (lane >= 8 * h) & (lane < 8 * h + 8)
    if width > DS:
        own = own | (lane == DS + h) | (lane == DS + 16 + h)
    return own.astype(F32).astype(BF)


def head_rows(product, h):
    low, high = product[:SIDE_HEAD_DIM], product[SIDE_HEAD_DIM:]
    if isinstance(h, int):
        return high if h % 2 else low
    return jnp.where(h % 2 == 1, high, low)


def pair(base, h):
    return at(base + 16 * (h // 2), 16, 16)


def own_rows(h, base=0):
    return at(base + SIDE_HEAD_DIM * h, SIDE_HEAD_DIM, SIDE_HEAD_DIM)


def side_scores(half, h, k, qkvt_ref, e_ref, bias_ref, safe):
    rows = slice(half * HALF, (half + 1) * HALF)
    s = dot(k[rows] * head_mask(h, DS), qkvt_ref[:DS, rows]) * (LOG2E * SIDE_HEAD_DIM**-0.5)
    e_ref[half * SIDE_HEADS + h], total = exponentials(s, half, bias_ref, safe)
    return total


def side_values(half, h, qkvt_ref, e_ref, ctxt_ref, inv_ref, total):
    rows = slice(half * HALF, (half + 1) * HALF)
    inv = 1.0 / total
    mixed = dot(qkvt_ref[pair(2 * DS, h), rows], e_ref[half * SIDE_HEADS + h])
    ctxt_ref[own_rows(h), rows] = head_rows(mixed, h) * inv
    inv_ref[own_rows(h), rows] = jnp.broadcast_to(inv, (SIDE_HEAD_DIM, HALF))


def side_kernel(
    first_ref,
    lens_ref,
    mid_ref,
    w1a_ref,
    w1b_ref,
    w2a_ref,
    w2b_ref,
    fgain_ref,
    side_ref,
    cot_ref,
    alpha_ref,
    gain1_ref,
    gain2_ref,
    downt_ref,
    sq_ref,
    sk_ref,
    sv_ref,
    proj_ref,
    expand_ref,
    shrinkt_ref,
    bb_out_ref,
    out_ref,
    state_ref,
    mine_ref,
    other_ref,
    w2_ref,
    hid_ref,
    nb_ref,
    f_ref,
    grads_ref,
    acc_ref,
    cols_ref,
    wqkvt_ref,
    bias_ref,
    e_ref,
    et_ref,
    ds_ref,
    inv_ref,
    ctxt_ref,
    qkvt_ref,
    dq_ref,
):
    r = pl.program_id(0)
    last = pl.num_programs(0) - 1
    units = w1a_ref.shape[1]

    @pl.when(r == 0)
    def _():
        w2_ref[:units] = w2a_ref[...]
        w2_ref[units:] = w2b_ref[...]
        grads_ref[...] = jnp.zeros_like(grads_ref)
        acc_ref[...] = jnp.zeros_like(acc_ref)
        for i, ref in enumerate((alpha_ref, gain1_ref, gain2_ref)):
            cols_ref[i] = jnp.broadcast_to(jnp.broadcast_to(ref[...].reshape(1, DS), (8, DS)).T[:, 0:1], (DS, ROW_LEN))
        wqkvt_ref[:DS] = sq_ref[...].T
        wqkvt_ref[DS : 2 * DS] = sk_ref[...].T
        wqkvt_ref[2 * DS :] = sv_ref[...].T

    shift, docs = row_starts(first_ref, lens_ref, r)
    back = (ROW_LEN - shift) & (ROW_LEN - 1)
    fill_bias(bias_ref, docs)

    middle = mid_ref[...]
    nb_ref[...] = (middle * lax.rsqrt(jnp.mean(middle * middle, axis=1, keepdims=True) + EPS) * fgain_ref[...].reshape(1, D)).astype(BF)
    for i, w in enumerate((w1a_ref, w1b_ref)):
        for c in range(0, units, 256):
            hid_ref[:, i * units + c : i * units + c + 256] = gelu(dot(nb_ref[...], w[:, c : c + 256])).astype(BF)

    for c in range(0, ROW_LEN, 128):
        f_ref[c : c + 128] = mid_ref[c : c + 128] + dot(hid_ref[c : c + 128], w2_ref[...])
    bb = f_ref[...].astype(BF)
    bb_out_ref[...] = turn_rows(f_ref, back).astype(BF)

    gain1, gain2 = cols_ref[1], cols_ref[2]
    mixing = 1.0 / (1.0 + jnp.exp(cols_ref[0] * -10.0))
    side = pltpu.roll(side_ref[...].astype(F32), back, 1)
    cot = pltpu.roll(cot_ref[...].astype(F32), back, 1)
    cotb = cot.astype(BF)
    lowered = dot(downt_ref[...], bb, 1, 1)
    inputs = mixing * lowered + (1.0 - mixing) * side
    scale1 = lax.rsqrt(jnp.mean(inputs * inputs, axis=0, keepdims=True) + EPS)
    fnt = (inputs * scale1 * gain1).astype(BF)
    qkvt_ref[...] = dot(wqkvt_ref[...], fnt).astype(BF)
    k, v = qkvt_ref[DS : 2 * DS].T, qkvt_ref[2 * DS :].T
    blocks = [(half, h) for half in range(2) for h in range(SIDE_HEADS)]
    sums = [side_scores(half, h, k, qkvt_ref, e_ref, bias_ref, False) for half, h in blocks]
    for (half, h), total in zip(blocks, sums):
        side_values(half, h, qkvt_ref, e_ref, ctxt_ref, inv_ref, total)

    @pl.when(out_of_range(sums))
    def _():
        keys = qkvt_ref[DS : 2 * DS].T
        for half in range(2):

            def again(h, carry):
                side_values(half, h, qkvt_ref, e_ref, ctxt_ref, inv_ref, side_scores(half, h, keys, qkvt_ref, e_ref, bias_ref, True))
                return carry

            lax.fori_loop(0, SIDE_HEADS, again, 0)

    ctx = ctxt_ref[...]
    ctxb = ctx.astype(BF)
    middle_side = inputs + dot(proj_ref[...], ctxb, 0, 0)
    scale2 = lax.rsqrt(jnp.mean(middle_side * middle_side, axis=0, keepdims=True) + EPS)
    snt = (middle_side * scale2 * gain2).astype(BF)
    expanded = dot(expand_ref[...], snt, 0, 0)
    activated, slope = gelu_and_slope(expanded)
    activated = activated.astype(BF)
    side_out = middle_side + dot(shrinkt_ref[...], activated)
    out_ref[...] = pltpu.roll(side_out, shift, 1)

    activated_grad = dot(shrinkt_ref[...], cotb, 0, 0)
    expanded_grad = (activated_grad * slope).astype(BF)
    second_grad = dot(expand_ref[...], expanded_grad)
    w2 = second_grad * gain2
    ms = middle_side * scale2
    mean2 = jnp.mean(w2 * middle_side, axis=0, keepdims=True)
    middle_grad = cot + scale2 * w2 - ms * (scale2 * scale2) * mean2
    acc_ref[0] += second_grad * ms
    branch = middle_grad.astype(BF)
    context_grad = dot(proj_ref[...], branch).astype(BF).astype(F32)
    dop = (context_grad * inv_ref[...]).astype(BF)
    centre = jnp.sum((dop.astype(F32) * ctx).reshape(SIDE_HEADS, 8, ROW_LEN), axis=1)
    centre = jnp.concatenate([centre, jnp.zeros((4, ROW_LEN), F32)], axis=0)
    chigh = centre.astype(BF)
    clow = (centre - chigh.astype(F32)).astype(BF)
    dstack = jnp.concatenate([dop, -chigh, -clow], axis=0)
    vones = jnp.concatenate([v, jnp.ones((ROW_LEN, 32), BF)], axis=1)
    root = SIDE_HEAD_DIM**-0.5
    for n, (half, h) in enumerate(blocks):
        rows = slice(half * HALF, (half + 1) * HALF)
        dp = dot(vones[rows] * head_mask(h, 128), dstack[:, rows])
        ds_ref[n] = (e_ref[n].astype(F32) * dp).astype(BF)
        et_ref[n] = e_ref[n].T
    for n, (half, h) in enumerate(blocks):
        rows = slice(half * HALF, (half + 1) * HALF)
        dq_ref[own_rows(h), rows] = head_rows(dot(qkvt_ref[pair(DS, h), rows], ds_ref[n]), h) * root
        e_ref[n] = ds_ref[n].T
    for n, (half, h) in enumerate(blocks):
        rows = slice(half * HALF, (half + 1) * HALF)
        dq_ref[own_rows(h, 2 * DS), rows] = head_rows(dot(dop[16 * (h // 2) : 16 * (h // 2) + 16, rows], et_ref[n]), h)
    for n, (half, h) in enumerate(blocks):
        rows = slice(half * HALF, (half + 1) * HALF)
        dq_ref[own_rows(h, DS), rows] = head_rows(dot(qkvt_ref[pair(0, h), rows], e_ref[n]), h) * root
    dqkvt = dq_ref[...].astype(BF)
    first_grad = dot(wqkvt_ref[...], dqkvt, 0, 0)
    w1 = first_grad * gain1
    ins = inputs * scale1
    mean1 = jnp.mean(w1 * inputs, axis=0, keepdims=True)
    input_grad = middle_grad + scale1 * w1 - ins * (scale1 * scale1) * mean1
    acc_ref[1] += first_grad * ins
    acc_ref[2] += input_grad * (lowered - side)
    state_ref[...] = pltpu.roll((1.0 - mixing) * input_grad, shift, 1)
    low = D + 2 * SFF
    grads_ref[:, 0:D] += dot((mixing * input_grad).astype(BF), bb)
    grads_ref[:, D : D + SFF] += dot(snt, expanded_grad, 1, 1)
    grads_ref[:, D + SFF : low] += dot(cotb, activated, 1, 1)
    grads_ref[:, low : low + 3 * DS] += dot(fnt, dqkvt, 1, 1)
    grads_ref[:, low + 3 * DS : low + 4 * DS] += dot(ctxb, branch, 1, 1)

    @pl.when(r == last)
    def _():
        gate = 1.0 / (1.0 + jnp.exp(cols_ref[0][:, 0:1] * -10.0))
        total = [jnp.sum(acc_ref[i], axis=1, keepdims=True) for i in range(3)]
        total[2] = total[2] * (gate * (1.0 - gate)) * 10.0
        place = lax.broadcasted_iota(jnp.int32, (DS, 128), 1)
        grads_ref[:, low + 4 * DS :] = jnp.where(place == 0, total[0], jnp.where(place == 1, total[1], jnp.where(place == 2, total[2], 0.0)))
        half = DS // 2
        tensor = (first_ref[0] != 0).astype(jnp.int32)
        mine_ref[...] = grads_ref[pl.ds(pl.multiple_of(tensor * half, 8), half), :].astype(BF)
        other_ref[...] = grads_ref[pl.ds(pl.multiple_of((1 - tensor) * half, 8), half), :].astype(BF)


def whole(shape):
    return pl.BlockSpec(shape, lambda r, *_: (0,) * len(shape), pipeline_mode=pl.Buffered(1))


def params(limit):
    return pltpu.CompilerParams(vmem_limit_bytes=limit * 1024 * 1024, dimension_semantics=("arbitrary",))


def swap(x):
    return lax.ppermute(x, "tensor", [(0, 1), (1, 0)])


def sum_over(mine, other, batch):
    place = lax.axis_index("batch")
    group = place & 3

    def trade(x, bits):
        return lax.ppermute(x, "batch", [(i, i ^ bits) for i in range(batch)])

    def pick(parts, k):
        return jnp.where(k == 0, parts[0], jnp.where(k == 1, parts[1], jnp.where(k == 2, parts[2], parts[3])))

    part = mine.astype(F32) + swap(other).astype(F32)
    bit, grouped = 1, batch >= 4
    if grouped:
        parts = jnp.split(part.astype(BF), 4, axis=1)
        got = [trade(pick(parts, group ^ m), m).astype(F32) for m in (1, 2, 3)]
        part = (pick(parts, group).astype(F32) + got[0]) + (got[1] + got[2])
        bit = 4
    while bit < batch:
        sent = part.astype(BF)
        part = sent.astype(F32) + trade(sent, bit).astype(F32)
        bit *= 2
    sent = part.astype(BF)
    if grouped:
        got = [sent] + [trade(sent, m) for m in (1, 2, 3)]
        sent = jnp.concatenate([pick(got, group ^ j) for j in range(4)], axis=1)
    got = swap(sent)
    upper = lax.axis_index("tensor") != 0
    return jnp.concatenate([jnp.where(upper, got, sent), jnp.where(upper, sent, got)], axis=0).astype(F32)


def make_body(batch):
    def body(
        hidden_in,
        lengths,
        attn_gain,
        attn_query,
        attn_key,
        attn_value,
        attn_out,
        ffn_gain,
        ffn_in,
        ffn_out,
        side_state,
        gate_alpha,
        down_w,
        side_attn_gain,
        side_query,
        side_key,
        side_value,
        side_proj,
        side_ffn_gain,
        side_expand,
        side_shrink,
        cotangent,
    ):
        tokens = hidden_in.shape[0]
        rows = tokens // ROW_LEN
        units = ffn_in.shape[1]
        t = lax.axis_index("tensor")
        first = (t * rows).astype(jnp.int32).reshape(1)
        tile = pl.BlockSpec((ROW_LEN, D), lambda r, *_: (r, 0))
        hbm = pl.BlockSpec(memory_space=pltpu.HBM)
        lens = lengths.T

        def kernel(body, name, limit, in_specs, out_specs, out_shape, scratch):
            return pl.pallas_call(
                body,
                grid_spec=pltpu.PrefetchScalarGridSpec(
                    num_scalar_prefetch=2, grid=(rows,), in_specs=in_specs, out_specs=out_specs, scratch_shapes=scratch
                ),
                out_shape=out_shape,
                compiler_params=params(limit),
                name=name,
            )

        own_attn = (attn_query, attn_key, attn_value, attn_out)
        far_attn = [swap(w) for w in own_attn]
        turned, normed = kernel(
            turn_kernel,
            "turn_rows",
            9,
            [tile, whole((D,))],
            [tile, tile],
            [jax.ShapeDtypeStruct((tokens, D), BF)] * 2,
            [pltpu.VMEM((ROW_LEN, D), F32)],
        )(first, lens, hidden_in, attn_gain)
        far_attn, turned, normed, ffn_in, ffn_out = lax.optimization_barrier((far_attn, turned, normed, ffn_in, ffn_out))
        far_ffn = [swap(w) for w in (ffn_in, ffn_out)]
        mid = kernel(
            attention_kernel,
            "attention",
            22,
            [tile, tile] + [hbm] * 8,
            tile,
            jax.ShapeDtypeStruct((tokens, D), F32),
            [
                pltpu.VMEM((D, 3 * D), BF),
                pltpu.VMEM((D, D), BF),
                pltpu.VMEM((ROW_LEN, 3 * D), BF),
                pltpu.VMEM((D, ROW_LEN), BF),
                pltpu.VMEM((2 * HEADS, HALF, HALF), BF),
                pltpu.VMEM((D, ROW_LEN), BF),
                pltpu.VMEM((HALF, HALF), F32),
                pltpu.SemaphoreType.DMA((8,)),
            ],
        )(first, lens, turned, normed, *[w for both in zip(own_attn, far_attn) for w in both])
        side_tile = pl.BlockSpec((DS, ROW_LEN), lambda r, *_: (0, r))
        side = pltpu.VMEM((DS, ROW_LEN), F32)
        square = pltpu.VMEM((2 * SIDE_HEADS, HALF, HALF), BF)
        backbone, side_out, state_grad, mine, other = kernel(
            side_kernel,
            "forward_and_back",
            30,
            [tile]
            + [whole((D, units))] * 2
            + [whole((units, D))] * 2
            + [whole((D,)), side_tile, side_tile]
            + [whole((DS,))] * 3
            + [whole((DS, D))]
            + [whole((DS, DS))] * 4
            + [whole((DS, SFF))] * 2,
            [tile, side_tile, side_tile] + [pl.BlockSpec((DS // 2, GRAD_LANES), lambda r, *_: (0, 0))] * 2,
            [
                jax.ShapeDtypeStruct((tokens, D), BF),
                jax.ShapeDtypeStruct((DS, tokens), F32),
                jax.ShapeDtypeStruct((DS, tokens), F32),
                jax.ShapeDtypeStruct((DS // 2, GRAD_LANES), BF),
                jax.ShapeDtypeStruct((DS // 2, GRAD_LANES), BF),
            ],
            [
                pltpu.VMEM((2 * units, D), BF),
                pltpu.VMEM((ROW_LEN, 2 * units), BF),
                pltpu.VMEM((ROW_LEN, D), BF),
                pltpu.VMEM((ROW_LEN, D), F32),
                pltpu.VMEM((DS, GRAD_LANES), F32),
                pltpu.VMEM((3, DS, ROW_LEN), F32),
                pltpu.VMEM((3, DS, ROW_LEN), F32),
                pltpu.VMEM((3 * DS, DS), BF),
                pltpu.VMEM((HALF, HALF), F32),
                square,
                square,
                square,
                side,
                side,
                pltpu.VMEM((3 * DS, ROW_LEN), BF),
                pltpu.VMEM((3 * DS, ROW_LEN), F32),
            ],
        )(
            first,
            lens,
            mid,
            ffn_in,
            far_ffn[0],
            ffn_out,
            far_ffn[1],
            ffn_gain,
            side_state.T,
            cotangent.T,
            gate_alpha,
            side_attn_gain,
            side_ffn_gain,
            down_w.T,
            side_query,
            side_key,
            side_value,
            side_proj,
            side_expand,
            side_shrink.T,
        )
        g = sum_over(mine, other, batch)
        low = D + 2 * SFF
        return (
            backbone,
            side_out.T,
            state_grad.T,
            g[:, :D].T,
            g[:, low + 4 * DS + 2],
            g[:, low + 4 * DS + 1],
            g[:, low : low + DS],
            g[:, low + DS : low + 2 * DS],
            g[:, low + 2 * DS : low + 3 * DS],
            g[:, low + 3 * DS : low + 4 * DS],
            g[:, low + 4 * DS],
            g[:, D : D + SFF],
            g[:, D + SFF : low].T,
        )

    return body


def solution(mesh):
    split = P(("batch", "tensor"), None)
    return jax.shard_map(
        make_body(mesh.shape["batch"]),
        mesh=mesh,
        in_specs=(
            split,
            P("batch", None),
            P(),
            P(None, "tensor"),
            P(None, "tensor"),
            P(None, "tensor"),
            P("tensor", None),
            P(),
            P(None, "tensor"),
            P("tensor", None),
            split,
            P(),
            P(),
            P(),
            P(),
            P(),
            P(),
            P(),
            P(),
            P(),
            P(),
            split,
        ),
        out_specs=(split, split, split) + (P(),) * 10,
        check_vma=False,
    )
```

time: 160 us -> 129 us (0.81)
  Pallas kernels: 111 us -> 89.2 us
  waiting for transfers between devices: 25.9 us -> 14.5 us
  local copies, waits for them, and re-layouts: 2.99 us -> 6.55 us
    pallas_call x3, Pallas kernels: 111 us -> 89.2 us  [the longest x1 63.2 us: body(): kernel(side_kernel, 'forward_and_back', 30, [tile] + [whole((D, units))]...]
    ppermute x8, waiting for transfers between devices: 10.6 us -> 2.51 us  [swap(): return lax.ppermute(x, 'tensor', [(0, 1), (1, 0)])]
    unnamed x6 -> x46, local copies, waits for them, and re-layouts: 2.26 us -> 5.82 us
    ppermute x6 -> x8, waiting for transfers between devices: 15.4 us -> 12 us  [trade(): return lax.ppermute(x, 'batch', [(i, i ^ bits) for i in range(batch)])]
    ppermute x6 -> x8, starting transfers between devices: 13 us -> 12.6 us  [trade(): return lax.ppermute(x, 'batch', [(i, i ^ bits) for i in range(batch)])]
  transfers between devices with their start and end apart: 14 -> 16, of which waited for: 9 -> 10; matrix products, arithmetic and copies ran while one was open for 0% -> 0% of each run, Pallas kernels for 24% -> 20%
where the time goes in v3:
time: 129 us
  Pallas kernels  89.2 us (69%)
  starting transfers between devices  14.8 us (11%)
  waiting for transfers between devices  14.5 us (11%)
  local copies, waits for them, and re-layouts  6.55 us (5%)
  other arithmetic  2.5 us (2%)
    pallas_call x1, Pallas kernels, body(): kernel(side_kernel, 'forward_and_back', 30, [tile] + [whole((D, units))]...  63.2 us
    pallas_call x1, Pallas kernels, body(): kernel(attention_kernel, 'attention', 22, [tile, tile] + [hbm] * 8, tile,...  22.8 us
    ppermute x8, starting transfers between devices, trade(): return lax.ppermute(x, 'batch', [(i, i ^ bits) for i in range(batch)])  12.6 us
    ppermute x8, waiting for transfers between devices, trade(): return lax.ppermute(x, 'batch', [(i, i ^ bits) for i in range(batch)])  12 us
    unnamed x46, local copies, waits for them, and re-layouts  5.82 us
    pallas_call x1, Pallas kernels, body(): kernel(turn_kernel, 'turn_rows', 9, [tile, whole((D,))], [tile, tile], [j...  3.24 us
  transfers between devices with their start and end apart: 16, of which 10 were waited for; matrix products, arithmetic and copies ran while one was open for 0% of the time, Pallas kernels for 20%

profile of v3, /device:TPU:0, one launch (start us, length us, event | category | flops | bytes accessed | tf_op | source)
XLA Modules:
  0.0 128.6 jit_solution(7719783758351123515)
XLA Ops:
  0.7 0.5 collective-permute-start
  1.3 0.4 collective-permute-start.2
  1.8 2.1 %copy-done = bf16[2560,768]{1,0:T(8,128)(2,1)S(1)} copy-done((bf16[2560,768]{1,0:T(8,128)(2,1)S(1)}, bf16[2560,768]{1,0:T(8,128)(2,1)}, u32[]{:S(2)}) %copy-start) | copy-done | bytes 3932184
  3.9 0.7 copy-done.12
  4.6 0.7 copy-done.19
  5.3 3.2 %turn_rows.1 = (bf16[2560,768]{1,0:T(8,128)(2,1)S(1)}, bf16[2560,768]{1,0:T(8,128)(2,1)S(1)}) custom-call(s32[1]{0:T(128)} %bitcast.first_ref, s32[8,10]{1,0:T(8,128)S(1)} %bitcast.16, bf16[2560,768]{1,0:T(8,128)(2,1)S(1)} %copy-done, f32[768]{0:T(1024)S(1)} %copy-done.19), custom_call_target="tpu_custom_call" | custom-call | tf_op jit(solution)/shard_map/turn_rows/pallas_call | solution.py:498
  8.6 0.5 collective-permute-start.4
  9.2 1.2 copy-done.5
  10.4 1.1 copy-done.6
  11.5 22.8 %attention.1.mid_ref = f32[2560,768]{1,0:T(8,128)S(1)} custom-call(s32[1]{0:T(128)} %bitcast.first_ref, s32[8,10]{1,0:T(8,128)S(1)} %bitcast.17, bf16[2560,768]{1,0:T(8,128)(2,1)S(1)} %get-tuple-element.30.turned_ref, bf16[2560,768]{1,0:T(8,128)(2,1)S(1)} %get-tuple-element.31.normed_ref, bf16[768,384]{1,0:T(8,128)(2,1)S(1)} %copy-done.3, ...), custom_call_target="tpu_custom_call" | custom-call | tf_op jit(solution)/shard_map/attention/pallas_call | solution.py:509
  34.5 63.2 %forward_and_back.1 = (bf16[2560,768]{1,0:T(8,128)(2,1)}, f32[96,2560]{1,0:T(8,128)}, f32[96,2560]{1,0:T(8,128)}, bf16[48,2048]{1,0:T(8,128)(2,1)S(1)}, bf16[48,2048]{1,0:T(8,128)(2,1)S(1)}) custom-call(s32[1]{0:T(128)} %bitcast.first_ref, s32[8,10]{1,0:T(8,128)S(1)} %bitcast.18, f32[2560,768]{1,0:T(8,128)S(1)} %attention.1.mid_ref, ...), custom_call_target="tpu_custom_call" | custom-call | tf_op jit(solution)/shard_map/forward_and_back/pallas_call | solution.py:530
  97.7 0.5 collective-permute-start.6
  98.1 1.1 collective-permute-done.6
  99.3 2.9 %collective-permute-start.7 = (bf16[48,512]{1,0:T(8,128)(2,1)S(1)}, bf16[48,512]{1,0:T(8,128)(2,1)S(1)}, u32[]{:S(2)}, u32[]{:S(2)}) collective-permute-start(bf16[48,512]{1,0:T(8,128)(2,1)S(1)} %get-tuple-element.58), channel_id=1, source_target_pairs={{0,2},{2,0},{4,6},{6,4},{8,10},{10,8},{12,14},{14,12},{16,18},{18,... | collective-permute-start | bytes 147464 | tf_op jit(solution)/shard_map/ppermute | solution.py:426
  102.2 1.5 %collective-permute-start.8 = (bf16[48,512]{1,0:T(8,128)(2,1)S(1)}, bf16[48,512]{1,0:T(8,128)(2,1)S(1)}, u32[]{:S(2)}, u32[]{:S(2)}) collective-permute-start(bf16[48,512]{1,0:T(8,128)(2,1)S(1)} %get-tuple-element.59), channel_id=1, source_target_pairs={{0,4},{2,6},{4,0},{6,2},{8,12},{10,14},{12,8},{14,10},{16,20},{18,... | collective-permute-start | bytes 147464 | tf_op jit(solution)/shard_map/ppermute | solution.py:426
  103.8 0.4 collective-permute-done.7
  104.3 2.0 %collective-permute-done.8 = bf16[48,512]{1,0:T(8,128)(2,1)S(1)} collective-permute-done((bf16[48,512]{1,0:T(8,128)(2,1)S(1)}, bf16[48,512]{1,0:T(8,128)(2,1)S(1)}, u32[]{:S(2)}, u32[]{:S(2)}) %collective-permute-start.8) | collective-permute-done | bytes 49184 | tf_op jit(solution)/shard_map/ppermute | solution.py:426
  106.3 2.5 %collective-permute-done.9 = bf16[48,512]{1,0:T(8,128)(2,1)S(1)} collective-permute-done((bf16[48,512]{1,0:T(8,128)(2,1)S(1)}, bf16[48,512]{1,0:T(8,128)(2,1)S(1)}, u32[]{:S(2)}, u32[]{:S(2)}) %collective-permute-start.9) | collective-permute-done | bytes 49184 | tf_op jit(solution)/shard_map/ppermute | solution.py:426
  108.8 1.6 %collective-permute-start.10 = (bf16[48,512]{1,0:T(8,128)(2,1)S(1)}, bf16[48,512]{1,0:T(8,128)(2,1)S(1)}, u32[]{:S(2)}, u32[]{:S(2)}) collective-permute-start(bf16[48,512]{1,0:T(8,128)(2,1)S(1)} %add_convert_fusion.3), channel_id=1, source_target_pairs={{0,8},{2,10},{4,12},{6,14},{8,0},{10,2},{12,4},{14,6},{16,24},{18,... | collective-permute-start | bytes 147464 | tf_op jit(solution)/shard_map/ppermute | solution.py:426
  110.5 2.5 %collective-permute-done.10 = bf16[48,512]{1,0:T(8,128)(2,1)S(1)} collective-permute-done((bf16[48,512]{1,0:T(8,128)(2,1)S(1)}, bf16[48,512]{1,0:T(8,128)(2,1)S(1)}, u32[]{:S(2)}, u32[]{:S(2)}) %collective-permute-start.10) | collective-permute-done | bytes 49184 | tf_op jit(solution)/shard_map/ppermute | solution.py:426
  113.0 2.9 %collective-permute-start.11 = (bf16[48,512]{1,0:T(8,128)(2,1)S(1)}, bf16[48,512]{1,0:T(8,128)(2,1)S(1)}, u32[]{:S(2)}, u32[]{:S(2)}) collective-permute-start(bf16[48,512]{1,0:T(8,128)(2,1)S(1)} %add_convert_fusion.2), channel_id=1, source_target_pairs={{0,16},{2,18},{4,20},{6,22},{8,24},{10,26},{12,28},{14,30},{16,0},... | collective-permute-start | bytes 147464 | tf_op jit(solution)/shard_map/ppermute | solution.py:426
  115.9 2.2 %collective-permute-done.11 = bf16[48,512]{1,0:T(8,128)(2,1)S(1)} collective-permute-done((bf16[48,512]{1,0:T(8,128)(2,1)S(1)}, bf16[48,512]{1,0:T(8,128)(2,1)S(1)}, u32[]{:S(2)}, u32[]{:S(2)}) %collective-permute-start.11) | collective-permute-done | bytes 49184 | tf_op jit(solution)/shard_map/ppermute | solution.py:426
  118.1 0.6 collective-permute-start.12
  119.0 2.7 %collective-permute-start.14 = (bf16[48,512]{1,0:T(8,128)(2,1)S(1)}, bf16[48,512]{1,0:T(8,128)(2,1)S(1)}, u32[]{:S(2)}, u32[]{:S(2)}) collective-permute-start(bf16[48,512]{1,0:T(8,128)(2,1)S(1)} %add_convert_fusion.1), channel_id=1, source_target_pairs={{0,6},{2,4},{4,2},{6,0},{8,14},{10,12},{12,10},{14,8},{16,22},{18,... | collective-permute-start | bytes 147464 | tf_op jit(solution)/shard_map/ppermute | solution.py:426
  121.6 0.6 collective-permute-done.12
  122.2 0.5 collective-permute-done.13
  122.8 1.2 collective-permute-done.14
  124.1 1.4 %collective-permute-done.15 = bf16[48,2048]{1,0:T(8,128)(2,1)S(1)} collective-permute-done((bf16[48,2048]{1,0:T(8,128)(2,1)S(1)}, bf16[48,2048]{1,0:T(8,128)(2,1)S(1)}, u32[]{:S(2)}, u32[]{:S(2)}) %collective-permute-start.15) | collective-permute-done | bytes 196640 | tf_op jit(solution)/shard_map/ppermute | solution.py:418
  125.6 0.7 convert_bitcast_fusion
  126.4 0.7 maximum_convert_fusion.2
  127.1 0.7 convert_reduce_fusion
  127.9 0.7 slice_bitcast_fusion
  (63 shorter events, 1.1 us)
Async XLA Ops:
  0.6 8.5 %copy-start.13 = (s32[10,8]{0,1:T(8,128)S(1)}, s32[10,8]{0,1:T(8,128)}, u32[]{:S(2)}) copy-start(s32[10,8]{0,1:T(8,128)} %param.23) | copy-start | bytes 964
  0.7 7.8 %collective-permute-start = (bf16[768,384]{1,0:T(8,128)(2,1)}, bf16[768,384]{1,0:T(8,128)(2,1)S(1)}, u32[]{:S(2)}, u32[]{:S(2)}) collective-permute-start(bf16[768,384]{1,0:T(8,128)(2,1)} %wqa_ref.1), channel_id=1, source_target_pairs={{0,1},{1,0},{2,3},{3,2},{4,5},{5,4},{6,7},{7,6},{8,9},{9,8},{10,11... | collective-permute-start | bytes 1769480 | tf_op jit(solution)/shard_map/ppermute | solution.py:418
  1.2 7.3 %collective-permute-start.1 = (bf16[768,384]{1,0:T(8,128)(2,1)}, bf16[768,384]{1,0:T(8,128)(2,1)S(1)}, u32[]{:S(2)}, u32[]{:S(2)}) collective-permute-start(bf16[768,384]{1,0:T(8,128)(2,1)} %wka_ref.1), channel_id=1, source_target_pairs={{0,1},{1,0},{2,3},{3,2},{4,5},{5,4},{6,7},{7,6},{8,9},{9,8},{10,11... | collective-permute-start | bytes 1769480 | tf_op jit(solution)/shard_map/ppermute | solution.py:418
  1.3 7.3 %collective-permute-start.2 = (bf16[768,384]{1,0:T(8,128)(2,1)}, bf16[768,384]{1,0:T(8,128)(2,1)S(1)}, u32[]{:S(2)}, u32[]{:S(2)}) collective-permute-start(bf16[768,384]{1,0:T(8,128)(2,1)} %wva_ref.1), channel_id=1, source_target_pairs={{0,1},{1,0},{2,3},{3,2},{4,5},{5,4},{6,7},{7,6},{8,9},{9,8},{10,11... | collective-permute-start | bytes 1769480 | tf_op jit(solution)/shard_map/ppermute | solution.py:418
  1.7 6.9 %collective-permute-start.3 = (bf16[384,768]{1,0:T(8,128)(2,1)}, bf16[384,768]{1,0:T(8,128)(2,1)S(1)}, u32[]{:S(2)}, u32[]{:S(2)}) collective-permute-start(bf16[384,768]{1,0:T(8,128)(2,1)} %woa_ref.1), channel_id=1, source_target_pairs={{0,1},{1,0},{2,3},{3,2},{4,5},{5,4},{6,7},{7,6},{8,9},{9,8},{10,11... | collective-permute-start | bytes 1769480 | tf_op jit(solution)/shard_map/ppermute | solution.py:418
  5.3 3.9 %copy-start.4 = (bf16[768,384]{1,0:T(8,128)(2,1)S(1)}, bf16[768,384]{1,0:T(8,128)(2,1)}, u32[]{:S(2)}) copy-start(bf16[768,384]{1,0:T(8,128)(2,1)} %wka_ref.1) | copy-start | bytes 1769476
  8.5 25.8 %copy-start.20 = (f32[96]{0:T(128)S(1)}, f32[96]{0:T(128)}, u32[]{:S(2)}) copy-start(f32[96]{0:T(128)} %alpha_ref.1) | copy-start | bytes 1156
  8.6 25.8 %copy-start.21 = (f32[96]{0:T(128)S(1)}, f32[96]{0:T(128)}, u32[]{:S(2)}) copy-start(f32[96]{0:T(128)} %gain1_ref.1) | copy-start | bytes 1156
  8.6 25.8 %copy-start.22 = (f32[96]{0:T(128)S(1)}, f32[96]{0:T(128)}, u32[]{:S(2)}) copy-start(f32[96]{0:T(128)} %gain2_ref.1) | copy-start | bytes 1156
  8.6 25.8 %copy-start.2 = (bf16[1536,768]{1,0:T(8,128)(2,1)S(1)}, bf16[1536,768]{1,0:T(8,128)(2,1)}, u32[]{:S(2)}) copy-start(bf16[1536,768]{1,0:T(8,128)(2,1)} %w2a_ref) | copy-start | bytes 7077892
  8.6 25.8 %collective-permute-start.4 = (bf16[768,1536]{1,0:T(8,128)(2,1)S(1)}, bf16[768,1536]{1,0:T(8,128)(2,1)S(1)}, u32[]{:S(2)}, u32[]{:S(2)}) collective-permute-start(bf16[768,1536]{1,0:T(8,128)(2,1)S(1)} %copy-done.1), channel_id=1, source_target_pairs={{0,1},{1,0},{2,3},{3,2},{4,5},{5,4},{6,7},{7,6},{8,9},{9,8},{10,11... | collective-permute-start | bytes 7077896 | tf_op jit(solution)/shard_map/ppermute | solution.py:418
  9.1 25.3 %collective-permute-start.5 = (bf16[1536,768]{1,0:T(8,128)(2,1)}, bf16[1536,768]{1,0:T(8,128)(2,1)S(1)}, u32[]{:S(2)}, u32[]{:S(2)}) collective-permute-start(bf16[1536,768]{1,0:T(8,128)(2,1)} %w2a_ref), channel_id=1, source_target_pairs={{0,1},{1,0},{2,3},{3,2},{4,5},{5,4},{6,7},{7,6},{8,9},{9,8},{10,11... | collective-permute-start | bytes 7077896 | tf_op jit(solution)/shard_map/ppermute | solution.py:418
  11.4 23.0 %copy-start.7 = (bf16[2560,96]{0,1:T(8,128)(2,1)S(1)}, bf16[2560,96]{0,1:T(8,128)(2,1)}, u32[]{:S(2)}) copy-start(bf16[2560,96]{0,1:T(8,128)(2,1)} %param.32) | copy-start | bytes 1474564
  11.4 23.0 %copy-start.8 = (bf16[2560,96]{0,1:T(8,128)(2,1)S(1)}, bf16[2560,96]{0,1:T(8,128)(2,1)}, u32[]{:S(2)}) copy-start(bf16[2560,96]{0,1:T(8,128)(2,1)} %param.43) | copy-start | bytes 1474564
  11.4 23.0 %copy-start.9 = (bf16[768,96]{0,1:T(8,128)(2,1)S(1)}, bf16[768,96]{0,1:T(8,128)(2,1)}, u32[]{:S(2)}) copy-start(bf16[768,96]{0,1:T(8,128)(2,1)} %param.34) | copy-start | bytes 442372
  11.4 23.0 %copy-start.10 = (bf16[96,384]{1,0:T(8,128)(2,1)S(1)}, bf16[96,384]{1,0:T(8,128)(2,1)}, u32[]{:S(2)}) copy-start(bf16[96,384]{1,0:T(8,128)(2,1)} %expand_ref.1) | copy-start | bytes 221188
  11.4 23.0 %copy-start.11 = (bf16[384,96]{0,1:T(8,128)(2,1)S(1)}, bf16[384,96]{0,1:T(8,128)(2,1)}, u32[]{:S(2)}) copy-start(bf16[384,96]{0,1:T(8,128)(2,1)} %param.42) | copy-start | bytes 221188
  11.5 23.0 %copy-start.14 = (bf16[96,96]{1,0:T(8,128)(2,1)S(1)}, bf16[96,96]{1,0:T(8,128)(2,1)}, u32[]{:S(2)}) copy-start(bf16[96,96]{1,0:T(8,128)(2,1)} %sq_ref.1) | copy-start | bytes 55300
  11.5 23.0 %copy-start.15 = (bf16[96,96]{1,0:T(8,128)(2,1)S(1)}, bf16[96,96]{1,0:T(8,128)(2,1)}, u32[]{:S(2)}) copy-start(bf16[96,96]{1,0:T(8,128)(2,1)} %sk_ref.1) | copy-start | bytes 55300
  11.5 23.0 %copy-start.16 = (bf16[96,96]{1,0:T(8,128)(2,1)S(1)}, bf16[96,96]{1,0:T(8,128)(2,1)}, u32[]{:S(2)}) copy-start(bf16[96,96]{1,0:T(8,128)(2,1)} %sv_ref.1) | copy-start | bytes 55300
  11.5 23.0 %copy-start.17 = (bf16[96,96]{1,0:T(8,128)(2,1)S(1)}, bf16[96,96]{1,0:T(8,128)(2,1)}, u32[]{:S(2)}) copy-start(bf16[96,96]{1,0:T(8,128)(2,1)} %proj_ref.1) | copy-start | bytes 55300
  11.5 23.0 %copy-start.18 = (f32[768]{0:T(1024)S(1)}, f32[768]{0:T(1024)}, u32[]{:S(2)}) copy-start(f32[768]{0:T(1024)} %fgain_ref.1) | copy-start | bytes 9220
  97.7 1.5 %collective-permute-start.6 = (bf16[48,2048]{1,0:T(8,128)(2,1)S(1)}, bf16[48,2048]{1,0:T(8,128)(2,1)S(1)}, u32[]{:S(2)}, u32[]{:S(2)}) collective-permute-start(bf16[48,2048]{1,0:T(8,128)(2,1)S(1)} %get-tuple-element.42), channel_id=1, source_target_pairs={{0,1},{1,0},{2,3},{3,2},{4,5},{5,4},{6,7},{7,6},{8,9},{9,8},{10,11... | collective-permute-start | bytes 589832 | tf_op jit(solution)/shard_map/ppermute | solution.py:418
  99.3 5.0 %collective-permute-start.7 = (bf16[48,512]{1,0:T(8,128)(2,1)S(1)}, bf16[48,512]{1,0:T(8,128)(2,1)S(1)}, u32[]{:S(2)}, u32[]{:S(2)}) collective-permute-start(bf16[48,512]{1,0:T(8,128)(2,1)S(1)} %get-tuple-element.58), channel_id=1, source_target_pairs={{0,2},{2,0},{4,6},{6,4},{8,10},{10,8},{12,14},{14,12},{16,18},{18,... | collective-permute-start | bytes 147464 | tf_op jit(solution)/shard_map/ppermute | solution.py:426
  102.2 4.1 %collective-permute-start.8 = (bf16[48,512]{1,0:T(8,128)(2,1)S(1)}, bf16[48,512]{1,0:T(8,128)(2,1)S(1)}, u32[]{:S(2)}, u32[]{:S(2)}) collective-permute-start(bf16[48,512]{1,0:T(8,128)(2,1)S(1)} %get-tuple-element.59), channel_id=1, source_target_pairs={{0,4},{2,6},{4,0},{6,2},{8,12},{10,14},{12,8},{14,10},{16,20},{18,... | collective-permute-start | bytes 147464 | tf_op jit(solution)/shard_map/ppermute | solution.py:426
  103.7 5.1 %collective-permute-start.9 = (bf16[48,512]{1,0:T(8,128)(2,1)S(1)}, bf16[48,512]{1,0:T(8,128)(2,1)S(1)}, u32[]{:S(2)}, u32[]{:S(2)}) collective-permute-start(bf16[48,512]{1,0:T(8,128)(2,1)S(1)} %select_select_fusion.4), channel_id=1, source_target_pairs={{0,6},{2,4},{4,2},{6,0},{8,14},{10,12},{12,10},{14,8},{16,22},{18,... | collective-permute-start | bytes 147464 | tf_op jit(solution)/shard_map/ppermute | solution.py:426
  108.8 4.2 %collective-permute-start.10 = (bf16[48,512]{1,0:T(8,128)(2,1)S(1)}, bf16[48,512]{1,0:T(8,128)(2,1)S(1)}, u32[]{:S(2)}, u32[]{:S(2)}) collective-permute-start(bf16[48,512]{1,0:T(8,128)(2,1)S(1)} %add_convert_fusion.3), channel_id=1, source_target_pairs={{0,8},{2,10},{4,12},{6,14},{8,0},{10,2},{12,4},{14,6},{16,24},{18,... | collective-permute-start | bytes 147464 | tf_op jit(solution)/shard_map/ppermute | solution.py:426
  113.0 5.1 %collective-permute-start.11 = (bf16[48,512]{1,0:T(8,128)(2,1)S(1)}, bf16[48,512]{1,0:T(8,128)(2,1)S(1)}, u32[]{:S(2)}, u32[]{:S(2)}) collective-permute-start(bf16[48,512]{1,0:T(8,128)(2,1)S(1)} %add_convert_fusion.2), channel_id=1, source_target_pairs={{0,16},{2,18},{4,20},{6,22},{8,24},{10,26},{12,28},{14,30},{16,0},... | collective-permute-start | bytes 147464 | tf_op jit(solution)/shard_map/ppermute | solution.py:426
  118.1 4.2 %collective-permute-start.12 = (bf16[48,512]{1,0:T(8,128)(2,1)S(1)}, bf16[48,512]{1,0:T(8,128)(2,1)S(1)}, u32[]{:S(2)}, u32[]{:S(2)}) collective-permute-start(bf16[48,512]{1,0:T(8,128)(2,1)S(1)} %add_convert_fusion.1), channel_id=1, source_target_pairs={{0,2},{2,0},{4,6},{6,4},{8,10},{10,8},{12,14},{14,12},{16,18},{18,... | collective-permute-start | bytes 147464 | tf_op jit(solution)/shard_map/ppermute | solution.py:426
  118.7 4.1 %collective-permute-start.13 = (bf16[48,512]{1,0:T(8,128)(2,1)S(1)}, bf16[48,512]{1,0:T(8,128)(2,1)S(1)}, u32[]{:S(2)}, u32[]{:S(2)}) collective-permute-start(bf16[48,512]{1,0:T(8,128)(2,1)S(1)} %add_convert_fusion.1), channel_id=1, source_target_pairs={{0,4},{2,6},{4,0},{6,2},{8,12},{10,14},{12,8},{14,10},{16,20},{18,... | collective-permute-start | bytes 147464 | tf_op jit(solution)/shard_map/ppermute | solution.py:426
  119.0 5.0 %collective-permute-start.14 = (bf16[48,512]{1,0:T(8,128)(2,1)S(1)}, bf16[48,512]{1,0:T(8,128)(2,1)S(1)}, u32[]{:S(2)}, u32[]{:S(2)}) collective-permute-start(bf16[48,512]{1,0:T(8,128)(2,1)S(1)} %add_convert_fusion.1), channel_id=1, source_target_pairs={{0,6},{2,4},{4,2},{6,0},{8,14},{10,12},{12,10},{14,8},{16,22},{18,... | collective-permute-start | bytes 147464 | tf_op jit(solution)/shard_map/ppermute | solution.py:426
  124.0 1.5 %collective-permute-start.15 = (bf16[48,2048]{1,0:T(8,128)(2,1)S(1)}, bf16[48,2048]{1,0:T(8,128)(2,1)S(1)}, u32[]{:S(2)}, u32[]{:S(2)}) collective-permute-start(bf16[48,2048]{1,0:T(8,128)(2,1)S(1)} %pad_maximum_fusion), channel_id=1, source_target_pairs={{0,1},{1,0},{2,3},{3,2},{4,5},{5,4},{6,7},{7,6},{8,9},{9,8},{10,11... | collective-permute-start | bytes 589832 | tf_op jit(solution)/shard_map/ppermute | solution.py:418
  (7 other events, 13.0 us)

commit v4 on v3

--- a/solution.py
+++ b/solution.py
@@ -18,6 +18,8 @@
 SEGS = 8
 HALF = 256
 GRAD_LANES = 2048
+LAG_FORWARD = 6
+LAG_BACK = 4
 LOG2E = 1.4426950408889634
 EPS = 1e-06
 
@@ -131,9 +133,18 @@
         pltpu.make_async_copy(src, dst, sems.at[i]).wait()
 
 
-def turn_kernel(first_ref, lens_ref, x_ref, gain_ref, turned_ref, normed_ref, raw_ref):
-    shift, _ = row_starts(first_ref, lens_ref, pl.program_id(0))
-    raw_ref[...] = x_ref[...].astype(F32)
+def turn_kernel(first_ref, lens_ref, x_ref, gain_ref, turned_ref, normed_ref, held_ref, raw_ref, sems):
+    r = pl.program_id(0)
+    rows = held_ref.shape[0]
+    copies = [(x_ref.at[i * ROW_LEN : (i + 1) * ROW_LEN], held_ref.at[i]) for i in range(rows)]
+
+    @pl.when(r == 0)
+    def _():
+        start_copies(copies, sems)
+
+    pltpu.make_async_copy(x_ref.at[pl.ds(pl.multiple_of(r * ROW_LEN, ROW_LEN), ROW_LEN)], held_ref.at[r], sems.at[r]).wait()
+    shift, _ = row_starts(first_ref, lens_ref, r)
+    raw_ref[...] = held_ref[r].astype(F32)
     x = turn_rows(raw_ref, shift)
     turned_ref[...] = x.astype(BF)
     normed_ref[...] = (x * lax.rsqrt(jnp.mean(x * x, axis=1, keepdims=True) + EPS) * gain_ref[...].reshape(1, D)).astype(BF)
@@ -235,7 +246,9 @@
 def side_kernel(
     first_ref,
     lens_ref,
+    mid0_ref,
     mid_ref,
+    next_ref,
     w1a_ref,
     w1b_ref,
     w2a_ref,
@@ -274,19 +287,26 @@
     ctxt_ref,
     qkvt_ref,
     dq_ref,
+    turned_ref,
 ):
     r = pl.program_id(0)
     last = pl.num_programs(0) - 1
     units = w1a_ref.shape[1]
 
+    def norm_ahead(ref):
+        middle = ref[...]
+        nb_ref[...] = (middle * lax.rsqrt(jnp.mean(middle * middle, axis=1, keepdims=True) + EPS) * fgain_ref[...].reshape(1, D)).astype(BF)
+
     @pl.when(r == 0)
     def _():
+        norm_ahead(mid0_ref)
         w2_ref[:units] = w2a_ref[...]
         w2_ref[units:] = w2b_ref[...]
         grads_ref[...] = jnp.zeros_like(grads_ref)
         acc_ref[...] = jnp.zeros_like(acc_ref)
         for i, ref in enumerate((alpha_ref, gain1_ref, gain2_ref)):
             cols_ref[i] = jnp.broadcast_to(jnp.broadcast_to(ref[...].reshape(1, DS), (8, DS)).T[:, 0:1], (DS, ROW_LEN))
+        cols_ref[0] = 1.0 / (1.0 + jnp.exp(cols_ref[0] * -10.0))
         wqkvt_ref[:DS] = sq_ref[...].T
         wqkvt_ref[DS : 2 * DS] = sk_ref[...].T
         wqkvt_ref[2 * DS :] = sv_ref[...].T
@@ -295,32 +315,35 @@
     back = (ROW_LEN - shift) & (ROW_LEN - 1)
     fill_bias(bias_ref, docs)
 
-    middle = mid_ref[...]
-    nb_ref[...] = (middle * lax.rsqrt(jnp.mean(middle * middle, axis=1, keepdims=True) + EPS) * fgain_ref[...].reshape(1, D)).astype(BF)
+    turned_ref[0] = pltpu.roll(side_ref[...].astype(F32), back, 1)
+    turned_ref[1] = pltpu.roll(cot_ref[...].astype(F32), back, 1)
+
     for i, w in enumerate((w1a_ref, w1b_ref)):
         for c in range(0, units, 256):
             hid_ref[:, i * units + c : i * units + c + 256] = gelu(dot(nb_ref[...], w[:, c : c + 256])).astype(BF)
 
-    for c in range(0, ROW_LEN, 128):
-        f_ref[c : c + 128] = mid_ref[c : c + 128] + dot(hid_ref[c : c + 128], w2_ref[...])
+    for c in range(0, ROW_LEN, 256):
+        f_ref[c : c + 256] = mid_ref[c : c + 256] + dot(hid_ref[c : c + 256], w2_ref[...])
+    norm_ahead(next_ref)
     bb = f_ref[...].astype(BF)
     bb_out_ref[...] = turn_rows(f_ref, back).astype(BF)
 
-    gain1, gain2 = cols_ref[1], cols_ref[2]
-    mixing = 1.0 / (1.0 + jnp.exp(cols_ref[0] * -10.0))
-    side = pltpu.roll(side_ref[...].astype(F32), back, 1)
-    cot = pltpu.roll(cot_ref[...].astype(F32), back, 1)
-    cotb = cot.astype(BF)
+    mixing, gain1, gain2 = cols_ref[0], cols_ref[1], cols_ref[2]
     lowered = dot(downt_ref[...], bb, 1, 1)
+    activated_grad = dot(shrinkt_ref[...], turned_ref[1].astype(BF), 0, 0)
+    side = turned_ref[0]
     inputs = mixing * lowered + (1.0 - mixing) * side
     scale1 = lax.rsqrt(jnp.mean(inputs * inputs, axis=0, keepdims=True) + EPS)
     fnt = (inputs * scale1 * gain1).astype(BF)
     qkvt_ref[...] = dot(wqkvt_ref[...], fnt).astype(BF)
     k, v = qkvt_ref[DS : 2 * DS].T, qkvt_ref[2 * DS :].T
     blocks = [(half, h) for half in range(2) for h in range(SIDE_HEADS)]
-    sums = [side_scores(half, h, k, qkvt_ref, e_ref, bias_ref, False) for half, h in blocks]
-    for (half, h), total in zip(blocks, sums):
-        side_values(half, h, qkvt_ref, e_ref, ctxt_ref, inv_ref, total)
+    sums = []
+    for n, (half, h) in enumerate(blocks + [(None, None)] * LAG_FORWARD):
+        if n < len(blocks):
+            sums.append(side_scores(half, h, k, qkvt_ref, e_ref, bias_ref, False))
+        if n >= LAG_FORWARD:
+            side_values(*blocks[n - LAG_FORWARD], qkvt_ref, e_ref, ctxt_ref, inv_ref, sums[n - LAG_FORWARD])
 
     @pl.when(out_of_range(sums))
     def _():
@@ -341,12 +364,15 @@
     expanded = dot(expand_ref[...], snt, 0, 0)
     activated, slope = gelu_and_slope(expanded)
     activated = activated.astype(BF)
+    expanded_grad = (activated_grad * slope).astype(BF)
+    second_grad = dot(expand_ref[...], expanded_grad)
+    low = D + 2 * SFF
+    cot = turned_ref[1]
+    cotb = cot.astype(BF)
     side_out = middle_side + dot(shrinkt_ref[...], activated)
     out_ref[...] = pltpu.roll(side_out, shift, 1)
-
-    activated_grad = dot(shrinkt_ref[...], cotb, 0, 0)
-    expanded_grad = (activated_grad * slope).astype(BF)
-    second_grad = dot(expand_ref[...], expanded_grad)
+    grads_ref[:, D : D + SFF] += dot(snt, expanded_grad, 1, 1)
+    grads_ref[:, D + SFF : low] += dot(cotb, activated, 1, 1)
     w2 = second_grad * gain2
     ms = middle_side * scale2
     mean2 = jnp.mean(w2 * middle_side, axis=0, keepdims=True)
@@ -354,6 +380,7 @@
     acc_ref[0] += second_grad * ms
     branch = middle_grad.astype(BF)
     context_grad = dot(proj_ref[...], branch).astype(BF).astype(F32)
+    grads_ref[:, low + 3 * DS : low + 4 * DS] += dot(ctxb, branch, 1, 1)
     dop = (context_grad * inv_ref[...]).astype(BF)
     centre = jnp.sum((dop.astype(F32) * ctx).reshape(SIDE_HEADS, 8, ROW_LEN), axis=1)
     centre = jnp.concatenate([centre, jnp.zeros((4, ROW_LEN), F32)], axis=0)
@@ -362,23 +389,37 @@
     dstack = jnp.concatenate([dop, -chigh, -clow], axis=0)
     vones = jnp.concatenate([v, jnp.ones((ROW_LEN, 32), BF)], axis=1)
     root = SIDE_HEAD_DIM**-0.5
-    for n, (half, h) in enumerate(blocks):
+
+    def score_step(n):
+        half, h = blocks[n]
         rows = slice(half * HALF, (half + 1) * HALF)
         dp = dot(vones[rows] * head_mask(h, 128), dstack[:, rows])
         ds_ref[n] = (e_ref[n].astype(F32) * dp).astype(BF)
         et_ref[n] = e_ref[n].T
-    for n, (half, h) in enumerate(blocks):
+
+    def query_step(n):
+        half, h = blocks[n]
         rows = slice(half * HALF, (half + 1) * HALF)
         dq_ref[own_rows(h), rows] = head_rows(dot(qkvt_ref[pair(DS, h), rows], ds_ref[n]), h) * root
         e_ref[n] = ds_ref[n].T
-    for n, (half, h) in enumerate(blocks):
+
+    def value_step(n):
+        half, h = blocks[n]
         rows = slice(half * HALF, (half + 1) * HALF)
         dq_ref[own_rows(h, 2 * DS), rows] = head_rows(dot(dop[16 * (h // 2) : 16 * (h // 2) + 16, rows], et_ref[n]), h)
-    for n, (half, h) in enumerate(blocks):
+
+    def key_step(n):
+        half, h = blocks[n]
         rows = slice(half * HALF, (half + 1) * HALF)
         dq_ref[own_rows(h, DS), rows] = head_rows(dot(qkvt_ref[pair(0, h), rows], e_ref[n]), h) * root
+
+    for n in range(len(blocks) + 3 * LAG_BACK):
+        for i, step in enumerate((score_step, query_step, value_step, key_step)):
+            if 0 <= n - i * LAG_BACK < len(blocks):
+                step(n - i * LAG_BACK)
     dqkvt = dq_ref[...].astype(BF)
     first_grad = dot(wqkvt_ref[...], dqkvt, 0, 0)
+    grads_ref[:, low : low + 3 * DS] += dot(fnt, dqkvt, 1, 1)
     w1 = first_grad * gain1
     ins = inputs * scale1
     mean1 = jnp.mean(w1 * inputs, axis=0, keepdims=True)
@@ -386,16 +427,11 @@
     acc_ref[1] += first_grad * ins
     acc_ref[2] += input_grad * (lowered - side)
     state_ref[...] = pltpu.roll((1.0 - mixing) * input_grad, shift, 1)
-    low = D + 2 * SFF
     grads_ref[:, 0:D] += dot((mixing * input_grad).astype(BF), bb)
-    grads_ref[:, D : D + SFF] += dot(snt, expanded_grad, 1, 1)
-    grads_ref[:, D + SFF : low] += dot(cotb, activated, 1, 1)
-    grads_ref[:, low : low + 3 * DS] += dot(fnt, dqkvt, 1, 1)
-    grads_ref[:, low + 3 * DS : low + 4 * DS] += dot(ctxb, branch, 1, 1)
 
     @pl.when(r == last)
     def _():
-        gate = 1.0 / (1.0 + jnp.exp(cols_ref[0][:, 0:1] * -10.0))
+        gate = cols_ref[0][:, 0:1]
         total = [jnp.sum(acc_ref[i], axis=1, keepdims=True) for i in range(3)]
         total[2] = total[2] * (gate * (1.0 - gate)) * 10.0
         place = lax.broadcasted_iota(jnp.int32, (DS, 128), 1)
@@ -443,9 +479,26 @@
     if grouped:
         got = [sent] + [trade(sent, m) for m in (1, 2, 3)]
         sent = jnp.concatenate([pick(got, group ^ j) for j in range(4)], axis=1)
-    got = swap(sent)
-    upper = lax.axis_index("tensor") != 0
-    return jnp.concatenate([jnp.where(upper, got, sent), jnp.where(upper, sent, got)], axis=0).astype(F32)
+    return sent, swap(sent)
+
+
+def unpack_kernel(tensor_ref, sent_ref, got_ref, down_ref, alpha_ref, gain1_ref, q_ref, k_ref, v_ref, proj_ref, gain2_ref, expand_ref, shrink_ref):
+    upper = tensor_ref[0] != 0
+
+    def both(first, end):
+        sent, got = sent_ref[:, first:end].astype(F32), got_ref[:, first:end].astype(F32)
+        return jnp.concatenate([jnp.where(upper, got, sent), jnp.where(upper, sent, got)], axis=0)
+
+    low = D + 2 * SFF
+    down_ref[...] = both(0, D)
+    expand_ref[...] = both(D, D + SFF)
+    shrink_ref[...] = both(D + SFF, low)
+    squares = both(low, low + 4 * DS)
+    for i, ref in enumerate((q_ref, k_ref, v_ref, proj_ref)):
+        ref[...] = squares[:, i * DS : (i + 1) * DS]
+    vectors = both(low + 4 * DS, low + 4 * DS + 128).T
+    for i, ref in enumerate((gain2_ref, gain1_ref, alpha_ref)):
+        ref[...] = vectors[i]
 
 
 def make_body(batch):
@@ -495,14 +548,17 @@
 
         own_attn = (attn_query, attn_key, attn_value, attn_out)
         far_attn = [swap(w) for w in own_attn]
+        own_attn = [pltpu.with_memory_space_constraint(w, pltpu.HBM) for w in own_attn]
+        hidden_in = pltpu.with_memory_space_constraint(hidden_in, pltpu.HBM)
+        attn_gain = pltpu.with_memory_space_constraint(attn_gain, pltpu.HBM)
         turned, normed = kernel(
             turn_kernel,
             "turn_rows",
-            9,
-            [tile, whole((D,))],
+            13,
+            [hbm, whole((D,))],
             [tile, tile],
             [jax.ShapeDtypeStruct((tokens, D), BF)] * 2,
-            [pltpu.VMEM((ROW_LEN, D), F32)],
+            [pltpu.VMEM((rows, ROW_LEN, D), BF), pltpu.VMEM((ROW_LEN, D), F32), pltpu.SemaphoreType.DMA((rows,))],
         )(first, lens, hidden_in, attn_gain)
         far_attn, turned, normed, ffn_in, ffn_out = lax.optimization_barrier((far_attn, turned, normed, ffn_in, ffn_out))
         far_ffn = [swap(w) for w in (ffn_in, ffn_out)]
@@ -530,8 +586,8 @@
         backbone, side_out, state_grad, mine, other = kernel(
             side_kernel,
             "forward_and_back",
-            30,
-            [tile]
+            32,
+            [whole((ROW_LEN, D)), tile, pl.BlockSpec((ROW_LEN, D), lambda r, *_: (jnp.minimum(r + 1, rows - 1), 0))]
             + [whole((D, units))] * 2
             + [whole((units, D))] * 2
             + [whole((D,)), side_tile, side_tile]
@@ -564,10 +620,13 @@
                 side,
                 pltpu.VMEM((3 * DS, ROW_LEN), BF),
                 pltpu.VMEM((3 * DS, ROW_LEN), F32),
+                pltpu.VMEM((2, DS, ROW_LEN), F32),
             ],
         )(
             first,
             lens,
+            mid,
+            mid,
             mid,
             ffn_in,
             far_ffn[0],
@@ -587,23 +646,21 @@
             side_expand,
             side_shrink.T,
         )
-        g = sum_over(mine, other, batch)
-        low = D + 2 * SFF
-        return (
-            backbone,
-            side_out.T,
-            state_grad.T,
-            g[:, :D].T,
-            g[:, low + 4 * DS + 2],
-            g[:, low + 4 * DS + 1],
-            g[:, low : low + DS],
-            g[:, low + DS : low + 2 * DS],
-            g[:, low + 2 * DS : low + 3 * DS],
-            g[:, low + 3 * DS : low + 4 * DS],
-            g[:, low + 4 * DS],
-            g[:, D : D + SFF],
-            g[:, D + SFF : low].T,
-        )
+        square_out = jax.ShapeDtypeStruct((DS, DS), F32)
+        vector_out = jax.ShapeDtypeStruct((DS,), F32)
+        wide_out = jax.ShapeDtypeStruct((DS, SFF), F32)
+        vmem = pl.BlockSpec(memory_space=pltpu.VMEM)
+        down, alpha, gain1, query, key, value, proj, gain2, expand, shrink = pl.pallas_call(
+            unpack_kernel,
+            in_specs=[pl.BlockSpec(memory_space=pltpu.SMEM), vmem, vmem],
+            out_specs=[vmem] * 10,
+            out_shape=[jax.ShapeDtypeStruct((DS, D), F32), vector_out, vector_out]
+            + [square_out] * 4
+            + [vector_out, wide_out, wide_out],
+            compiler_params=pltpu.CompilerParams(vmem_limit_bytes=6 * 1024 * 1024),
+            name="unpack",
+        )(first, *sum_over(mine, other, batch))
+        return backbone, side_out.T, state_grad.T, down.T, alpha, gain1, query, key, value, proj, gain2, expand, shrink.T
 
     return body
 

time: 129 us -> 121 us (0.938)
  local copies, waits for them, and re-layouts: 6.55 us -> 0.78 us
  other arithmetic: 2.5 us -> 0.2 us
    unnamed x46 -> x34, local copies, waits for them, and re-layouts: 5.82 us -> 0.78 us
    slice x2 -> x0, other arithmetic: 1.44 us -> none  [the longest x1 0.73 us: body(): g[:, low + 3 * DS:low + 4 * DS]]
    pallas_call x1, Pallas kernels: 22.8 us -> 24.2 us  [body(): kernel(attention_kernel, 'attention', 22, [tile, tile] + [hbm] * 8, tile,...]
    pallas_call x2 -> x3, Pallas kernels: 66.4 us -> 65.5 us  [the longest x1 59.4 us: body(): kernel(side_kernel, 'forward_and_back', 32, [whole((ROW_LEN, D)), tile, p...]
  transfers between devices with their start and end apart: 16 -> 16, of which waited for: 10 -> 10; matrix products, arithmetic and copies ran while one was open for 0% -> 0% of each run, Pallas kernels for 20% -> 24%
where the time goes in v4:
time: 121 us
  Pallas kernels  89.7 us (74%)
  starting transfers between devices  14.8 us (12%)
  waiting for transfers between devices  14.5 us (12%)
    pallas_call x1, Pallas kernels, body(): kernel(side_kernel, 'forward_and_back', 32, [whole((ROW_LEN, D)), tile, p...  59.4 us
    pallas_call x1, Pallas kernels, body(): kernel(attention_kernel, 'attention', 22, [tile, tile] + [hbm] * 8, tile,...  24.2 us
    ppermute x8, starting transfers between devices, trade(): return lax.ppermute(x, 'batch', [(i, i ^ bits) for i in range(batch)])  12.6 us
    ppermute x8, waiting for transfers between devices, trade(): return lax.ppermute(x, 'batch', [(i, i ^ bits) for i in range(batch)])  11.9 us
    pallas_call x1, Pallas kernels, body(): kernel(turn_kernel, 'turn_rows', 13, [hbm, whole((D,))], [tile, tile], [j...  5.13 us
    ppermute x8, waiting for transfers between devices, swap(): return lax.ppermute(x, 'tensor', [(0, 1), (1, 0)])  2.51 us
  transfers between devices with their start and end apart: 16, of which 10 were waited for; matrix products, arithmetic and copies ran while one was open for 0% of the time, Pallas kernels for 24%

profile of v4, /device:TPU:0, one launch (start us, length us, event | category | flops | bytes accessed | tf_op | source)
XLA Modules:
  0.0 121.0 jit_solution(7767339400201892441)
XLA Ops:
  0.7 0.5 collective-permute-start
  1.2 0.1 collective-permute-start.1
  1.3 0.4 collective-permute-start.2
  1.7 0.1 collective-permute-start.3
  1.8 0.7 copy-done.7
  2.5 5.1 %turn_rows.1 = (bf16[2560,768]{1,0:T(8,128)(2,1)S(1)}, bf16[2560,768]{1,0:T(8,128)(2,1)S(1)}) custom-call(s32[1]{0:T(128)} %bitcast.first_ref.tensor_ref, s32[8,10]{1,0:T(8,128)S(1)} %bitcast.14, bf16[2560,768]{1,0:T(8,128)(2,1)} %x_ref.1, f32[768]{0:T(1024)} %gain_ref.1), custom_call_target="tpu_custom_call" | custom-call | tf_op jit(solution)/shard_map/turn_rows/pallas_call | solution.py:554
  7.6 0.0 copy-start.1
  7.8 0.5 collective-permute-start.4
  8.3 0.1 collective-permute-start.5
  8.4 24.2 %attention.1.mid0_ref.mid_ref.next_ref = f32[2560,768]{1,0:T(8,128)S(1)} custom-call(s32[1]{0:T(128)} %bitcast.first_ref.tensor_ref, s32[8,10]{1,0:T(8,128)S(1)} %bitcast.15, bf16[2560,768]{1,0:T(8,128)(2,1)S(1)} %get-tuple-element.40.turned_ref, bf16[2560,768]{1,0:T(8,128)(2,1)S(1)} %get-tuple-element.41.normed_ref, bf16[768,384]{1,0:T(8,128)(2,1)} %wqa_ref.1, ...), custom_call_target="tpu_custom_call" | custom-call | tf_op jit(solution)/shard_map/attention/pallas_call | solution.py:565
  32.8 59.4 %forward_and_back.1 = (bf16[2560,768]{1,0:T(8,128)(2,1)}, f32[96,2560]{1,0:T(8,128)}, f32[96,2560]{1,0:T(8,128)}, bf16[48,2048]{1,0:T(8,128)(2,1)S(1)}, bf16[48,2048]{1,0:T(8,128)(2,1)S(1)}) custom-call(s32[1]{0:T(128)} %bitcast.first_ref.tensor_ref, s32[8,10]{1,0:T(8,128)S(1)} %bitcast.16, f32[2560,768]{1,0:T(8,128)S(1)} %attention.1.mid0_ref.mid_ref.next_ref, ...), custom_call_target="tpu_custom_call" | custom-call | tf_op jit(solution)/shard_map/forward_and_back/pallas_call | solution.py:586
  92.2 0.4 collective-permute-start.6
  92.6 1.1 collective-permute-done.6
  93.8 2.9 %collective-permute-start.7 = (bf16[48,512]{1,0:T(8,128)(2,1)S(1)}, bf16[48,512]{1,0:T(8,128)(2,1)S(1)}, u32[]{:S(2)}, u32[]{:S(2)}) collective-permute-start(bf16[48,512]{1,0:T(8,128)(2,1)S(1)} %get-tuple-element.67), channel_id=1, source_target_pairs={{0,2},{2,0},{4,6},{6,4},{8,10},{10,8},{12,14},{14,12},{16,18},{18,... | collective-permute-start | bytes 147464 | tf_op jit(solution)/shard_map/ppermute | solution.py:462
  96.7 1.5 %collective-permute-start.8 = (bf16[48,512]{1,0:T(8,128)(2,1)S(1)}, bf16[48,512]{1,0:T(8,128)(2,1)S(1)}, u32[]{:S(2)}, u32[]{:S(2)}) collective-permute-start(bf16[48,512]{1,0:T(8,128)(2,1)S(1)} %get-tuple-element.68), channel_id=1, source_target_pairs={{0,4},{2,6},{4,0},{6,2},{8,12},{10,14},{12,8},{14,10},{16,20},{18,... | collective-permute-start | bytes 147464 | tf_op jit(solution)/shard_map/ppermute | solution.py:462
  98.2 0.1 collective-permute-start.9
  98.3 0.4 collective-permute-done.7
  98.8 2.0 %collective-permute-done.8 = bf16[48,512]{1,0:T(8,128)(2,1)S(1)} collective-permute-done((bf16[48,512]{1,0:T(8,128)(2,1)S(1)}, bf16[48,512]{1,0:T(8,128)(2,1)S(1)}, u32[]{:S(2)}, u32[]{:S(2)}) %collective-permute-start.8) | collective-permute-done | bytes 49184 | tf_op jit(solution)/shard_map/ppermute | solution.py:462
  100.8 2.5 %collective-permute-done.9 = bf16[48,512]{1,0:T(8,128)(2,1)S(1)} collective-permute-done((bf16[48,512]{1,0:T(8,128)(2,1)S(1)}, bf16[48,512]{1,0:T(8,128)(2,1)S(1)}, u32[]{:S(2)}, u32[]{:S(2)}) %collective-permute-start.9) | collective-permute-done | bytes 49184 | tf_op jit(solution)/shard_map/ppermute | solution.py:462
  103.3 1.6 %collective-permute-start.10 = (bf16[48,512]{1,0:T(8,128)(2,1)S(1)}, bf16[48,512]{1,0:T(8,128)(2,1)S(1)}, u32[]{:S(2)}, u32[]{:S(2)}) collective-permute-start(bf16[48,512]{1,0:T(8,128)(2,1)S(1)} %add_convert_fusion.3), channel_id=1, source_target_pairs={{0,8},{2,10},{4,12},{6,14},{8,0},{10,2},{12,4},{14,6},{16,24},{18,... | collective-permute-start | bytes 147464 | tf_op jit(solution)/shard_map/ppermute | solution.py:462
  105.0 2.5 %collective-permute-done.10 = bf16[48,512]{1,0:T(8,128)(2,1)S(1)} collective-permute-done((bf16[48,512]{1,0:T(8,128)(2,1)S(1)}, bf16[48,512]{1,0:T(8,128)(2,1)S(1)}, u32[]{:S(2)}, u32[]{:S(2)}) %collective-permute-start.10) | collective-permute-done | bytes 49184 | tf_op jit(solution)/shard_map/ppermute | solution.py:462
  107.5 2.9 %collective-permute-start.11 = (bf16[48,512]{1,0:T(8,128)(2,1)S(1)}, bf16[48,512]{1,0:T(8,128)(2,1)S(1)}, u32[]{:S(2)}, u32[]{:S(2)}) collective-permute-start(bf16[48,512]{1,0:T(8,128)(2,1)S(1)} %add_convert_fusion.2), channel_id=1, source_target_pairs={{0,16},{2,18},{4,20},{6,22},{8,24},{10,26},{12,28},{14,30},{16,0},... | collective-permute-start | bytes 147464 | tf_op jit(solution)/shard_map/ppermute | solution.py:462
  110.4 2.1 %collective-permute-done.11 = bf16[48,512]{1,0:T(8,128)(2,1)S(1)} collective-permute-done((bf16[48,512]{1,0:T(8,128)(2,1)S(1)}, bf16[48,512]{1,0:T(8,128)(2,1)S(1)}, u32[]{:S(2)}, u32[]{:S(2)}) %collective-permute-start.11) | collective-permute-done | bytes 49184 | tf_op jit(solution)/shard_map/ppermute | solution.py:462
  112.6 0.6 collective-permute-start.12
  113.2 0.3 collective-permute-start.13
  113.5 2.7 %collective-permute-start.14 = (bf16[48,512]{1,0:T(8,128)(2,1)S(1)}, bf16[48,512]{1,0:T(8,128)(2,1)S(1)}, u32[]{:S(2)}, u32[]{:S(2)}) collective-permute-start(bf16[48,512]{1,0:T(8,128)(2,1)S(1)} %add_convert_fusion.1), channel_id=1, source_target_pairs={{0,6},{2,4},{4,2},{6,0},{8,14},{10,12},{12,10},{14,8},{16,22},{18,... | collective-permute-start | bytes 147464 | tf_op jit(solution)/shard_map/ppermute | solution.py:462
  116.1 0.6 collective-permute-done.12
  116.7 0.5 collective-permute-done.13
  117.3 1.2 collective-permute-done.14
  118.5 0.1 collective-permute-start.15
  118.6 1.4 %collective-permute-done.15.got_ref = bf16[48,2048]{1,0:T(8,128)(2,1)S(1)} collective-permute-done((bf16[48,2048]{1,0:T(8,128)(2,1)S(1)}, bf16[48,2048]{1,0:T(8,128)(2,1)S(1)}, u32[]{:S(2)}, u32[]{:S(2)}) %collective-permute-start.15) | collective-permute-done | bytes 196640 | tf_op jit(solution)/shard_map/ppermute | solution.py:454
  120.0 0.9 unpack.1
  (46 shorter events, 0.3 us)
Async XLA Ops:
  0.6 7.0 %copy-start = (bf16[768,1536]{1,0:T(8,128)(2,1)S(1)}, bf16[768,1536]{1,0:T(8,128)(2,1)}, u32[]{:S(2)}) copy-start(bf16[768,1536]{1,0:T(8,128)(2,1)} %w1a_ref) | copy-start | bytes 7077892
  0.7 6.9 %collective-permute-start = (bf16[768,384]{1,0:T(8,128)(2,1)}, bf16[768,384]{1,0:T(8,128)(2,1)S(1)}, u32[]{:S(2)}, u32[]{:S(2)}) collective-permute-start(bf16[768,384]{1,0:T(8,128)(2,1)} %wqa_ref.1), channel_id=1, source_target_pairs={{0,1},{1,0},{2,3},{3,2},{4,5},{5,4},{6,7},{7,6},{8,9},{9,8},{10,11... | collective-permute-start | bytes 1769480 | tf_op jit(solution)/shard_map/ppermute | solution.py:454
  1.2 6.4 %collective-permute-start.1 = (bf16[768,384]{1,0:T(8,128)(2,1)}, bf16[768,384]{1,0:T(8,128)(2,1)S(1)}, u32[]{:S(2)}, u32[]{:S(2)}) collective-permute-start(bf16[768,384]{1,0:T(8,128)(2,1)} %wka_ref.1), channel_id=1, source_target_pairs={{0,1},{1,0},{2,3},{3,2},{4,5},{5,4},{6,7},{7,6},{8,9},{9,8},{10,11... | collective-permute-start | bytes 1769480 | tf_op jit(solution)/shard_map/ppermute | solution.py:454
  1.3 6.4 %collective-permute-start.2 = (bf16[768,384]{1,0:T(8,128)(2,1)}, bf16[768,384]{1,0:T(8,128)(2,1)}, u32[]{:S(2)}, u32[]{:S(2)}) collective-permute-start(bf16[768,384]{1,0:T(8,128)(2,1)} %wva_ref.1), channel_id=1, source_target_pairs={{0,1},{1,0},{2,3},{3,2},{4,5},{5,4},{6,7},{7,6},{8,9},{9,8},{10,11... | collective-permute-start | bytes 1769480 | tf_op jit(solution)/shard_map/ppermute | solution.py:454
  1.7 5.9 %collective-permute-start.3 = (bf16[384,768]{1,0:T(8,128)(2,1)}, bf16[384,768]{1,0:T(8,128)(2,1)}, u32[]{:S(2)}, u32[]{:S(2)}) collective-permute-start(bf16[384,768]{1,0:T(8,128)(2,1)} %woa_ref.1), channel_id=1, source_target_pairs={{0,1},{1,0},{2,3},{3,2},{4,5},{5,4},{6,7},{7,6},{8,9},{9,8},{10,11... | collective-permute-start | bytes 1769480 | tf_op jit(solution)/shard_map/ppermute | solution.py:454
  2.5 5.9 %copy-start.8 = (s32[10,8]{0,1:T(8,128)S(1)}, s32[10,8]{0,1:T(8,128)}, u32[]{:S(2)}) copy-start(s32[10,8]{0,1:T(8,128)} %param.23) | copy-start | bytes 964
  7.6 25.0 %copy-start.1 = (bf16[1536,768]{1,0:T(8,128)(2,1)S(1)}, bf16[1536,768]{1,0:T(8,128)(2,1)}, u32[]{:S(2)}) copy-start(bf16[1536,768]{1,0:T(8,128)(2,1)} %w2a_ref) | copy-start | bytes 7077892
  7.7 25.0 %copy-start.2 = (bf16[2560,96]{0,1:T(8,128)(2,1)S(1)}, bf16[2560,96]{0,1:T(8,128)(2,1)}, u32[]{:S(2)}) copy-start(bf16[2560,96]{0,1:T(8,128)(2,1)} %param.32) | copy-start | bytes 1474564
  7.7 25.0 %copy-start.3 = (bf16[2560,96]{0,1:T(8,128)(2,1)S(1)}, bf16[2560,96]{0,1:T(8,128)(2,1)}, u32[]{:S(2)}) copy-start(bf16[2560,96]{0,1:T(8,128)(2,1)} %param.43) | copy-start | bytes 1474564
  7.7 25.0 %copy-start.4 = (bf16[768,96]{0,1:T(8,128)(2,1)S(1)}, bf16[768,96]{0,1:T(8,128)(2,1)}, u32[]{:S(2)}) copy-start(bf16[768,96]{0,1:T(8,128)(2,1)} %param.34) | copy-start | bytes 442372
  7.7 25.0 %copy-start.5 = (bf16[96,384]{1,0:T(8,128)(2,1)S(1)}, bf16[96,384]{1,0:T(8,128)(2,1)}, u32[]{:S(2)}) copy-start(bf16[96,384]{1,0:T(8,128)(2,1)} %expand_ref.1) | copy-start | bytes 221188
  7.7 25.0 %copy-start.6 = (bf16[384,96]{0,1:T(8,128)(2,1)S(1)}, bf16[384,96]{0,1:T(8,128)(2,1)}, u32[]{:S(2)}) copy-start(bf16[384,96]{0,1:T(8,128)(2,1)} %param.42) | copy-start | bytes 221188
  7.7 25.0 %copy-start.9 = (bf16[96,96]{1,0:T(8,128)(2,1)S(1)}, bf16[96,96]{1,0:T(8,128)(2,1)}, u32[]{:S(2)}) copy-start(bf16[96,96]{1,0:T(8,128)(2,1)} %sq_ref.1) | copy-start | bytes 55300
  7.7 25.0 %copy-start.10 = (bf16[96,96]{1,0:T(8,128)(2,1)S(1)}, bf16[96,96]{1,0:T(8,128)(2,1)}, u32[]{:S(2)}) copy-start(bf16[96,96]{1,0:T(8,128)(2,1)} %sk_ref.1) | copy-start | bytes 55300
  7.7 25.0 %copy-start.11 = (bf16[96,96]{1,0:T(8,128)(2,1)S(1)}, bf16[96,96]{1,0:T(8,128)(2,1)}, u32[]{:S(2)}) copy-start(bf16[96,96]{1,0:T(8,128)(2,1)} %sv_ref.1) | copy-start | bytes 55300
  7.8 25.0 %copy-start.12 = (bf16[96,96]{1,0:T(8,128)(2,1)S(1)}, bf16[96,96]{1,0:T(8,128)(2,1)}, u32[]{:S(2)}) copy-start(bf16[96,96]{1,0:T(8,128)(2,1)} %proj_ref.1) | copy-start | bytes 55300
  7.8 25.0 %copy-start.13 = (f32[768]{0:T(1024)S(1)}, f32[768]{0:T(1024)}, u32[]{:S(2)}) copy-start(f32[768]{0:T(1024)} %fgain_ref.1) | copy-start | bytes 9220
  7.8 25.0 %copy-start.14 = (f32[96]{0:T(128)S(1)}, f32[96]{0:T(128)}, u32[]{:S(2)}) copy-start(f32[96]{0:T(128)} %alpha_ref.1) | copy-start | bytes 1156
  7.8 25.0 %copy-start.15 = (f32[96]{0:T(128)S(1)}, f32[96]{0:T(128)}, u32[]{:S(2)}) copy-start(f32[96]{0:T(128)} %gain1_ref.1) | copy-start | bytes 1156
  7.8 25.0 %copy-start.16 = (f32[96]{0:T(128)S(1)}, f32[96]{0:T(128)}, u32[]{:S(2)}) copy-start(f32[96]{0:T(128)} %gain2_ref.1) | copy-start | bytes 1156
  7.8 24.8 %collective-permute-start.4 = (bf16[768,1536]{1,0:T(8,128)(2,1)S(1)}, bf16[768,1536]{1,0:T(8,128)(2,1)S(1)}, u32[]{:S(2)}, u32[]{:S(2)}) collective-permute-start(bf16[768,1536]{1,0:T(8,128)(2,1)S(1)} %copy-done), channel_id=1, source_target_pairs={{0,1},{1,0},{2,3},{3,2},{4,5},{5,4},{6,7},{7,6},{8,9},{9,8},{10,11... | collective-permute-start | bytes 7077896 | tf_op jit(solution)/shard_map/ppermute | solution.py:454
  8.3 24.3 %collective-permute-start.5 = (bf16[1536,768]{1,0:T(8,128)(2,1)}, bf16[1536,768]{1,0:T(8,128)(2,1)S(1)}, u32[]{:S(2)}, u32[]{:S(2)}) collective-permute-start(bf16[1536,768]{1,0:T(8,128)(2,1)} %w2a_ref), channel_id=1, source_target_pairs={{0,1},{1,0},{2,3},{3,2},{4,5},{5,4},{6,7},{7,6},{8,9},{9,8},{10,11... | collective-permute-start | bytes 7077896 | tf_op jit(solution)/shard_map/ppermute | solution.py:454
  92.2 1.5 %collective-permute-start.6 = (bf16[48,2048]{1,0:T(8,128)(2,1)S(1)}, bf16[48,2048]{1,0:T(8,128)(2,1)S(1)}, u32[]{:S(2)}, u32[]{:S(2)}) collective-permute-start(bf16[48,2048]{1,0:T(8,128)(2,1)S(1)} %get-tuple-element.52), channel_id=1, source_target_pairs={{0,1},{1,0},{2,3},{3,2},{4,5},{5,4},{6,7},{7,6},{8,9},{9,8},{10,11... | collective-permute-start | bytes 589832 | tf_op jit(solution)/shard_map/ppermute | solution.py:454
  93.8 5.0 %collective-permute-start.7 = (bf16[48,512]{1,0:T(8,128)(2,1)S(1)}, bf16[48,512]{1,0:T(8,128)(2,1)S(1)}, u32[]{:S(2)}, u32[]{:S(2)}) collective-permute-start(bf16[48,512]{1,0:T(8,128)(2,1)S(1)} %get-tuple-element.67), channel_id=1, source_target_pairs={{0,2},{2,0},{4,6},{6,4},{8,10},{10,8},{12,14},{14,12},{16,18},{18,... | collective-permute-start | bytes 147464 | tf_op jit(solution)/shard_map/ppermute | solution.py:462
  96.7 4.1 %collective-permute-start.8 = (bf16[48,512]{1,0:T(8,128)(2,1)S(1)}, bf16[48,512]{1,0:T(8,128)(2,1)S(1)}, u32[]{:S(2)}, u32[]{:S(2)}) collective-permute-start(bf16[48,512]{1,0:T(8,128)(2,1)S(1)} %get-tuple-element.68), channel_id=1, source_target_pairs={{0,4},{2,6},{4,0},{6,2},{8,12},{10,14},{12,8},{14,10},{16,20},{18,... | collective-permute-start | bytes 147464 | tf_op jit(solution)/shard_map/ppermute | solution.py:462
  98.2 5.1 %collective-permute-start.9 = (bf16[48,512]{1,0:T(8,128)(2,1)S(1)}, bf16[48,512]{1,0:T(8,128)(2,1)S(1)}, u32[]{:S(2)}, u32[]{:S(2)}) collective-permute-start(bf16[48,512]{1,0:T(8,128)(2,1)S(1)} %select_select_fusion.4), channel_id=1, source_target_pairs={{0,6},{2,4},{4,2},{6,0},{8,14},{10,12},{12,10},{14,8},{16,22},{18,... | collective-permute-start | bytes 147464 | tf_op jit(solution)/shard_map/ppermute | solution.py:462
  103.3 4.2 %collective-permute-start.10 = (bf16[48,512]{1,0:T(8,128)(2,1)S(1)}, bf16[48,512]{1,0:T(8,128)(2,1)S(1)}, u32[]{:S(2)}, u32[]{:S(2)}) collective-permute-start(bf16[48,512]{1,0:T(8,128)(2,1)S(1)} %add_convert_fusion.3), channel_id=1, source_target_pairs={{0,8},{2,10},{4,12},{6,14},{8,0},{10,2},{12,4},{14,6},{16,24},{18,... | collective-permute-start | bytes 147464 | tf_op jit(solution)/shard_map/ppermute | solution.py:462
  107.5 5.1 %collective-permute-start.11 = (bf16[48,512]{1,0:T(8,128)(2,1)S(1)}, bf16[48,512]{1,0:T(8,128)(2,1)S(1)}, u32[]{:S(2)}, u32[]{:S(2)}) collective-permute-start(bf16[48,512]{1,0:T(8,128)(2,1)S(1)} %add_convert_fusion.2), channel_id=1, source_target_pairs={{0,16},{2,18},{4,20},{6,22},{8,24},{10,26},{12,28},{14,30},{16,0},... | collective-permute-start | bytes 147464 | tf_op jit(solution)/shard_map/ppermute | solution.py:462
  112.6 4.2 %collective-permute-start.12 = (bf16[48,512]{1,0:T(8,128)(2,1)S(1)}, bf16[48,512]{1,0:T(8,128)(2,1)S(1)}, u32[]{:S(2)}, u32[]{:S(2)}) collective-permute-start(bf16[48,512]{1,0:T(8,128)(2,1)S(1)} %add_convert_fusion.1), channel_id=1, source_target_pairs={{0,2},{2,0},{4,6},{6,4},{8,10},{10,8},{12,14},{14,12},{16,18},{18,... | collective-permute-start | bytes 147464 | tf_op jit(solution)/shard_map/ppermute | solution.py:462
  113.2 4.1 %collective-permute-start.13 = (bf16[48,512]{1,0:T(8,128)(2,1)S(1)}, bf16[48,512]{1,0:T(8,128)(2,1)S(1)}, u32[]{:S(2)}, u32[]{:S(2)}) collective-permute-start(bf16[48,512]{1,0:T(8,128)(2,1)S(1)} %add_convert_fusion.1), channel_id=1, source_target_pairs={{0,4},{2,6},{4,0},{6,2},{8,12},{10,14},{12,8},{14,10},{16,20},{18,... | collective-permute-start | bytes 147464 | tf_op jit(solution)/shard_map/ppermute | solution.py:462
  113.5 5.0 %collective-permute-start.14 = (bf16[48,512]{1,0:T(8,128)(2,1)S(1)}, bf16[48,512]{1,0:T(8,128)(2,1)S(1)}, u32[]{:S(2)}, u32[]{:S(2)}) collective-permute-start(bf16[48,512]{1,0:T(8,128)(2,1)S(1)} %add_convert_fusion.1), channel_id=1, source_target_pairs={{0,6},{2,4},{4,2},{6,0},{8,14},{10,12},{12,10},{14,8},{16,22},{18,... | collective-permute-start | bytes 147464 | tf_op jit(solution)/shard_map/ppermute | solution.py:462
  118.5 1.5 %collective-permute-start.15 = (bf16[48,2048]{1,0:T(8,128)(2,1)S(1)}, bf16[48,2048]{1,0:T(8,128)(2,1)S(1)}, u32[]{:S(2)}, u32[]{:S(2)}) collective-permute-start(bf16[48,2048]{1,0:T(8,128)(2,1)S(1)} %pad_maximum_fusion.sent_ref), channel_id=1, source_target_pairs={{0,1},{1,0},{2,3},{3,2},{4,5},{5,4},{6,7},{7,6},{8,9},{9,8},{10,11... | collective-permute-start | bytes 589832 | tf_op jit(solution)/shard_map/ppermute | solution.py:454
  (1 other events, 0.7 us)

commit v5 on v4

--- a/solution.py
+++ b/solution.py
@@ -88,8 +88,7 @@
         s = s + bias_ref[...]
     if safe:
         s = s - jnp.max(s, axis=0, keepdims=True)
-    e = jnp.exp2(s)
-    return e.astype(BF), jnp.sum(e, axis=0, keepdims=True)
+    return jnp.exp2(s)
 
 
 def out_of_range(sums):
@@ -111,9 +110,10 @@
     rows = slice(half * HALF, (half + 1) * HALF)
     q2 = qkv_ref[rows, at(p * 128, 128, 128)]
     k2 = qkv_ref[rows, at(D + p * 128, 128, 128)]
-    s = dot(k2 * keep.astype(F32).astype(BF), q2, 1, 1) * (LOG2E / 8.0)
-    e_ref[half * HEADS + h], total = exponentials(s, half, bias_ref, safe)
-    return total
+    s = dot(k2 * keep.astype(F32).astype(BF), q2, 1, 1)
+    e = exponentials(s, half, bias_ref, safe)
+    e_ref[half * HEADS + h] = e.astype(BF)
+    return jnp.sum(e, axis=0, keepdims=True)
 
 
 def frozen_values(half, h, vt_ref, e_ref, ctxt_ref, total):
@@ -133,59 +133,67 @@
         pltpu.make_async_copy(src, dst, sems.at[i]).wait()
 
 
-def turn_kernel(first_ref, lens_ref, x_ref, gain_ref, turned_ref, normed_ref, held_ref, raw_ref, sems):
+def turn_kernel(first_ref, lens_ref, x_ref, wq_ref, wk_ref, wv_ref, turned_ref, joined_ref, held_ref, raw_ref, sems, joined_sems):
     r = pl.program_id(0)
     rows = held_ref.shape[0]
     copies = [(x_ref.at[i * ROW_LEN : (i + 1) * ROW_LEN], held_ref.at[i]) for i in range(rows)]
+    joins = [(w, joined_ref.at[i]) for i, w in enumerate((wq_ref, wk_ref, wv_ref))]
 
     @pl.when(r == 0)
     def _():
         start_copies(copies, sems)
+        start_copies(joins, joined_sems)
 
     pltpu.make_async_copy(x_ref.at[pl.ds(pl.multiple_of(r * ROW_LEN, ROW_LEN), ROW_LEN)], held_ref.at[r], sems.at[r]).wait()
     shift, _ = row_starts(first_ref, lens_ref, r)
     raw_ref[...] = held_ref[r].astype(F32)
-    x = turn_rows(raw_ref, shift)
-    turned_ref[...] = x.astype(BF)
-    normed_ref[...] = (x * lax.rsqrt(jnp.mean(x * x, axis=1, keepdims=True) + EPS) * gain_ref[...].reshape(1, D)).astype(BF)
+    turned_ref[...] = turn_rows(raw_ref, shift).astype(BF)
+
+    @pl.when(r == rows - 1)
+    def _():
+        wait_copies(joins, joined_sems, 0, 3)
 
 
 def attention_kernel(
     first_ref,
     lens_ref,
+    turned0_ref,
     turned_ref,
-    normed_ref,
-    wqa_ref,
-    wqb_ref,
-    wka_ref,
-    wkb_ref,
-    wva_ref,
-    wvb_ref,
-    woa_ref,
-    wob_ref,
-    mid_ref,
+    gain_ref,
+    joined_ref,
+    wq_ref,
+    wk_ref,
+    wv_ref,
+    ctxt_ref,
     wqkv_ref,
-    wo_ref,
     qkv_ref,
     vt_ref,
     e_ref,
-    ctxt_ref,
     bias_ref,
+    nb_ref,
     sems,
 ):
     r = pl.program_id(0)
-    cols = woa_ref.shape[0]
-    copies = [(w, wqkv_ref.at[:, i * cols : (i + 1) * cols]) for i, w in enumerate((wqa_ref, wqb_ref, wka_ref, wkb_ref, wva_ref, wvb_ref))]
-    copies += [(woa_ref, wo_ref.at[:cols]), (wob_ref, wo_ref.at[cols:])]
+    cols = wq_ref.shape[1]
+    copies = []
+    for i, far in enumerate((wq_ref, wk_ref, wv_ref)):
+        copies += [(joined_ref.at[i], wqkv_ref.at[:, i * D : i * D + cols]), (far, wqkv_ref.at[:, i * D + cols : (i + 1) * D])]
+
+    def norm_ahead(ref):
+        x = ref[...].astype(F32)
+        nb_ref[...] = (x * lax.rsqrt(jnp.mean(x * x, axis=1, keepdims=True) + EPS) * gain_ref[...].reshape(1, D)).astype(BF)
 
     @pl.when(r == 0)
     def _():
         start_copies(copies, sems)
-        wait_copies(copies, sems, 0, 8)
+        norm_ahead(turned0_ref)
+        wait_copies(copies, sems, 0, 6)
 
     _, docs = row_starts(first_ref, lens_ref, r)
     fill_bias(bias_ref, docs)
-    qkv_ref[...] = dot(normed_ref[...], wqkv_ref[...]).astype(BF)
+    qkv_ref[:, :D] = (dot(nb_ref[...], wqkv_ref[:, :D]) * (LOG2E * HEAD_DIM**-0.5)).astype(BF)
+    qkv_ref[:, D:] = dot(nb_ref[...], wqkv_ref[:, D:]).astype(BF)
+    norm_ahead(turned_ref)
     vt_ref[...] = qkv_ref[:, 2 * D :].T
     blocks = [(half, h) for half in range(2) for h in range(HEADS)]
     sums = [frozen_scores(half, h, qkv_ref, e_ref, bias_ref, False) for half, h in blocks]
@@ -201,8 +209,6 @@
                 return carry
 
             lax.fori_loop(0, HEADS, again, 0)
-
-    mid_ref[...] = turned_ref[...].astype(F32) + dot(ctxt_ref[...].T, wo_ref[...])
 
 
 def head_mask(h, width):
@@ -230,25 +236,29 @@
 
 def side_scores(half, h, k, qkvt_ref, e_ref, bias_ref, safe):
     rows = slice(half * HALF, (half + 1) * HALF)
-    s = dot(k[rows] * head_mask(h, DS), qkvt_ref[:DS, rows]) * (LOG2E * SIDE_HEAD_DIM**-0.5)
-    e_ref[half * SIDE_HEADS + h], total = exponentials(s, half, bias_ref, safe)
+    s = dot(k[rows] * head_mask(h, DS), qkvt_ref[:DS, rows])
+    e_ref[half * SIDE_HEADS + h] = exponentials(s, half, bias_ref, safe).astype(BF)
+
+
+def side_values(half, h, vt_ref, e_ref, ctxt_ref, inv_ref):
+    rows = slice(half * HALF, (half + 1) * HALF)
+    mixed = dot(vt_ref[at(16 * h, 16, 16), rows], e_ref[half * SIDE_HEADS + h])
+    total = mixed[8:9]
+    inv = 1.0 / total
+    ctxt_ref[own_rows(h), rows] = mixed[:8] * inv
+    inv_ref[own_rows(h), rows] = jnp.broadcast_to(inv, (SIDE_HEAD_DIM, HALF))
     return total
-
-
-def side_values(half, h, qkvt_ref, e_ref, ctxt_ref, inv_ref, total):
-    rows = slice(half * HALF, (half + 1) * HALF)
-    inv = 1.0 / total
-    mixed = dot(qkvt_ref[pair(2 * DS, h), rows], e_ref[half * SIDE_HEADS + h])
-    ctxt_ref[own_rows(h), rows] = head_rows(mixed, h) * inv
-    inv_ref[own_rows(h), rows] = jnp.broadcast_to(inv, (SIDE_HEAD_DIM, HALF))
 
 
 def side_kernel(
     first_ref,
     lens_ref,
-    mid0_ref,
-    mid_ref,
-    next_ref,
+    ctx0_ref,
+    turned0_ref,
+    ctx_ref,
+    turned_ref,
+    woa_ref,
+    wob_ref,
     w1a_ref,
     w1b_ref,
     w2a_ref,
@@ -271,7 +281,9 @@
     state_ref,
     mine_ref,
     other_ref,
+    wo_ref,
     w2_ref,
+    mid_ref,
     hid_ref,
     nb_ref,
     f_ref,
@@ -287,19 +299,29 @@
     ctxt_ref,
     qkvt_ref,
     dq_ref,
-    turned_ref,
+    rolled_ref,
+    vt_ref,
 ):
     r = pl.program_id(0)
     last = pl.num_programs(0) - 1
     units = w1a_ref.shape[1]
 
-    def norm_ahead(ref):
-        middle = ref[...]
+    def middle_ahead(ctx, turned, half):
+        rows = slice(half * HALF, (half + 1) * HALF)
+        mid_ref[rows] = turned[rows].astype(F32) + dot(ctx[:, rows].T, wo_ref[...])
+
+    def norm_ahead():
+        middle = mid_ref[...]
         nb_ref[...] = (middle * lax.rsqrt(jnp.mean(middle * middle, axis=1, keepdims=True) + EPS) * fgain_ref[...].reshape(1, D)).astype(BF)
 
     @pl.when(r == 0)
     def _():
-        norm_ahead(mid0_ref)
+        heads = woa_ref.shape[0]
+        wo_ref[:heads] = woa_ref[...]
+        wo_ref[heads:] = wob_ref[...]
+        middle_ahead(ctx0_ref, turned0_ref, 0)
+        middle_ahead(ctx0_ref, turned0_ref, 1)
+        norm_ahead()
         w2_ref[:units] = w2a_ref[...]
         w2_ref[units:] = w2b_ref[...]
         grads_ref[...] = jnp.zeros_like(grads_ref)
@@ -315,8 +337,8 @@
     back = (ROW_LEN - shift) & (ROW_LEN - 1)
     fill_bias(bias_ref, docs)
 
-    turned_ref[0] = pltpu.roll(side_ref[...].astype(F32), back, 1)
-    turned_ref[1] = pltpu.roll(cot_ref[...].astype(F32), back, 1)
+    rolled_ref[0] = pltpu.roll(side_ref[...].astype(F32), back, 1)
+    rolled_ref[1] = pltpu.roll(cot_ref[...].astype(F32), back, 1)
 
     for i, w in enumerate((w1a_ref, w1b_ref)):
         for c in range(0, units, 256):
@@ -324,26 +346,31 @@
 
     for c in range(0, ROW_LEN, 256):
         f_ref[c : c + 256] = mid_ref[c : c + 256] + dot(hid_ref[c : c + 256], w2_ref[...])
-    norm_ahead(next_ref)
     bb = f_ref[...].astype(BF)
-    bb_out_ref[...] = turn_rows(f_ref, back).astype(BF)
 
     mixing, gain1, gain2 = cols_ref[0], cols_ref[1], cols_ref[2]
     lowered = dot(downt_ref[...], bb, 1, 1)
-    activated_grad = dot(shrinkt_ref[...], turned_ref[1].astype(BF), 0, 0)
-    side = turned_ref[0]
+    activated_grad = dot(shrinkt_ref[...], rolled_ref[1].astype(BF), 0, 0)
+    middle_ahead(ctx_ref, turned_ref, 0)
+    side = rolled_ref[0]
     inputs = mixing * lowered + (1.0 - mixing) * side
     scale1 = lax.rsqrt(jnp.mean(inputs * inputs, axis=0, keepdims=True) + EPS)
     fnt = (inputs * scale1 * gain1).astype(BF)
-    qkvt_ref[...] = dot(wqkvt_ref[...], fnt).astype(BF)
+    qkv = dot(wqkvt_ref[...], fnt)
+    qkvt_ref[:DS] = (qkv[:DS] * (LOG2E * SIDE_HEAD_DIM**-0.5)).astype(BF)
+    qkvt_ref[DS:] = qkv[DS:].astype(BF)
+    ones = jnp.ones((SIDE_HEADS, 8, ROW_LEN), F32)
+    vt_ref[...] = jnp.concatenate([qkv[2 * DS :].reshape(SIDE_HEADS, 8, ROW_LEN), ones], axis=1).reshape(2 * DS, ROW_LEN).astype(BF)
+    middle_ahead(ctx_ref, turned_ref, 1)
     k, v = qkvt_ref[DS : 2 * DS].T, qkvt_ref[2 * DS :].T
+    norm_ahead()
     blocks = [(half, h) for half in range(2) for h in range(SIDE_HEADS)]
     sums = []
     for n, (half, h) in enumerate(blocks + [(None, None)] * LAG_FORWARD):
         if n < len(blocks):
-            sums.append(side_scores(half, h, k, qkvt_ref, e_ref, bias_ref, False))
+            side_scores(half, h, k, qkvt_ref, e_ref, bias_ref, False)
         if n >= LAG_FORWARD:
-            side_values(*blocks[n - LAG_FORWARD], qkvt_ref, e_ref, ctxt_ref, inv_ref, sums[n - LAG_FORWARD])
+            sums.append(side_values(*blocks[n - LAG_FORWARD], vt_ref, e_ref, ctxt_ref, inv_ref))
 
     @pl.when(out_of_range(sums))
     def _():
@@ -351,7 +378,8 @@
         for half in range(2):
 
             def again(h, carry):
-                side_values(half, h, qkvt_ref, e_ref, ctxt_ref, inv_ref, side_scores(half, h, keys, qkvt_ref, e_ref, bias_ref, True))
+                side_scores(half, h, keys, qkvt_ref, e_ref, bias_ref, True)
+                side_values(half, h, vt_ref, e_ref, ctxt_ref, inv_ref)
                 return carry
 
             lax.fori_loop(0, SIDE_HEADS, again, 0)
@@ -367,7 +395,7 @@
     expanded_grad = (activated_grad * slope).astype(BF)
     second_grad = dot(expand_ref[...], expanded_grad)
     low = D + 2 * SFF
-    cot = turned_ref[1]
+    cot = rolled_ref[1]
     cotb = cot.astype(BF)
     side_out = middle_side + dot(shrinkt_ref[...], activated)
     out_ref[...] = pltpu.roll(side_out, shift, 1)
@@ -411,13 +439,14 @@
     def key_step(n):
         half, h = blocks[n]
         rows = slice(half * HALF, (half + 1) * HALF)
-        dq_ref[own_rows(h, DS), rows] = head_rows(dot(qkvt_ref[pair(0, h), rows], e_ref[n]), h) * root
+        dq_ref[own_rows(h, DS), rows] = head_rows(dot(qkvt_ref[pair(0, h), rows], e_ref[n]), h) * (1.0 / LOG2E)
 
     for n in range(len(blocks) + 3 * LAG_BACK):
         for i, step in enumerate((score_step, query_step, value_step, key_step)):
             if 0 <= n - i * LAG_BACK < len(blocks):
                 step(n - i * LAG_BACK)
     dqkvt = dq_ref[...].astype(BF)
+    bb_out_ref[...] = turn_rows(f_ref, back).astype(BF)
     first_grad = dot(wqkvt_ref[...], dqkvt, 0, 0)
     grads_ref[:, low : low + 3 * DS] += dot(fnt, dqkvt, 1, 1)
     w1 = first_grad * gain1
@@ -533,7 +562,7 @@
         first = (t * rows).astype(jnp.int32).reshape(1)
         tile = pl.BlockSpec((ROW_LEN, D), lambda r, *_: (r, 0))
         hbm = pl.BlockSpec(memory_space=pltpu.HBM)
-        lens = lengths.T
+        lens = pltpu.with_memory_space_constraint(lengths.T, pltpu.HBM)
 
         def kernel(body, name, limit, in_specs, out_specs, out_shape, scratch):
             return pl.pallas_call(
@@ -546,40 +575,46 @@
                 name=name,
             )
 
-        own_attn = (attn_query, attn_key, attn_value, attn_out)
+        own_attn = (attn_query, attn_key, attn_value)
         far_attn = [swap(w) for w in own_attn]
         own_attn = [pltpu.with_memory_space_constraint(w, pltpu.HBM) for w in own_attn]
         hidden_in = pltpu.with_memory_space_constraint(hidden_in, pltpu.HBM)
         attn_gain = pltpu.with_memory_space_constraint(attn_gain, pltpu.HBM)
-        turned, normed = kernel(
+        turned, joined = kernel(
             turn_kernel,
             "turn_rows",
-            13,
-            [hbm, whole((D,))],
-            [tile, tile],
-            [jax.ShapeDtypeStruct((tokens, D), BF)] * 2,
-            [pltpu.VMEM((rows, ROW_LEN, D), BF), pltpu.VMEM((ROW_LEN, D), F32), pltpu.SemaphoreType.DMA((rows,))],
-        )(first, lens, hidden_in, attn_gain)
-        far_attn, turned, normed, ffn_in, ffn_out = lax.optimization_barrier((far_attn, turned, normed, ffn_in, ffn_out))
-        far_ffn = [swap(w) for w in (ffn_in, ffn_out)]
-        mid = kernel(
+            11,
+            [hbm] * 4,
+            [tile, pl.BlockSpec(memory_space=pl.ANY)],
+            [jax.ShapeDtypeStruct((tokens, D), BF), jax.ShapeDtypeStruct((3, D, attn_query.shape[1]), BF)],
+            [
+                pltpu.VMEM((rows, ROW_LEN, D), BF),
+                pltpu.VMEM((ROW_LEN, D), F32),
+                pltpu.SemaphoreType.DMA((rows,)),
+                pltpu.SemaphoreType.DMA((3,)),
+            ],
+        )(first, lens, hidden_in, *own_attn)
+        far_attn, turned, attn_out, ffn_in, ffn_out = lax.optimization_barrier((far_attn, turned, attn_out, ffn_in, ffn_out))
+        far_out, far_in, far_shrink = [swap(w) for w in (attn_out, ffn_in, ffn_out)]
+        next_tile = pl.BlockSpec((ROW_LEN, D), lambda r, *_: (jnp.minimum(r + 1, rows - 1), 0))
+        wide_tile = pl.BlockSpec((D, ROW_LEN), lambda r, *_: (0, r))
+        ctx = kernel(
             attention_kernel,
             "attention",
-            22,
-            [tile, tile] + [hbm] * 8,
-            tile,
-            jax.ShapeDtypeStruct((tokens, D), F32),
+            20,
+            [whole((ROW_LEN, D)), next_tile, whole((D,)), pl.BlockSpec(memory_space=pl.ANY)] + [hbm] * 3,
+            wide_tile,
+            jax.ShapeDtypeStruct((D, tokens), BF),
             [
                 pltpu.VMEM((D, 3 * D), BF),
-                pltpu.VMEM((D, D), BF),
                 pltpu.VMEM((ROW_LEN, 3 * D), BF),
                 pltpu.VMEM((D, ROW_LEN), BF),
                 pltpu.VMEM((2 * HEADS, HALF, HALF), BF),
-                pltpu.VMEM((D, ROW_LEN), BF),
                 pltpu.VMEM((HALF, HALF), F32),
-                pltpu.SemaphoreType.DMA((8,)),
+                pltpu.VMEM((ROW_LEN, D), BF),
+                pltpu.SemaphoreType.DMA((6,)),
             ],
-        )(first, lens, turned, normed, *[w for both in zip(own_attn, far_attn) for w in both])
+        )(first, lens, turned, turned, attn_gain, joined, *far_attn)
         side_tile = pl.BlockSpec((DS, ROW_LEN), lambda r, *_: (0, r))
         side = pltpu.VMEM((DS, ROW_LEN), F32)
         square = pltpu.VMEM((2 * SIDE_HEADS, HALF, HALF), BF)
@@ -587,7 +622,13 @@
             side_kernel,
             "forward_and_back",
             32,
-            [whole((ROW_LEN, D)), tile, pl.BlockSpec((ROW_LEN, D), lambda r, *_: (jnp.minimum(r + 1, rows - 1), 0))]
+            [
+                whole((D, ROW_LEN)),
+                whole((ROW_LEN, D)),
+                pl.BlockSpec((D, ROW_LEN), lambda r, *_: (0, jnp.minimum(r + 1, rows - 1))),
+                next_tile,
+            ]
+            + [whole((D // 2, D))] * 2
             + [whole((D, units))] * 2
             + [whole((units, D))] * 2
             + [whole((D,)), side_tile, side_tile]
@@ -604,7 +645,9 @@
                 jax.ShapeDtypeStruct((DS // 2, GRAD_LANES), BF),
             ],
             [
+                pltpu.VMEM((D, D), BF),
                 pltpu.VMEM((2 * units, D), BF),
+                pltpu.VMEM((ROW_LEN, D), F32),
                 pltpu.VMEM((ROW_LEN, 2 * units), BF),
                 pltpu.VMEM((ROW_LEN, D), BF),
                 pltpu.VMEM((ROW_LEN, D), F32),
@@ -621,17 +664,21 @@
                 pltpu.VMEM((3 * DS, ROW_LEN), BF),
                 pltpu.VMEM((3 * DS, ROW_LEN), F32),
                 pltpu.VMEM((2, DS, ROW_LEN), F32),
+                pltpu.VMEM((2 * DS, ROW_LEN), BF),
             ],
         )(
             first,
             lens,
-            mid,
-            mid,
-            mid,
+            ctx,
+            turned,
+            ctx,
+            turned,
+            attn_out,
+            far_out,
             ffn_in,
-            far_ffn[0],
+            far_in,
             ffn_out,
-            far_ffn[1],
+            far_shrink,
             ffn_gain,
             side_state.T,
             cotangent.T,

time: 121 us -> 119 us (0.983)
  Pallas kernels: 89.7 us -> 87.9 us
    pallas_call x3, Pallas kernels: 88.8 us -> 86.9 us  [the longest x1 62.3 us: body(): kernel(side_kernel, 'forward_and_back', 32, [whole((D, ROW_LEN)), whole((...]
  transfers between devices with their start and end apart: 16 -> 16, of which waited for: 10 -> 10; matrix products, arithmetic and copies ran while one was open for 0% -> 0% of each run, Pallas kernels for 24% -> 21%
where the time goes in v5:
time: 119 us; the launch traced here: 118 us
  Pallas kernels  87.9 us (74%)
  starting transfers between devices  14.8 us (12%)
  waiting for transfers between devices  14.5 us (12%)
    pallas_call x1, Pallas kernels, body(): kernel(side_kernel, 'forward_and_back', 32, [whole((D, ROW_LEN)), whole((...  62.3 us
    pallas_call x1, Pallas kernels, body(): kernel(attention_kernel, 'attention', 20, [whole((ROW_LEN, D)), next_tile...  20.4 us
    ppermute x8, starting transfers between devices, trade(): return lax.ppermute(x, 'batch', [(i, i ^ bits) for i in range(batch)])  12.6 us
    ppermute x8, waiting for transfers between devices, trade(): return lax.ppermute(x, 'batch', [(i, i ^ bits) for i in range(batch)])  12 us
    pallas_call x1, Pallas kernels, body(): kernel(turn_kernel, 'turn_rows', 11, [hbm] * 4, [tile, pl.BlockSpec(memor...  4.23 us
    ppermute x8, waiting for transfers between devices, swap(): return lax.ppermute(x, 'tensor', [(0, 1), (1, 0)])  2.51 us
  transfers between devices with their start and end apart: 16, of which 10 were waited for; matrix products, arithmetic and copies ran while one was open for 0% of the time, Pallas kernels for 21%

profile of v5, /device:TPU:0, one launch (start us, length us, event | category | flops | bytes accessed | tf_op | source)
XLA Modules:
  0.0 118.4 jit_solution(5925735230274454854)
XLA Ops:
  0.6 0.5 collective-permute-start
  1.2 0.1 collective-permute-start.1
  1.2 0.4 collective-permute-start.2
  1.7 4.2 %turn_rows.1 = (bf16[2560,768]{1,0:T(8,128)(2,1)S(1)}, bf16[3,768,384]{2,1,0:T(8,128)(2,1)S(1)}) custom-call(s32[1]{0:T(128)} %bitcast.first_ref.tensor_ref, s32[8,10]{1,0:T(8,128)} %bitcast.14, bf16[2560,768]{1,0:T(8,128)(2,1)} %x_ref.1, bf16[768,384]{1,0:T(8,128)(2,1)} %wq_ref.1, bf16[768,384]{1,0:T(8,128)(2,1)} %wk_ref.1, bf16[768,384]{1,0:T(8,128)(2,1)} %wv_ref.1), custom_call_target="tpu_custom_call" | custom-call | tf_op jit(solution)/shard_map/turn_rows/pallas_call | solution.py:583
  6.0 0.1 collective-permute-start.4
  6.1 0.4 collective-permute-start.5
  6.5 0.1 collective-permute-start.3
  6.7 0.0 copy-start.8
  6.7 0.0 copy-start.9
  6.8 20.4 %attention.1.ctx0_ref.ctx_ref = bf16[768,2560]{1,0:T(8,128)(2,1)S(1)} custom-call(s32[1]{0:T(128)} %bitcast.first_ref.tensor_ref, s32[8,10]{1,0:T(8,128)} %bitcast.15, bf16[2560,768]{1,0:T(8,128)(2,1)S(1)} %get-tuple-element.38.turned0_ref.turned_ref, bf16[2560,768]{1,0:T(8,128)(2,1)S(1)} %get-tuple-element.38.turned0_ref.turned_ref, f32[768]{0:T(1024)} %gain_ref.1, ...), custom_call_target="tpu_custom_call" | custom-call | tf_op jit(solution)/shard_map/attention/pallas_call | solution.py:601
  27.3 62.3 %forward_and_back.1 = (bf16[2560,768]{1,0:T(8,128)(2,1)}, f32[96,2560]{1,0:T(8,128)}, f32[96,2560]{1,0:T(8,128)}, bf16[48,2048]{1,0:T(8,128)(2,1)S(1)}, bf16[48,2048]{1,0:T(8,128)(2,1)S(1)}) custom-call(s32[1]{0:T(128)} %bitcast.first_ref.tensor_ref, s32[8,10]{1,0:T(8,128)} %bitcast.16, bf16[768,2560]{1,0:T(8,128)(2,1)S(1)} %attention.1.ctx0_ref.ctx_ref, ...), custom_call_target="tpu_custom_call" | custom-call | tf_op jit(solution)/shard_map/forward_and_back/pallas_call | solution.py:621
  89.6 0.5 collective-permute-start.6
  90.1 1.1 collective-permute-done.6
  91.2 2.9 %collective-permute-start.7 = (bf16[48,512]{1,0:T(8,128)(2,1)S(1)}, bf16[48,512]{1,0:T(8,128)(2,1)S(1)}, u32[]{:S(2)}, u32[]{:S(2)}) collective-permute-start(bf16[48,512]{1,0:T(8,128)(2,1)S(1)} %get-tuple-element.65), channel_id=1, source_target_pairs={{0,2},{2,0},{4,6},{6,4},{8,10},{10,8},{12,14},{14,12},{16,18},{18,... | collective-permute-start | bytes 147464 | tf_op jit(solution)/shard_map/ppermute | solution.py:491
  94.1 1.5 %collective-permute-start.8 = (bf16[48,512]{1,0:T(8,128)(2,1)S(1)}, bf16[48,512]{1,0:T(8,128)(2,1)S(1)}, u32[]{:S(2)}, u32[]{:S(2)}) collective-permute-start(bf16[48,512]{1,0:T(8,128)(2,1)S(1)} %get-tuple-element.66), channel_id=1, source_target_pairs={{0,4},{2,6},{4,0},{6,2},{8,12},{10,14},{12,8},{14,10},{16,20},{18,... | collective-permute-start | bytes 147464 | tf_op jit(solution)/shard_map/ppermute | solution.py:491
  95.7 0.1 collective-permute-start.9
  95.8 0.4 collective-permute-done.7
  96.2 2.0 %collective-permute-done.8 = bf16[48,512]{1,0:T(8,128)(2,1)S(1)} collective-permute-done((bf16[48,512]{1,0:T(8,128)(2,1)S(1)}, bf16[48,512]{1,0:T(8,128)(2,1)S(1)}, u32[]{:S(2)}, u32[]{:S(2)}) %collective-permute-start.8) | collective-permute-done | bytes 49184 | tf_op jit(solution)/shard_map/ppermute | solution.py:491
  98.2 2.5 %collective-permute-done.9 = bf16[48,512]{1,0:T(8,128)(2,1)S(1)} collective-permute-done((bf16[48,512]{1,0:T(8,128)(2,1)S(1)}, bf16[48,512]{1,0:T(8,128)(2,1)S(1)}, u32[]{:S(2)}, u32[]{:S(2)}) %collective-permute-start.9) | collective-permute-done | bytes 49184 | tf_op jit(solution)/shard_map/ppermute | solution.py:491
  100.8 1.6 %collective-permute-start.10 = (bf16[48,512]{1,0:T(8,128)(2,1)S(1)}, bf16[48,512]{1,0:T(8,128)(2,1)S(1)}, u32[]{:S(2)}, u32[]{:S(2)}) collective-permute-start(bf16[48,512]{1,0:T(8,128)(2,1)S(1)} %add_convert_fusion.3), channel_id=1, source_target_pairs={{0,8},{2,10},{4,12},{6,14},{8,0},{10,2},{12,4},{14,6},{16,24},{18,... | collective-permute-start | bytes 147464 | tf_op jit(solution)/shard_map/ppermute | solution.py:491
  102.4 2.5 %collective-permute-done.10 = bf16[48,512]{1,0:T(8,128)(2,1)S(1)} collective-permute-done((bf16[48,512]{1,0:T(8,128)(2,1)S(1)}, bf16[48,512]{1,0:T(8,128)(2,1)S(1)}, u32[]{:S(2)}, u32[]{:S(2)}) %collective-permute-start.10) | collective-permute-done | bytes 49184 | tf_op jit(solution)/shard_map/ppermute | solution.py:491
  105.0 2.9 %collective-permute-start.11 = (bf16[48,512]{1,0:T(8,128)(2,1)S(1)}, bf16[48,512]{1,0:T(8,128)(2,1)S(1)}, u32[]{:S(2)}, u32[]{:S(2)}) collective-permute-start(bf16[48,512]{1,0:T(8,128)(2,1)S(1)} %add_convert_fusion.2), channel_id=1, source_target_pairs={{0,16},{2,18},{4,20},{6,22},{8,24},{10,26},{12,28},{14,30},{16,0},... | collective-permute-start | bytes 147464 | tf_op jit(solution)/shard_map/ppermute | solution.py:491
  107.9 2.2 %collective-permute-done.11 = bf16[48,512]{1,0:T(8,128)(2,1)S(1)} collective-permute-done((bf16[48,512]{1,0:T(8,128)(2,1)S(1)}, bf16[48,512]{1,0:T(8,128)(2,1)S(1)}, u32[]{:S(2)}, u32[]{:S(2)}) %collective-permute-start.11) | collective-permute-done | bytes 49184 | tf_op jit(solution)/shard_map/ppermute | solution.py:491
  110.0 0.6 collective-permute-start.12
  110.6 0.3 collective-permute-start.13
  110.9 2.7 %collective-permute-start.14 = (bf16[48,512]{1,0:T(8,128)(2,1)S(1)}, bf16[48,512]{1,0:T(8,128)(2,1)S(1)}, u32[]{:S(2)}, u32[]{:S(2)}) collective-permute-start(bf16[48,512]{1,0:T(8,128)(2,1)S(1)} %add_convert_fusion.1), channel_id=1, source_target_pairs={{0,6},{2,4},{4,2},{6,0},{8,14},{10,12},{12,10},{14,8},{16,22},{18,... | collective-permute-start | bytes 147464 | tf_op jit(solution)/shard_map/ppermute | solution.py:491
  113.6 0.6 collective-permute-done.12
  114.2 0.5 collective-permute-done.13
  114.7 1.2 %collective-permute-done.14 = bf16[48,512]{1,0:T(8,128)(2,1)S(1)} collective-permute-done((bf16[48,512]{1,0:T(8,128)(2,1)S(1)}, bf16[48,512]{1,0:T(8,128)(2,1)S(1)}, u32[]{:S(2)}, u32[]{:S(2)}) %collective-permute-start.14) | collective-permute-done | bytes 49184 | tf_op jit(solution)/shard_map/ppermute | solution.py:491
  116.0 0.1 collective-permute-start.15
  116.1 1.4 %collective-permute-done.15.got_ref = bf16[48,2048]{1,0:T(8,128)(2,1)S(1)} collective-permute-done((bf16[48,2048]{1,0:T(8,128)(2,1)S(1)}, bf16[48,2048]{1,0:T(8,128)(2,1)S(1)}, u32[]{:S(2)}, u32[]{:S(2)}) %collective-permute-start.15) | collective-permute-done | bytes 196640 | tf_op jit(solution)/shard_map/ppermute | solution.py:483
  117.5 0.9 unpack.1
  (44 shorter events, 0.3 us)
Async XLA Ops:
  0.6 5.3 %collective-permute-start = (bf16[768,384]{1,0:T(8,128)(2,1)}, bf16[768,384]{1,0:T(8,128)(2,1)S(1)}, u32[]{:S(2)}, u32[]{:S(2)}) collective-permute-start(bf16[768,384]{1,0:T(8,128)(2,1)} %wq_ref.1), channel_id=1, source_target_pairs={{0,1},{1,0},{2,3},{3,2},{4,5},{5,4},{6,7},{7,6},{8,9},{9,8},{10,11... | collective-permute-start | bytes 1769480 | tf_op jit(solution)/shard_map/ppermute | solution.py:483
  1.2 4.8 %collective-permute-start.1 = (bf16[768,384]{1,0:T(8,128)(2,1)}, bf16[768,384]{1,0:T(8,128)(2,1)S(1)}, u32[]{:S(2)}, u32[]{:S(2)}) collective-permute-start(bf16[768,384]{1,0:T(8,128)(2,1)} %wk_ref.1), channel_id=1, source_target_pairs={{0,1},{1,0},{2,3},{3,2},{4,5},{5,4},{6,7},{7,6},{8,9},{9,8},{10,11... | collective-permute-start | bytes 1769480 | tf_op jit(solution)/shard_map/ppermute | solution.py:483
  1.2 4.7 %collective-permute-start.2 = (bf16[768,384]{1,0:T(8,128)(2,1)}, bf16[768,384]{1,0:T(8,128)(2,1)S(1)}, u32[]{:S(2)}, u32[]{:S(2)}) collective-permute-start(bf16[768,384]{1,0:T(8,128)(2,1)} %wv_ref.1), channel_id=1, source_target_pairs={{0,1},{1,0},{2,3},{3,2},{4,5},{5,4},{6,7},{7,6},{8,9},{9,8},{10,11... | collective-permute-start | bytes 1769480 | tf_op jit(solution)/shard_map/ppermute | solution.py:483
  1.7 4.3 %copy-start = (bf16[768,1536]{1,0:T(8,128)(2,1)S(1)}, bf16[768,1536]{1,0:T(8,128)(2,1)}, u32[]{:S(2)}) copy-start(bf16[768,1536]{1,0:T(8,128)(2,1)} %w1a_ref) | copy-start | bytes 7077892
  1.7 4.4 %copy-start.1 = (bf16[1536,768]{1,0:T(8,128)(2,1)S(1)}, bf16[1536,768]{1,0:T(8,128)(2,1)}, u32[]{:S(2)}) copy-start(bf16[1536,768]{1,0:T(8,128)(2,1)} %w2a_ref) | copy-start | bytes 7077892
  1.7 4.9 %copy-start.2 = (bf16[384,768]{1,0:T(8,128)(2,1)S(1)}, bf16[384,768]{1,0:T(8,128)(2,1)}, u32[]{:S(2)}) copy-start(bf16[384,768]{1,0:T(8,128)(2,1)} %woa_ref) | copy-start | bytes 1769476
  6.0 21.2 %collective-permute-start.4 = (bf16[768,1536]{1,0:T(8,128)(2,1)S(1)}, bf16[768,1536]{1,0:T(8,128)(2,1)S(1)}, u32[]{:S(2)}, u32[]{:S(2)}) collective-permute-start(bf16[768,1536]{1,0:T(8,128)(2,1)S(1)} %copy-done), channel_id=1, source_target_pairs={{0,1},{1,0},{2,3},{3,2},{4,5},{5,4},{6,7},{7,6},{8,9},{9,8},{10,11... | collective-permute-start | bytes 7077896 | tf_op jit(solution)/shard_map/ppermute | solution.py:483
  6.1 21.1 %collective-permute-start.5 = (bf16[1536,768]{1,0:T(8,128)(2,1)S(1)}, bf16[1536,768]{1,0:T(8,128)(2,1)S(1)}, u32[]{:S(2)}, u32[]{:S(2)}) collective-permute-start(bf16[1536,768]{1,0:T(8,128)(2,1)S(1)} %copy-done.1), channel_id=1, source_target_pairs={{0,1},{1,0},{2,3},{3,2},{4,5},{5,4},{6,7},{7,6},{8,9},{9,8},{10,11... | collective-permute-start | bytes 7077896 | tf_op jit(solution)/shard_map/ppermute | solution.py:483
  6.5 20.6 %collective-permute-start.3 = (bf16[384,768]{1,0:T(8,128)(2,1)S(1)}, bf16[384,768]{1,0:T(8,128)(2,1)S(1)}, u32[]{:S(2)}, u32[]{:S(2)}) collective-permute-start(bf16[384,768]{1,0:T(8,128)(2,1)S(1)} %copy-done.2), channel_id=1, source_target_pairs={{0,1},{1,0},{2,3},{3,2},{4,5},{5,4},{6,7},{7,6},{8,9},{9,8},{10,11... | collective-permute-start | bytes 1769480 | tf_op jit(solution)/shard_map/ppermute | solution.py:483
  6.6 20.6 %copy-start.3 = (bf16[2560,96]{0,1:T(8,128)(2,1)S(1)}, bf16[2560,96]{0,1:T(8,128)(2,1)}, u32[]{:S(2)}) copy-start(bf16[2560,96]{0,1:T(8,128)(2,1)} %param.32) | copy-start | bytes 1474564
  6.6 20.6 %copy-start.4 = (bf16[2560,96]{0,1:T(8,128)(2,1)S(1)}, bf16[2560,96]{0,1:T(8,128)(2,1)}, u32[]{:S(2)}) copy-start(bf16[2560,96]{0,1:T(8,128)(2,1)} %param.43) | copy-start | bytes 1474564
  6.6 20.6 %copy-start.5 = (bf16[768,96]{0,1:T(8,128)(2,1)S(1)}, bf16[768,96]{0,1:T(8,128)(2,1)}, u32[]{:S(2)}) copy-start(bf16[768,96]{0,1:T(8,128)(2,1)} %param.34) | copy-start | bytes 442372
  6.6 20.6 %copy-start.6 = (bf16[96,384]{1,0:T(8,128)(2,1)S(1)}, bf16[96,384]{1,0:T(8,128)(2,1)}, u32[]{:S(2)}) copy-start(bf16[96,384]{1,0:T(8,128)(2,1)} %expand_ref.1) | copy-start | bytes 221188
  6.6 20.6 %copy-start.7 = (bf16[384,96]{0,1:T(8,128)(2,1)S(1)}, bf16[384,96]{0,1:T(8,128)(2,1)}, u32[]{:S(2)}) copy-start(bf16[384,96]{0,1:T(8,128)(2,1)} %param.42) | copy-start | bytes 221188
  6.7 20.6 %copy-start.8 = (bf16[96,96]{1,0:T(8,128)(2,1)S(1)}, bf16[96,96]{1,0:T(8,128)(2,1)}, u32[]{:S(2)}) copy-start(bf16[96,96]{1,0:T(8,128)(2,1)} %sq_ref.1) | copy-start | bytes 55300
  6.7 20.6 %copy-start.9 = (bf16[96,96]{1,0:T(8,128)(2,1)S(1)}, bf16[96,96]{1,0:T(8,128)(2,1)}, u32[]{:S(2)}) copy-start(bf16[96,96]{1,0:T(8,128)(2,1)} %sk_ref.1) | copy-start | bytes 55300
  6.7 20.6 %copy-start.10 = (bf16[96,96]{1,0:T(8,128)(2,1)S(1)}, bf16[96,96]{1,0:T(8,128)(2,1)}, u32[]{:S(2)}) copy-start(bf16[96,96]{1,0:T(8,128)(2,1)} %sv_ref.1) | copy-start | bytes 55300
  6.7 20.6 %copy-start.11 = (bf16[96,96]{1,0:T(8,128)(2,1)S(1)}, bf16[96,96]{1,0:T(8,128)(2,1)}, u32[]{:S(2)}) copy-start(bf16[96,96]{1,0:T(8,128)(2,1)} %proj_ref.1) | copy-start | bytes 55300
  6.7 20.6 %copy-start.12 = (f32[768]{0:T(1024)S(1)}, f32[768]{0:T(1024)}, u32[]{:S(2)}) copy-start(f32[768]{0:T(1024)} %fgain_ref.1) | copy-start | bytes 9220
  6.7 20.6 %copy-start.13 = (f32[96]{0:T(128)S(1)}, f32[96]{0:T(128)}, u32[]{:S(2)}) copy-start(f32[96]{0:T(128)} %alpha_ref.1) | copy-start | bytes 1156
  6.7 20.6 %copy-start.14 = (f32[96]{0:T(128)S(1)}, f32[96]{0:T(128)}, u32[]{:S(2)}) copy-start(f32[96]{0:T(128)} %gain1_ref.1) | copy-start | bytes 1156
  6.7 20.6 %copy-start.15 = (f32[96]{0:T(128)S(1)}, f32[96]{0:T(128)}, u32[]{:S(2)}) copy-start(f32[96]{0:T(128)} %gain2_ref.1) | copy-start | bytes 1156
  89.6 1.5 %collective-permute-start.6 = (bf16[48,2048]{1,0:T(8,128)(2,1)S(1)}, bf16[48,2048]{1,0:T(8,128)(2,1)S(1)}, u32[]{:S(2)}, u32[]{:S(2)}) collective-permute-start(bf16[48,2048]{1,0:T(8,128)(2,1)S(1)} %get-tuple-element.50), channel_id=1, source_target_pairs={{0,1},{1,0},{2,3},{3,2},{4,5},{5,4},{6,7},{7,6},{8,9},{9,8},{10,11... | collective-permute-start | bytes 589832 | tf_op jit(solution)/shard_map/ppermute | solution.py:483
  91.2 5.0 %collective-permute-start.7 = (bf16[48,512]{1,0:T(8,128)(2,1)S(1)}, bf16[48,512]{1,0:T(8,128)(2,1)S(1)}, u32[]{:S(2)}, u32[]{:S(2)}) collective-permute-start(bf16[48,512]{1,0:T(8,128)(2,1)S(1)} %get-tuple-element.65), channel_id=1, source_target_pairs={{0,2},{2,0},{4,6},{6,4},{8,10},{10,8},{12,14},{14,12},{16,18},{18,... | collective-permute-start | bytes 147464 | tf_op jit(solution)/shard_map/ppermute | solution.py:491
  94.1 4.1 %collective-permute-start.8 = (bf16[48,512]{1,0:T(8,128)(2,1)S(1)}, bf16[48,512]{1,0:T(8,128)(2,1)S(1)}, u32[]{:S(2)}, u32[]{:S(2)}) collective-permute-start(bf16[48,512]{1,0:T(8,128)(2,1)S(1)} %get-tuple-element.66), channel_id=1, source_target_pairs={{0,4},{2,6},{4,0},{6,2},{8,12},{10,14},{12,8},{14,10},{16,20},{18,... | collective-permute-start | bytes 147464 | tf_op jit(solution)/shard_map/ppermute | solution.py:491
  95.7 5.1 %collective-permute-start.9 = (bf16[48,512]{1,0:T(8,128)(2,1)S(1)}, bf16[48,512]{1,0:T(8,128)(2,1)S(1)}, u32[]{:S(2)}, u32[]{:S(2)}) collective-permute-start(bf16[48,512]{1,0:T(8,128)(2,1)S(1)} %select_select_fusion.4), channel_id=1, source_target_pairs={{0,6},{2,4},{4,2},{6,0},{8,14},{10,12},{12,10},{14,8},{16,22},{18,... | collective-permute-start | bytes 147464 | tf_op jit(solution)/shard_map/ppermute | solution.py:491
  100.8 4.2 %collective-permute-start.10 = (bf16[48,512]{1,0:T(8,128)(2,1)S(1)}, bf16[48,512]{1,0:T(8,128)(2,1)S(1)}, u32[]{:S(2)}, u32[]{:S(2)}) collective-permute-start(bf16[48,512]{1,0:T(8,128)(2,1)S(1)} %add_convert_fusion.3), channel_id=1, source_target_pairs={{0,8},{2,10},{4,12},{6,14},{8,0},{10,2},{12,4},{14,6},{16,24},{18,... | collective-permute-start | bytes 147464 | tf_op jit(solution)/shard_map/ppermute | solution.py:491
  105.0 5.1 %collective-permute-start.11 = (bf16[48,512]{1,0:T(8,128)(2,1)S(1)}, bf16[48,512]{1,0:T(8,128)(2,1)S(1)}, u32[]{:S(2)}, u32[]{:S(2)}) collective-permute-start(bf16[48,512]{1,0:T(8,128)(2,1)S(1)} %add_convert_fusion.2), channel_id=1, source_target_pairs={{0,16},{2,18},{4,20},{6,22},{8,24},{10,26},{12,28},{14,30},{16,0},... | collective-permute-start | bytes 147464 | tf_op jit(solution)/shard_map/ppermute | solution.py:491
  110.0 4.2 %collective-permute-start.12 = (bf16[48,512]{1,0:T(8,128)(2,1)S(1)}, bf16[48,512]{1,0:T(8,128)(2,1)S(1)}, u32[]{:S(2)}, u32[]{:S(2)}) collective-permute-start(bf16[48,512]{1,0:T(8,128)(2,1)S(1)} %add_convert_fusion.1), channel_id=1, source_target_pairs={{0,2},{2,0},{4,6},{6,4},{8,10},{10,8},{12,14},{14,12},{16,18},{18,... | collective-permute-start | bytes 147464 | tf_op jit(solution)/shard_map/ppermute | solution.py:491
  110.6 4.1 %collective-permute-start.13 = (bf16[48,512]{1,0:T(8,128)(2,1)S(1)}, bf16[48,512]{1,0:T(8,128)(2,1)S(1)}, u32[]{:S(2)}, u32[]{:S(2)}) collective-permute-start(bf16[48,512]{1,0:T(8,128)(2,1)S(1)} %add_convert_fusion.1), channel_id=1, source_target_pairs={{0,4},{2,6},{4,0},{6,2},{8,12},{10,14},{12,8},{14,10},{16,20},{18,... | collective-permute-start | bytes 147464 | tf_op jit(solution)/shard_map/ppermute | solution.py:491
  110.9 5.0 %collective-permute-start.14 = (bf16[48,512]{1,0:T(8,128)(2,1)S(1)}, bf16[48,512]{1,0:T(8,128)(2,1)S(1)}, u32[]{:S(2)}, u32[]{:S(2)}) collective-permute-start(bf16[48,512]{1,0:T(8,128)(2,1)S(1)} %add_convert_fusion.1), channel_id=1, source_target_pairs={{0,6},{2,4},{4,2},{6,0},{8,14},{10,12},{12,10},{14,8},{16,22},{18,... | collective-permute-start | bytes 147464 | tf_op jit(solution)/shard_map/ppermute | solution.py:491
  116.0 1.5 %collective-permute-start.15 = (bf16[48,2048]{1,0:T(8,128)(2,1)S(1)}, bf16[48,2048]{1,0:T(8,128)(2,1)S(1)}, u32[]{:S(2)}, u32[]{:S(2)}) collective-permute-start(bf16[48,2048]{1,0:T(8,128)(2,1)S(1)} %pad_maximum_fusion.sent_ref), channel_id=1, source_target_pairs={{0,1},{1,0},{2,3},{3,2},{4,5},{5,4},{6,7},{7,6},{8,9},{9,8},{10,11... | collective-permute-start | bytes 589832 | tf_op jit(solution)/shard_map/ppermute | solution.py:483

commit v6 on v5

--- a/solution.py
+++ b/solution.py
@@ -38,10 +38,9 @@
 def gelu_and_slope(x):
     x2 = x * x
     u = x * (x2 * (0.7978845608028654 * 0.044715) + 0.7978845608028654)
-    t = jnp.tanh(u)
-    h = 0.5 * x
-    du = 0.7978845608028654 * 3.0 * 0.044715 * x2 + 0.7978845608028654
-    return h + h * t, 0.5 + 0.5 * t + h * (1.0 - t * t) * du
+    p = 0.5 + 0.5 * jnp.tanh(u)
+    out = x * p
+    return out, p + out * (1.0 - p) * (x2 * (1.5957691216057308 * 3.0 * 0.044715) + 1.5957691216057308)
 
 
 def row_starts(first_ref, lens_ref, r):
@@ -110,7 +109,7 @@
     rows = slice(half * HALF, (half + 1) * HALF)
     q2 = qkv_ref[rows, at(p * 128, 128, 128)]
     k2 = qkv_ref[rows, at(D + p * 128, 128, 128)]
-    s = dot(k2 * keep.astype(F32).astype(BF), q2, 1, 1)
+    s = dot(k2 * keep.astype(F32).astype(BF), q2, 1, 1) * (LOG2E * HEAD_DIM**-0.5)
     e = exponentials(s, half, bias_ref, safe)
     e_ref[half * HEADS + h] = e.astype(BF)
     return jnp.sum(e, axis=0, keepdims=True)
@@ -171,13 +170,9 @@
     e_ref,
     bias_ref,
     nb_ref,
-    sems,
 ):
     r = pl.program_id(0)
     cols = wq_ref.shape[1]
-    copies = []
-    for i, far in enumerate((wq_ref, wk_ref, wv_ref)):
-        copies += [(joined_ref.at[i], wqkv_ref.at[:, i * D : i * D + cols]), (far, wqkv_ref.at[:, i * D + cols : (i + 1) * D])]
 
     def norm_ahead(ref):
         x = ref[...].astype(F32)
@@ -185,14 +180,14 @@
 
     @pl.when(r == 0)
     def _():
-        start_copies(copies, sems)
         norm_ahead(turned0_ref)
-        wait_copies(copies, sems, 0, 6)
+        for i, far in enumerate((wq_ref, wk_ref, wv_ref)):
+            wqkv_ref[:, i * D : i * D + cols] = joined_ref[i]
+            wqkv_ref[:, i * D + cols : (i + 1) * D] = far[...]
 
     _, docs = row_starts(first_ref, lens_ref, r)
     fill_bias(bias_ref, docs)
-    qkv_ref[:, :D] = (dot(nb_ref[...], wqkv_ref[:, :D]) * (LOG2E * HEAD_DIM**-0.5)).astype(BF)
-    qkv_ref[:, D:] = dot(nb_ref[...], wqkv_ref[:, D:]).astype(BF)
+    qkv_ref[...] = dot(nb_ref[...], wqkv_ref[...]).astype(BF)
     norm_ahead(turned_ref)
     vt_ref[...] = qkv_ref[:, 2 * D :].T
     blocks = [(half, h) for half in range(2) for h in range(HEADS)]
@@ -236,7 +231,7 @@
 
 def side_scores(half, h, k, qkvt_ref, e_ref, bias_ref, safe):
     rows = slice(half * HALF, (half + 1) * HALF)
-    s = dot(k[rows] * head_mask(h, DS), qkvt_ref[:DS, rows])
+    s = dot(k[rows] * head_mask(h, DS), qkvt_ref[:DS, rows]) * (LOG2E * SIDE_HEAD_DIM**-0.5)
     e_ref[half * SIDE_HEADS + h] = exponentials(s, half, bias_ref, safe).astype(BF)
 
 
@@ -357,8 +352,7 @@
     scale1 = lax.rsqrt(jnp.mean(inputs * inputs, axis=0, keepdims=True) + EPS)
     fnt = (inputs * scale1 * gain1).astype(BF)
     qkv = dot(wqkvt_ref[...], fnt)
-    qkvt_ref[:DS] = (qkv[:DS] * (LOG2E * SIDE_HEAD_DIM**-0.5)).astype(BF)
-    qkvt_ref[DS:] = qkv[DS:].astype(BF)
+    qkvt_ref[...] = qkv.astype(BF)
     ones = jnp.ones((SIDE_HEADS, 8, ROW_LEN), F32)
     vt_ref[...] = jnp.concatenate([qkv[2 * DS :].reshape(SIDE_HEADS, 8, ROW_LEN), ones], axis=1).reshape(2 * DS, ROW_LEN).astype(BF)
     middle_ahead(ctx_ref, turned_ref, 1)
@@ -439,7 +433,7 @@
     def key_step(n):
         half, h = blocks[n]
         rows = slice(half * HALF, (half + 1) * HALF)
-        dq_ref[own_rows(h, DS), rows] = head_rows(dot(qkvt_ref[pair(0, h), rows], e_ref[n]), h) * (1.0 / LOG2E)
+        dq_ref[own_rows(h, DS), rows] = head_rows(dot(qkvt_ref[pair(0, h), rows], e_ref[n]), h) * root
 
     for n in range(len(blocks) + 3 * LAG_BACK):
         for i, step in enumerate((score_step, query_step, value_step, key_step)):
@@ -602,7 +596,7 @@
             attention_kernel,
             "attention",
             20,
-            [whole((ROW_LEN, D)), next_tile, whole((D,)), pl.BlockSpec(memory_space=pl.ANY)] + [hbm] * 3,
+            [whole((ROW_LEN, D)), next_tile, whole((D,)), whole((3, D, D // 2))] + [whole((D, D // 2))] * 3,
             wide_tile,
             jax.ShapeDtypeStruct((D, tokens), BF),
             [
@@ -612,7 +606,6 @@
                 pltpu.VMEM((2 * HEADS, HALF, HALF), BF),
                 pltpu.VMEM((HALF, HALF), F32),
                 pltpu.VMEM((ROW_LEN, D), BF),
-                pltpu.SemaphoreType.DMA((6,)),
             ],
         )(first, lens, turned, turned, attn_gain, joined, *far_attn)
         side_tile = pl.BlockSpec((DS, ROW_LEN), lambda r, *_: (0, r))

time: 119 us -> 119 us (level)
  no operation moved by 1% of the time
where the time goes in v6:
time: 119 us
  Pallas kernels  88 us (74%)
  starting transfers between devices  14.8 us (12%)
  waiting for transfers between devices  14.5 us (12%)
    pallas_call x1, Pallas kernels, body(): kernel(side_kernel, 'forward_and_back', 32, [whole((D, ROW_LEN)), whole((...  62.1 us
    pallas_call x1, Pallas kernels, body(): kernel(attention_kernel, 'attention', 20, [whole((ROW_LEN, D)), next_tile...  20.7 us
    ppermute x8, starting transfers between devices, trade(): return lax.ppermute(x, 'batch', [(i, i ^ bits) for i in range(batch)])  12.6 us
    ppermute x8, waiting for transfers between devices, trade(): return lax.ppermute(x, 'batch', [(i, i ^ bits) for i in range(batch)])  12 us
    pallas_call x1, Pallas kernels, body(): kernel(turn_kernel, 'turn_rows', 11, [hbm] * 4, [tile, pl.BlockSpec(memor...  4.23 us
    ppermute x8, waiting for transfers between devices, swap(): return lax.ppermute(x, 'tensor', [(0, 1), (1, 0)])  2.51 us
  transfers between devices with their start and end apart: 16, of which 10 were waited for; matrix products, arithmetic and copies ran while one was open for 0% of the time, Pallas kernels for 21%

profile of v6, /device:TPU:0, one launch (start us, length us, event | category | flops | bytes accessed | tf_op | source)
XLA Modules:
  0.0 118.6 jit_solution(9745454517115413971)
XLA Ops:
  0.6 0.5 collective-permute-start
  1.2 0.1 collective-permute-start.1
  1.2 0.4 collective-permute-start.2
  1.7 4.2 %turn_rows.1 = (bf16[2560,768]{1,0:T(8,128)(2,1)S(1)}, bf16[3,768,384]{2,1,0:T(8,128)(2,1)S(1)}) custom-call(s32[1]{0:T(128)} %bitcast.first_ref.tensor_ref, s32[8,10]{1,0:T(8,128)} %bitcast.14, bf16[2560,768]{1,0:T(8,128)(2,1)} %x_ref.1, bf16[768,384]{1,0:T(8,128)(2,1)} %wq_ref.1, bf16[768,384]{1,0:T(8,128)(2,1)} %wk_ref.1, bf16[768,384]{1,0:T(8,128)(2,1)} %wv_ref.1), custom_call_target="tpu_custom_call" | custom-call | tf_op jit(solution)/shard_map/turn_rows/pallas_call | solution.py:577
  6.0 0.1 collective-permute-start.4
  6.1 0.4 collective-permute-start.5
  6.5 0.1 collective-permute-start.3
  6.7 0.0 copy-start.8
  6.7 0.0 copy-start.9
  6.8 20.7 %attention.1.ctx0_ref.ctx_ref = bf16[768,2560]{1,0:T(8,128)(2,1)S(1)} custom-call(s32[1]{0:T(128)} %bitcast.first_ref.tensor_ref, s32[8,10]{1,0:T(8,128)} %bitcast.15, bf16[2560,768]{1,0:T(8,128)(2,1)S(1)} %get-tuple-element.38.turned0_ref.turned_ref, bf16[2560,768]{1,0:T(8,128)(2,1)S(1)} %get-tuple-element.38.turned0_ref.turned_ref, f32[768]{0:T(1024)} %gain_ref.1, ...), custom_call_target="tpu_custom_call" | custom-call | tf_op jit(solution)/shard_map/attention/pallas_call | solution.py:595
  27.7 62.1 %forward_and_back.1 = (bf16[2560,768]{1,0:T(8,128)(2,1)}, f32[96,2560]{1,0:T(8,128)}, f32[96,2560]{1,0:T(8,128)}, bf16[48,2048]{1,0:T(8,128)(2,1)S(1)}, bf16[48,2048]{1,0:T(8,128)(2,1)S(1)}) custom-call(s32[1]{0:T(128)} %bitcast.first_ref.tensor_ref, s32[8,10]{1,0:T(8,128)} %bitcast.16, bf16[768,2560]{1,0:T(8,128)(2,1)S(1)} %attention.1.ctx0_ref.ctx_ref, ...), custom_call_target="tpu_custom_call" | custom-call | tf_op jit(solution)/shard_map/forward_and_back/pallas_call | solution.py:614
  89.8 0.4 collective-permute-start.6
  90.2 1.1 collective-permute-done.6
  91.3 2.9 %collective-permute-start.7 = (bf16[48,512]{1,0:T(8,128)(2,1)S(1)}, bf16[48,512]{1,0:T(8,128)(2,1)S(1)}, u32[]{:S(2)}, u32[]{:S(2)}) collective-permute-start(bf16[48,512]{1,0:T(8,128)(2,1)S(1)} %get-tuple-element.65), channel_id=1, source_target_pairs={{0,2},{2,0},{4,6},{6,4},{8,10},{10,8},{12,14},{14,12},{16,18},{18,... | collective-permute-start | bytes 147464 | tf_op jit(solution)/shard_map/ppermute | solution.py:485
  94.3 1.5 %collective-permute-start.8 = (bf16[48,512]{1,0:T(8,128)(2,1)S(1)}, bf16[48,512]{1,0:T(8,128)(2,1)S(1)}, u32[]{:S(2)}, u32[]{:S(2)}) collective-permute-start(bf16[48,512]{1,0:T(8,128)(2,1)S(1)} %get-tuple-element.66), channel_id=1, source_target_pairs={{0,4},{2,6},{4,0},{6,2},{8,12},{10,14},{12,8},{14,10},{16,20},{18,... | collective-permute-start | bytes 147464 | tf_op jit(solution)/shard_map/ppermute | solution.py:485
  95.8 0.1 collective-permute-start.9
  95.9 0.4 collective-permute-done.7
  96.3 2.0 %collective-permute-done.8 = bf16[48,512]{1,0:T(8,128)(2,1)S(1)} collective-permute-done((bf16[48,512]{1,0:T(8,128)(2,1)S(1)}, bf16[48,512]{1,0:T(8,128)(2,1)S(1)}, u32[]{:S(2)}, u32[]{:S(2)}) %collective-permute-start.8) | collective-permute-done | bytes 49184 | tf_op jit(solution)/shard_map/ppermute | solution.py:485
  98.4 2.5 %collective-permute-done.9 = bf16[48,512]{1,0:T(8,128)(2,1)S(1)} collective-permute-done((bf16[48,512]{1,0:T(8,128)(2,1)S(1)}, bf16[48,512]{1,0:T(8,128)(2,1)S(1)}, u32[]{:S(2)}, u32[]{:S(2)}) %collective-permute-start.9) | collective-permute-done | bytes 49184 | tf_op jit(solution)/shard_map/ppermute | solution.py:485
  100.9 1.6 %collective-permute-start.10 = (bf16[48,512]{1,0:T(8,128)(2,1)S(1)}, bf16[48,512]{1,0:T(8,128)(2,1)S(1)}, u32[]{:S(2)}, u32[]{:S(2)}) collective-permute-start(bf16[48,512]{1,0:T(8,128)(2,1)S(1)} %add_convert_fusion.3), channel_id=1, source_target_pairs={{0,8},{2,10},{4,12},{6,14},{8,0},{10,2},{12,4},{14,6},{16,24},{18,... | collective-permute-start | bytes 147464 | tf_op jit(solution)/shard_map/ppermute | solution.py:485
  102.6 2.5 %collective-permute-done.10 = bf16[48,512]{1,0:T(8,128)(2,1)S(1)} collective-permute-done((bf16[48,512]{1,0:T(8,128)(2,1)S(1)}, bf16[48,512]{1,0:T(8,128)(2,1)S(1)}, u32[]{:S(2)}, u32[]{:S(2)}) %collective-permute-start.10) | collective-permute-done | bytes 49184 | tf_op jit(solution)/shard_map/ppermute | solution.py:485
  105.1 2.9 %collective-permute-start.11 = (bf16[48,512]{1,0:T(8,128)(2,1)S(1)}, bf16[48,512]{1,0:T(8,128)(2,1)S(1)}, u32[]{:S(2)}, u32[]{:S(2)}) collective-permute-start(bf16[48,512]{1,0:T(8,128)(2,1)S(1)} %add_convert_fusion.2), channel_id=1, source_target_pairs={{0,16},{2,18},{4,20},{6,22},{8,24},{10,26},{12,28},{14,30},{16,0},... | collective-permute-start | bytes 147464 | tf_op jit(solution)/shard_map/ppermute | solution.py:485
  108.0 2.2 %collective-permute-done.11 = bf16[48,512]{1,0:T(8,128)(2,1)S(1)} collective-permute-done((bf16[48,512]{1,0:T(8,128)(2,1)S(1)}, bf16[48,512]{1,0:T(8,128)(2,1)S(1)}, u32[]{:S(2)}, u32[]{:S(2)}) %collective-permute-start.11) | collective-permute-done | bytes 49184 | tf_op jit(solution)/shard_map/ppermute | solution.py:485
  110.2 0.6 collective-permute-start.12
  110.8 0.3 collective-permute-start.13
  111.1 2.6 %collective-permute-start.14 = (bf16[48,512]{1,0:T(8,128)(2,1)S(1)}, bf16[48,512]{1,0:T(8,128)(2,1)S(1)}, u32[]{:S(2)}, u32[]{:S(2)}) collective-permute-start(bf16[48,512]{1,0:T(8,128)(2,1)S(1)} %add_convert_fusion.1), channel_id=1, source_target_pairs={{0,6},{2,4},{4,2},{6,0},{8,14},{10,12},{12,10},{14,8},{16,22},{18,... | collective-permute-start | bytes 147464 | tf_op jit(solution)/shard_map/ppermute | solution.py:485
  113.7 0.6 collective-permute-done.12
  114.3 0.5 collective-permute-done.13
  114.8 1.2 %collective-permute-done.14 = bf16[48,512]{1,0:T(8,128)(2,1)S(1)} collective-permute-done((bf16[48,512]{1,0:T(8,128)(2,1)S(1)}, bf16[48,512]{1,0:T(8,128)(2,1)S(1)}, u32[]{:S(2)}, u32[]{:S(2)}) %collective-permute-start.14) | collective-permute-done | bytes 49184 | tf_op jit(solution)/shard_map/ppermute | solution.py:485
  116.1 0.1 collective-permute-start.15
  116.2 1.4 %collective-permute-done.15.got_ref = bf16[48,2048]{1,0:T(8,128)(2,1)S(1)} collective-permute-done((bf16[48,2048]{1,0:T(8,128)(2,1)S(1)}, bf16[48,2048]{1,0:T(8,128)(2,1)S(1)}, u32[]{:S(2)}, u32[]{:S(2)}) %collective-permute-start.15) | collective-permute-done | bytes 196640 | tf_op jit(solution)/shard_map/ppermute | solution.py:477
  117.6 0.9 unpack.1
  (44 shorter events, 0.3 us)
Async XLA Ops:
  0.6 5.3 %collective-permute-start = (bf16[768,384]{1,0:T(8,128)(2,1)}, bf16[768,384]{1,0:T(8,128)(2,1)S(1)}, u32[]{:S(2)}, u32[]{:S(2)}) collective-permute-start(bf16[768,384]{1,0:T(8,128)(2,1)} %wq_ref.1), channel_id=1, source_target_pairs={{0,1},{1,0},{2,3},{3,2},{4,5},{5,4},{6,7},{7,6},{8,9},{9,8},{10,11... | collective-permute-start | bytes 1769480 | tf_op jit(solution)/shard_map/ppermute | solution.py:477
  1.2 4.8 %collective-permute-start.1 = (bf16[768,384]{1,0:T(8,128)(2,1)}, bf16[768,384]{1,0:T(8,128)(2,1)S(1)}, u32[]{:S(2)}, u32[]{:S(2)}) collective-permute-start(bf16[768,384]{1,0:T(8,128)(2,1)} %wk_ref.1), channel_id=1, source_target_pairs={{0,1},{1,0},{2,3},{3,2},{4,5},{5,4},{6,7},{7,6},{8,9},{9,8},{10,11... | collective-permute-start | bytes 1769480 | tf_op jit(solution)/shard_map/ppermute | solution.py:477
  1.2 4.7 %collective-permute-start.2 = (bf16[768,384]{1,0:T(8,128)(2,1)}, bf16[768,384]{1,0:T(8,128)(2,1)S(1)}, u32[]{:S(2)}, u32[]{:S(2)}) collective-permute-start(bf16[768,384]{1,0:T(8,128)(2,1)} %wv_ref.1), channel_id=1, source_target_pairs={{0,1},{1,0},{2,3},{3,2},{4,5},{5,4},{6,7},{7,6},{8,9},{9,8},{10,11... | collective-permute-start | bytes 1769480 | tf_op jit(solution)/shard_map/ppermute | solution.py:477
  1.7 4.3 %copy-start = (bf16[768,1536]{1,0:T(8,128)(2,1)S(1)}, bf16[768,1536]{1,0:T(8,128)(2,1)}, u32[]{:S(2)}) copy-start(bf16[768,1536]{1,0:T(8,128)(2,1)} %w1a_ref) | copy-start | bytes 7077892
  1.7 4.4 %copy-start.1 = (bf16[1536,768]{1,0:T(8,128)(2,1)S(1)}, bf16[1536,768]{1,0:T(8,128)(2,1)}, u32[]{:S(2)}) copy-start(bf16[1536,768]{1,0:T(8,128)(2,1)} %w2a_ref) | copy-start | bytes 7077892
  1.7 4.9 %copy-start.2 = (bf16[384,768]{1,0:T(8,128)(2,1)S(1)}, bf16[384,768]{1,0:T(8,128)(2,1)}, u32[]{:S(2)}) copy-start(bf16[384,768]{1,0:T(8,128)(2,1)} %woa_ref) | copy-start | bytes 1769476
  6.0 21.6 %collective-permute-start.4 = (bf16[768,1536]{1,0:T(8,128)(2,1)S(1)}, bf16[768,1536]{1,0:T(8,128)(2,1)S(1)}, u32[]{:S(2)}, u32[]{:S(2)}) collective-permute-start(bf16[768,1536]{1,0:T(8,128)(2,1)S(1)} %copy-done), channel_id=1, source_target_pairs={{0,1},{1,0},{2,3},{3,2},{4,5},{5,4},{6,7},{7,6},{8,9},{9,8},{10,11... | collective-permute-start | bytes 7077896 | tf_op jit(solution)/shard_map/ppermute | solution.py:477
  6.1 21.4 %collective-permute-start.5 = (bf16[1536,768]{1,0:T(8,128)(2,1)S(1)}, bf16[1536,768]{1,0:T(8,128)(2,1)S(1)}, u32[]{:S(2)}, u32[]{:S(2)}) collective-permute-start(bf16[1536,768]{1,0:T(8,128)(2,1)S(1)} %copy-done.1), channel_id=1, source_target_pairs={{0,1},{1,0},{2,3},{3,2},{4,5},{5,4},{6,7},{7,6},{8,9},{9,8},{10,11... | collective-permute-start | bytes 7077896 | tf_op jit(solution)/shard_map/ppermute | solution.py:477
  6.5 21.0 %collective-permute-start.3 = (bf16[384,768]{1,0:T(8,128)(2,1)S(1)}, bf16[384,768]{1,0:T(8,128)(2,1)S(1)}, u32[]{:S(2)}, u32[]{:S(2)}) collective-permute-start(bf16[384,768]{1,0:T(8,128)(2,1)S(1)} %copy-done.2), channel_id=1, source_target_pairs={{0,1},{1,0},{2,3},{3,2},{4,5},{5,4},{6,7},{7,6},{8,9},{9,8},{10,11... | collective-permute-start | bytes 1769480 | tf_op jit(solution)/shard_map/ppermute | solution.py:477
  6.6 20.9 %copy-start.3 = (bf16[2560,96]{0,1:T(8,128)(2,1)S(1)}, bf16[2560,96]{0,1:T(8,128)(2,1)}, u32[]{:S(2)}) copy-start(bf16[2560,96]{0,1:T(8,128)(2,1)} %param.32) | copy-start | bytes 1474564
  6.6 20.9 %copy-start.4 = (bf16[2560,96]{0,1:T(8,128)(2,1)S(1)}, bf16[2560,96]{0,1:T(8,128)(2,1)}, u32[]{:S(2)}) copy-start(bf16[2560,96]{0,1:T(8,128)(2,1)} %param.43) | copy-start | bytes 1474564
  6.6 20.9 %copy-start.5 = (bf16[768,96]{0,1:T(8,128)(2,1)S(1)}, bf16[768,96]{0,1:T(8,128)(2,1)}, u32[]{:S(2)}) copy-start(bf16[768,96]{0,1:T(8,128)(2,1)} %param.34) | copy-start | bytes 442372
  6.6 20.9 %copy-start.6 = (bf16[96,384]{1,0:T(8,128)(2,1)S(1)}, bf16[96,384]{1,0:T(8,128)(2,1)}, u32[]{:S(2)}) copy-start(bf16[96,384]{1,0:T(8,128)(2,1)} %expand_ref.1) | copy-start | bytes 221188
  6.6 20.9 %copy-start.7 = (bf16[384,96]{0,1:T(8,128)(2,1)S(1)}, bf16[384,96]{0,1:T(8,128)(2,1)}, u32[]{:S(2)}) copy-start(bf16[384,96]{0,1:T(8,128)(2,1)} %param.42) | copy-start | bytes 221188
  6.7 20.9 %copy-start.8 = (bf16[96,96]{1,0:T(8,128)(2,1)S(1)}, bf16[96,96]{1,0:T(8,128)(2,1)}, u32[]{:S(2)}) copy-start(bf16[96,96]{1,0:T(8,128)(2,1)} %sq_ref.1) | copy-start | bytes 55300
  6.7 20.9 %copy-start.9 = (bf16[96,96]{1,0:T(8,128)(2,1)S(1)}, bf16[96,96]{1,0:T(8,128)(2,1)}, u32[]{:S(2)}) copy-start(bf16[96,96]{1,0:T(8,128)(2,1)} %sk_ref.1) | copy-start | bytes 55300
  6.7 20.9 %copy-start.10 = (bf16[96,96]{1,0:T(8,128)(2,1)S(1)}, bf16[96,96]{1,0:T(8,128)(2,1)}, u32[]{:S(2)}) copy-start(bf16[96,96]{1,0:T(8,128)(2,1)} %sv_ref.1) | copy-start | bytes 55300
  6.7 20.9 %copy-start.11 = (bf16[96,96]{1,0:T(8,128)(2,1)S(1)}, bf16[96,96]{1,0:T(8,128)(2,1)}, u32[]{:S(2)}) copy-start(bf16[96,96]{1,0:T(8,128)(2,1)} %proj_ref.1) | copy-start | bytes 55300
  6.7 20.9 %copy-start.12 = (f32[768]{0:T(1024)S(1)}, f32[768]{0:T(1024)}, u32[]{:S(2)}) copy-start(f32[768]{0:T(1024)} %fgain_ref.1) | copy-start | bytes 9220
  6.7 20.9 %copy-start.13 = (f32[96]{0:T(128)S(1)}, f32[96]{0:T(128)}, u32[]{:S(2)}) copy-start(f32[96]{0:T(128)} %alpha_ref.1) | copy-start | bytes 1156
  6.7 20.9 %copy-start.14 = (f32[96]{0:T(128)S(1)}, f32[96]{0:T(128)}, u32[]{:S(2)}) copy-start(f32[96]{0:T(128)} %gain1_ref.1) | copy-start | bytes 1156
  6.7 20.9 %copy-start.15 = (f32[96]{0:T(128)S(1)}, f32[96]{0:T(128)}, u32[]{:S(2)}) copy-start(f32[96]{0:T(128)} %gain2_ref.1) | copy-start | bytes 1156
  89.8 1.5 %collective-permute-start.6 = (bf16[48,2048]{1,0:T(8,128)(2,1)S(1)}, bf16[48,2048]{1,0:T(8,128)(2,1)S(1)}, u32[]{:S(2)}, u32[]{:S(2)}) collective-permute-start(bf16[48,2048]{1,0:T(8,128)(2,1)S(1)} %get-tuple-element.50), channel_id=1, source_target_pairs={{0,1},{1,0},{2,3},{3,2},{4,5},{5,4},{6,7},{7,6},{8,9},{9,8},{10,11... | collective-permute-start | bytes 589832 | tf_op jit(solution)/shard_map/ppermute | solution.py:477
  91.3 5.0 %collective-permute-start.7 = (bf16[48,512]{1,0:T(8,128)(2,1)S(1)}, bf16[48,512]{1,0:T(8,128)(2,1)S(1)}, u32[]{:S(2)}, u32[]{:S(2)}) collective-permute-start(bf16[48,512]{1,0:T(8,128)(2,1)S(1)} %get-tuple-element.65), channel_id=1, source_target_pairs={{0,2},{2,0},{4,6},{6,4},{8,10},{10,8},{12,14},{14,12},{16,18},{18,... | collective-permute-start | bytes 147464 | tf_op jit(solution)/shard_map/ppermute | solution.py:485
  94.3 4.1 %collective-permute-start.8 = (bf16[48,512]{1,0:T(8,128)(2,1)S(1)}, bf16[48,512]{1,0:T(8,128)(2,1)S(1)}, u32[]{:S(2)}, u32[]{:S(2)}) collective-permute-start(bf16[48,512]{1,0:T(8,128)(2,1)S(1)} %get-tuple-element.66), channel_id=1, source_target_pairs={{0,4},{2,6},{4,0},{6,2},{8,12},{10,14},{12,8},{14,10},{16,20},{18,... | collective-permute-start | bytes 147464 | tf_op jit(solution)/shard_map/ppermute | solution.py:485
  95.8 5.1 %collective-permute-start.9 = (bf16[48,512]{1,0:T(8,128)(2,1)S(1)}, bf16[48,512]{1,0:T(8,128)(2,1)S(1)}, u32[]{:S(2)}, u32[]{:S(2)}) collective-permute-start(bf16[48,512]{1,0:T(8,128)(2,1)S(1)} %select_select_fusion.4), channel_id=1, source_target_pairs={{0,6},{2,4},{4,2},{6,0},{8,14},{10,12},{12,10},{14,8},{16,22},{18,... | collective-permute-start | bytes 147464 | tf_op jit(solution)/shard_map/ppermute | solution.py:485
  100.9 4.2 %collective-permute-start.10 = (bf16[48,512]{1,0:T(8,128)(2,1)S(1)}, bf16[48,512]{1,0:T(8,128)(2,1)S(1)}, u32[]{:S(2)}, u32[]{:S(2)}) collective-permute-start(bf16[48,512]{1,0:T(8,128)(2,1)S(1)} %add_convert_fusion.3), channel_id=1, source_target_pairs={{0,8},{2,10},{4,12},{6,14},{8,0},{10,2},{12,4},{14,6},{16,24},{18,... | collective-permute-start | bytes 147464 | tf_op jit(solution)/shard_map/ppermute | solution.py:485
  105.1 5.1 %collective-permute-start.11 = (bf16[48,512]{1,0:T(8,128)(2,1)S(1)}, bf16[48,512]{1,0:T(8,128)(2,1)S(1)}, u32[]{:S(2)}, u32[]{:S(2)}) collective-permute-start(bf16[48,512]{1,0:T(8,128)(2,1)S(1)} %add_convert_fusion.2), channel_id=1, source_target_pairs={{0,16},{2,18},{4,20},{6,22},{8,24},{10,26},{12,28},{14,30},{16,0},... | collective-permute-start | bytes 147464 | tf_op jit(solution)/shard_map/ppermute | solution.py:485
  110.2 4.2 %collective-permute-start.12 = (bf16[48,512]{1,0:T(8,128)(2,1)S(1)}, bf16[48,512]{1,0:T(8,128)(2,1)S(1)}, u32[]{:S(2)}, u32[]{:S(2)}) collective-permute-start(bf16[48,512]{1,0:T(8,128)(2,1)S(1)} %add_convert_fusion.1), channel_id=1, source_target_pairs={{0,2},{2,0},{4,6},{6,4},{8,10},{10,8},{12,14},{14,12},{16,18},{18,... | collective-permute-start | bytes 147464 | tf_op jit(solution)/shard_map/ppermute | solution.py:485
  110.8 4.1 %collective-permute-start.13 = (bf16[48,512]{1,0:T(8,128)(2,1)S(1)}, bf16[48,512]{1,0:T(8,128)(2,1)S(1)}, u32[]{:S(2)}, u32[]{:S(2)}) collective-permute-start(bf16[48,512]{1,0:T(8,128)(2,1)S(1)} %add_convert_fusion.1), channel_id=1, source_target_pairs={{0,4},{2,6},{4,0},{6,2},{8,12},{10,14},{12,8},{14,10},{16,20},{18,... | collective-permute-start | bytes 147464 | tf_op jit(solution)/shard_map/ppermute | solution.py:485
  111.1 5.0 %collective-permute-start.14 = (bf16[48,512]{1,0:T(8,128)(2,1)S(1)}, bf16[48,512]{1,0:T(8,128)(2,1)S(1)}, u32[]{:S(2)}, u32[]{:S(2)}) collective-permute-start(bf16[48,512]{1,0:T(8,128)(2,1)S(1)} %add_convert_fusion.1), channel_id=1, source_target_pairs={{0,6},{2,4},{4,2},{6,0},{8,14},{10,12},{12,10},{14,8},{16,22},{18,... | collective-permute-start | bytes 147464 | tf_op jit(solution)/shard_map/ppermute | solution.py:485
  116.1 1.5 %collective-permute-start.15 = (bf16[48,2048]{1,0:T(8,128)(2,1)S(1)}, bf16[48,2048]{1,0:T(8,128)(2,1)S(1)}, u32[]{:S(2)}, u32[]{:S(2)}) collective-permute-start(bf16[48,2048]{1,0:T(8,128)(2,1)S(1)} %pad_maximum_fusion.sent_ref), channel_id=1, source_target_pairs={{0,1},{1,0},{2,3},{3,2},{4,5},{5,4},{6,7},{7,6},{8,9},{9,8},{10,11... | collective-permute-start | bytes 589832 | tf_op jit(solution)/shard_map/ppermute | solution.py:477

commit v7 on v6

--- a/solution.py
+++ b/solution.py
@@ -141,6 +141,9 @@
     @pl.when(r == 0)
     def _():
         start_copies(copies, sems)
+
+    @pl.when(r == min(1, rows - 1))
+    def _():
         start_copies(joins, joined_sems)
 
     pltpu.make_async_copy(x_ref.at[pl.ds(pl.multiple_of(r * ROW_LEN, ROW_LEN), ROW_LEN)], held_ref.at[r], sems.at[r]).wait()

time: 119 us -> 119 us (level)
  no operation moved by 1% of the time
where the time goes in v7:
time: 119 us
  Pallas kernels  88.2 us (74%)
  starting transfers between devices  14.8 us (12%)
  waiting for transfers between devices  14.5 us (12%)
    pallas_call x1, Pallas kernels, body(): kernel(side_kernel, 'forward_and_back', 32, [whole((D, ROW_LEN)), whole((...  62.1 us
    pallas_call x1, Pallas kernels, body(): kernel(attention_kernel, 'attention', 20, [whole((ROW_LEN, D)), next_tile...  20.7 us
    ppermute x8, starting transfers between devices, trade(): return lax.ppermute(x, 'batch', [(i, i ^ bits) for i in range(batch)])  12.6 us
    ppermute x8, waiting for transfers between devices, trade(): return lax.ppermute(x, 'batch', [(i, i ^ bits) for i in range(batch)])  12 us
    pallas_call x1, Pallas kernels, body(): kernel(turn_kernel, 'turn_rows', 11, [hbm] * 4, [tile, pl.BlockSpec(memor...  4.41 us
    ppermute x8, waiting for transfers between devices, swap(): return lax.ppermute(x, 'tensor', [(0, 1), (1, 0)])  2.51 us
  transfers between devices with their start and end apart: 16, of which 10 were waited for; matrix products, arithmetic and copies ran while one was open for 0% of the time, Pallas kernels for 21%

profile of v7, /device:TPU:0, one launch (start us, length us, event | category | flops | bytes accessed | tf_op | source)
XLA Modules:
  0.0 118.8 jit_solution(16146035473249824384)
XLA Ops:
  0.6 0.5 collective-permute-start
  1.2 0.1 collective-permute-start.1
  1.2 0.4 collective-permute-start.2
  1.7 4.4 %turn_rows.1 = (bf16[2560,768]{1,0:T(8,128)(2,1)S(1)}, bf16[3,768,384]{2,1,0:T(8,128)(2,1)S(1)}) custom-call(s32[1]{0:T(128)} %bitcast.first_ref.tensor_ref, s32[8,10]{1,0:T(8,128)} %bitcast.14, bf16[2560,768]{1,0:T(8,128)(2,1)} %x_ref.1, bf16[768,384]{1,0:T(8,128)(2,1)} %wq_ref.1, bf16[768,384]{1,0:T(8,128)(2,1)} %wk_ref.1, bf16[768,384]{1,0:T(8,128)(2,1)} %wv_ref.1), custom_call_target="tpu_custom_call" | custom-call | tf_op jit(solution)/shard_map/turn_rows/pallas_call | solution.py:580
  6.1 0.1 collective-permute-start.4
  6.3 0.4 collective-permute-start.5
  6.7 0.1 collective-permute-start.3
  6.8 0.0 copy-start.7
  6.8 0.0 copy-start.8
  6.9 20.7 %attention.1.ctx0_ref.ctx_ref = bf16[768,2560]{1,0:T(8,128)(2,1)S(1)} custom-call(s32[1]{0:T(128)} %bitcast.first_ref.tensor_ref, s32[8,10]{1,0:T(8,128)} %bitcast.15, bf16[2560,768]{1,0:T(8,128)(2,1)S(1)} %get-tuple-element.38.turned0_ref.turned_ref, bf16[2560,768]{1,0:T(8,128)(2,1)S(1)} %get-tuple-element.38.turned0_ref.turned_ref, f32[768]{0:T(1024)} %gain_ref.1, ...), custom_call_target="tpu_custom_call" | custom-call | tf_op jit(solution)/shard_map/attention/pallas_call | solution.py:598
  27.8 62.1 %forward_and_back.1 = (bf16[2560,768]{1,0:T(8,128)(2,1)}, f32[96,2560]{1,0:T(8,128)}, f32[96,2560]{1,0:T(8,128)}, bf16[48,2048]{1,0:T(8,128)(2,1)S(1)}, bf16[48,2048]{1,0:T(8,128)(2,1)S(1)}) custom-call(s32[1]{0:T(128)} %bitcast.first_ref.tensor_ref, s32[8,10]{1,0:T(8,128)} %bitcast.16, bf16[768,2560]{1,0:T(8,128)(2,1)S(1)} %attention.1.ctx0_ref.ctx_ref, ...), custom_call_target="tpu_custom_call" | custom-call | tf_op jit(solution)/shard_map/forward_and_back/pallas_call | solution.py:617
  89.9 0.4 collective-permute-start.6
  90.4 1.1 collective-permute-done.6
  91.5 2.9 %collective-permute-start.7 = (bf16[48,512]{1,0:T(8,128)(2,1)S(1)}, bf16[48,512]{1,0:T(8,128)(2,1)S(1)}, u32[]{:S(2)}, u32[]{:S(2)}) collective-permute-start(bf16[48,512]{1,0:T(8,128)(2,1)S(1)} %get-tuple-element.65), channel_id=1, source_target_pairs={{0,2},{2,0},{4,6},{6,4},{8,10},{10,8},{12,14},{14,12},{16,18},{18,... | collective-permute-start | bytes 147464 | tf_op jit(solution)/shard_map/ppermute | solution.py:488
  94.4 1.5 %collective-permute-start.8 = (bf16[48,512]{1,0:T(8,128)(2,1)S(1)}, bf16[48,512]{1,0:T(8,128)(2,1)S(1)}, u32[]{:S(2)}, u32[]{:S(2)}) collective-permute-start(bf16[48,512]{1,0:T(8,128)(2,1)S(1)} %get-tuple-element.66), channel_id=1, source_target_pairs={{0,4},{2,6},{4,0},{6,2},{8,12},{10,14},{12,8},{14,10},{16,20},{18,... | collective-permute-start | bytes 147464 | tf_op jit(solution)/shard_map/ppermute | solution.py:488
  96.0 0.1 collective-permute-start.9
  96.1 0.4 collective-permute-done.7
  96.5 2.0 %collective-permute-done.8 = bf16[48,512]{1,0:T(8,128)(2,1)S(1)} collective-permute-done((bf16[48,512]{1,0:T(8,128)(2,1)S(1)}, bf16[48,512]{1,0:T(8,128)(2,1)S(1)}, u32[]{:S(2)}, u32[]{:S(2)}) %collective-permute-start.8) | collective-permute-done | bytes 49184 | tf_op jit(solution)/shard_map/ppermute | solution.py:488
  98.5 2.5 %collective-permute-done.9 = bf16[48,512]{1,0:T(8,128)(2,1)S(1)} collective-permute-done((bf16[48,512]{1,0:T(8,128)(2,1)S(1)}, bf16[48,512]{1,0:T(8,128)(2,1)S(1)}, u32[]{:S(2)}, u32[]{:S(2)}) %collective-permute-start.9) | collective-permute-done | bytes 49184 | tf_op jit(solution)/shard_map/ppermute | solution.py:488
  101.1 1.6 %collective-permute-start.10 = (bf16[48,512]{1,0:T(8,128)(2,1)S(1)}, bf16[48,512]{1,0:T(8,128)(2,1)S(1)}, u32[]{:S(2)}, u32[]{:S(2)}) collective-permute-start(bf16[48,512]{1,0:T(8,128)(2,1)S(1)} %add_convert_fusion.3), channel_id=1, source_target_pairs={{0,8},{2,10},{4,12},{6,14},{8,0},{10,2},{12,4},{14,6},{16,24},{18,... | collective-permute-start | bytes 147464 | tf_op jit(solution)/shard_map/ppermute | solution.py:488
  102.7 2.5 %collective-permute-done.10 = bf16[48,512]{1,0:T(8,128)(2,1)S(1)} collective-permute-done((bf16[48,512]{1,0:T(8,128)(2,1)S(1)}, bf16[48,512]{1,0:T(8,128)(2,1)S(1)}, u32[]{:S(2)}, u32[]{:S(2)}) %collective-permute-start.10) | collective-permute-done | bytes 49184 | tf_op jit(solution)/shard_map/ppermute | solution.py:488
  105.3 2.9 %collective-permute-start.11 = (bf16[48,512]{1,0:T(8,128)(2,1)S(1)}, bf16[48,512]{1,0:T(8,128)(2,1)S(1)}, u32[]{:S(2)}, u32[]{:S(2)}) collective-permute-start(bf16[48,512]{1,0:T(8,128)(2,1)S(1)} %add_convert_fusion.2), channel_id=1, source_target_pairs={{0,16},{2,18},{4,20},{6,22},{8,24},{10,26},{12,28},{14,30},{16,0},... | collective-permute-start | bytes 147464 | tf_op jit(solution)/shard_map/ppermute | solution.py:488
  108.2 2.1 %collective-permute-done.11 = bf16[48,512]{1,0:T(8,128)(2,1)S(1)} collective-permute-done((bf16[48,512]{1,0:T(8,128)(2,1)S(1)}, bf16[48,512]{1,0:T(8,128)(2,1)S(1)}, u32[]{:S(2)}, u32[]{:S(2)}) %collective-permute-start.11) | collective-permute-done | bytes 49184 | tf_op jit(solution)/shard_map/ppermute | solution.py:488
  110.3 0.6 collective-permute-start.12
  110.9 0.3 collective-permute-start.13
  111.2 2.6 %collective-permute-start.14 = (bf16[48,512]{1,0:T(8,128)(2,1)S(1)}, bf16[48,512]{1,0:T(8,128)(2,1)S(1)}, u32[]{:S(2)}, u32[]{:S(2)}) collective-permute-start(bf16[48,512]{1,0:T(8,128)(2,1)S(1)} %add_convert_fusion.1), channel_id=1, source_target_pairs={{0,6},{2,4},{4,2},{6,0},{8,14},{10,12},{12,10},{14,8},{16,22},{18,... | collective-permute-start | bytes 147464 | tf_op jit(solution)/shard_map/ppermute | solution.py:488
  113.9 0.6 collective-permute-done.12
  114.5 0.5 collective-permute-done.13
  115.0 1.2 %collective-permute-done.14 = bf16[48,512]{1,0:T(8,128)(2,1)S(1)} collective-permute-done((bf16[48,512]{1,0:T(8,128)(2,1)S(1)}, bf16[48,512]{1,0:T(8,128)(2,1)S(1)}, u32[]{:S(2)}, u32[]{:S(2)}) %collective-permute-start.14) | collective-permute-done | bytes 49184 | tf_op jit(solution)/shard_map/ppermute | solution.py:488
  116.3 0.1 collective-permute-start.15
  116.4 1.4 %collective-permute-done.15.got_ref = bf16[48,2048]{1,0:T(8,128)(2,1)S(1)} collective-permute-done((bf16[48,2048]{1,0:T(8,128)(2,1)S(1)}, bf16[48,2048]{1,0:T(8,128)(2,1)S(1)}, u32[]{:S(2)}, u32[]{:S(2)}) %collective-permute-start.15) | collective-permute-done | bytes 196640 | tf_op jit(solution)/shard_map/ppermute | solution.py:480
  117.8 0.9 unpack.1
  (44 shorter events, 0.3 us)
Async XLA Ops:
  0.6 5.5 %collective-permute-start = (bf16[768,384]{1,0:T(8,128)(2,1)}, bf16[768,384]{1,0:T(8,128)(2,1)S(1)}, u32[]{:S(2)}, u32[]{:S(2)}) collective-permute-start(bf16[768,384]{1,0:T(8,128)(2,1)} %wq_ref.1), channel_id=1, source_target_pairs={{0,1},{1,0},{2,3},{3,2},{4,5},{5,4},{6,7},{7,6},{8,9},{9,8},{10,11... | collective-permute-start | bytes 1769480 | tf_op jit(solution)/shard_map/ppermute | solution.py:480
  1.2 4.9 %collective-permute-start.1 = (bf16[768,384]{1,0:T(8,128)(2,1)}, bf16[768,384]{1,0:T(8,128)(2,1)S(1)}, u32[]{:S(2)}, u32[]{:S(2)}) collective-permute-start(bf16[768,384]{1,0:T(8,128)(2,1)} %wk_ref.1), channel_id=1, source_target_pairs={{0,1},{1,0},{2,3},{3,2},{4,5},{5,4},{6,7},{7,6},{8,9},{9,8},{10,11... | collective-permute-start | bytes 1769480 | tf_op jit(solution)/shard_map/ppermute | solution.py:480
  1.2 4.9 %collective-permute-start.2 = (bf16[768,384]{1,0:T(8,128)(2,1)}, bf16[768,384]{1,0:T(8,128)(2,1)S(1)}, u32[]{:S(2)}, u32[]{:S(2)}) collective-permute-start(bf16[768,384]{1,0:T(8,128)(2,1)} %wv_ref.1), channel_id=1, source_target_pairs={{0,1},{1,0},{2,3},{3,2},{4,5},{5,4},{6,7},{7,6},{8,9},{9,8},{10,11... | collective-permute-start | bytes 1769480 | tf_op jit(solution)/shard_map/ppermute | solution.py:480
  1.7 4.5 %copy-start = (bf16[768,1536]{1,0:T(8,128)(2,1)S(1)}, bf16[768,1536]{1,0:T(8,128)(2,1)}, u32[]{:S(2)}) copy-start(bf16[768,1536]{1,0:T(8,128)(2,1)} %w1a_ref) | copy-start | bytes 7077892
  1.7 4.6 %copy-start.1 = (bf16[1536,768]{1,0:T(8,128)(2,1)S(1)}, bf16[1536,768]{1,0:T(8,128)(2,1)}, u32[]{:S(2)}) copy-start(bf16[1536,768]{1,0:T(8,128)(2,1)} %w2a_ref) | copy-start | bytes 7077892
  1.7 5.0 %copy-start.2 = (bf16[384,768]{1,0:T(8,128)(2,1)S(1)}, bf16[384,768]{1,0:T(8,128)(2,1)}, u32[]{:S(2)}) copy-start(bf16[384,768]{1,0:T(8,128)(2,1)} %woa_ref) | copy-start | bytes 1769476
  6.1 21.6 %collective-permute-start.4 = (bf16[768,1536]{1,0:T(8,128)(2,1)S(1)}, bf16[768,1536]{1,0:T(8,128)(2,1)S(1)}, u32[]{:S(2)}, u32[]{:S(2)}) collective-permute-start(bf16[768,1536]{1,0:T(8,128)(2,1)S(1)} %copy-done), channel_id=1, source_target_pairs={{0,1},{1,0},{2,3},{3,2},{4,5},{5,4},{6,7},{7,6},{8,9},{9,8},{10,11... | collective-permute-start | bytes 7077896 | tf_op jit(solution)/shard_map/ppermute | solution.py:480
  6.3 21.4 %collective-permute-start.5 = (bf16[1536,768]{1,0:T(8,128)(2,1)S(1)}, bf16[1536,768]{1,0:T(8,128)(2,1)S(1)}, u32[]{:S(2)}, u32[]{:S(2)}) collective-permute-start(bf16[1536,768]{1,0:T(8,128)(2,1)S(1)} %copy-done.1), channel_id=1, source_target_pairs={{0,1},{1,0},{2,3},{3,2},{4,5},{5,4},{6,7},{7,6},{8,9},{9,8},{10,11... | collective-permute-start | bytes 7077896 | tf_op jit(solution)/shard_map/ppermute | solution.py:480
  6.7 21.0 %collective-permute-start.3 = (bf16[384,768]{1,0:T(8,128)(2,1)S(1)}, bf16[384,768]{1,0:T(8,128)(2,1)S(1)}, u32[]{:S(2)}, u32[]{:S(2)}) collective-permute-start(bf16[384,768]{1,0:T(8,128)(2,1)S(1)} %copy-done.2), channel_id=1, source_target_pairs={{0,1},{1,0},{2,3},{3,2},{4,5},{5,4},{6,7},{7,6},{8,9},{9,8},{10,11... | collective-permute-start | bytes 1769480 | tf_op jit(solution)/shard_map/ppermute | solution.py:480
  6.8 20.9 %copy-start.3 = (bf16[2560,96]{0,1:T(8,128)(2,1)S(1)}, bf16[2560,96]{0,1:T(8,128)(2,1)}, u32[]{:S(2)}) copy-start(bf16[2560,96]{0,1:T(8,128)(2,1)} %param.32) | copy-start | bytes 1474564
  6.8 20.9 %copy-start.4 = (bf16[2560,96]{0,1:T(8,128)(2,1)S(1)}, bf16[2560,96]{0,1:T(8,128)(2,1)}, u32[]{:S(2)}) copy-start(bf16[2560,96]{0,1:T(8,128)(2,1)} %param.43) | copy-start | bytes 1474564
  6.8 20.9 %copy-start.5 = (bf16[768,96]{0,1:T(8,128)(2,1)S(1)}, bf16[768,96]{0,1:T(8,128)(2,1)}, u32[]{:S(2)}) copy-start(bf16[768,96]{0,1:T(8,128)(2,1)} %param.34) | copy-start | bytes 442372
  6.8 20.9 %copy-start.6 = (bf16[96,384]{1,0:T(8,128)(2,1)S(1)}, bf16[96,384]{1,0:T(8,128)(2,1)}, u32[]{:S(2)}) copy-start(bf16[96,384]{1,0:T(8,128)(2,1)} %expand_ref.1) | copy-start | bytes 221188
  6.8 20.9 %copy-start.7 = (bf16[384,96]{0,1:T(8,128)(2,1)S(1)}, bf16[384,96]{0,1:T(8,128)(2,1)}, u32[]{:S(2)}) copy-start(bf16[384,96]{0,1:T(8,128)(2,1)} %param.42) | copy-start | bytes 221188
  6.8 20.9 %copy-start.8 = (bf16[96,96]{1,0:T(8,128)(2,1)S(1)}, bf16[96,96]{1,0:T(8,128)(2,1)}, u32[]{:S(2)}) copy-start(bf16[96,96]{1,0:T(8,128)(2,1)} %sq_ref.1) | copy-start | bytes 55300
  6.8 20.9 %copy-start.9 = (bf16[96,96]{1,0:T(8,128)(2,1)S(1)}, bf16[96,96]{1,0:T(8,128)(2,1)}, u32[]{:S(2)}) copy-start(bf16[96,96]{1,0:T(8,128)(2,1)} %sk_ref.1) | copy-start | bytes 55300
  6.9 20.9 %copy-start.10 = (bf16[96,96]{1,0:T(8,128)(2,1)S(1)}, bf16[96,96]{1,0:T(8,128)(2,1)}, u32[]{:S(2)}) copy-start(bf16[96,96]{1,0:T(8,128)(2,1)} %sv_ref.1) | copy-start | bytes 55300
  6.9 20.9 %copy-start.11 = (bf16[96,96]{1,0:T(8,128)(2,1)S(1)}, bf16[96,96]{1,0:T(8,128)(2,1)}, u32[]{:S(2)}) copy-start(bf16[96,96]{1,0:T(8,128)(2,1)} %proj_ref.1) | copy-start | bytes 55300
  6.9 20.9 %copy-start.12 = (f32[768]{0:T(1024)S(1)}, f32[768]{0:T(1024)}, u32[]{:S(2)}) copy-start(f32[768]{0:T(1024)} %fgain_ref.1) | copy-start | bytes 9220
  6.9 20.9 %copy-start.13 = (f32[96]{0:T(128)S(1)}, f32[96]{0:T(128)}, u32[]{:S(2)}) copy-start(f32[96]{0:T(128)} %alpha_ref.1) | copy-start | bytes 1156
  6.9 20.9 %copy-start.14 = (f32[96]{0:T(128)S(1)}, f32[96]{0:T(128)}, u32[]{:S(2)}) copy-start(f32[96]{0:T(128)} %gain1_ref.1) | copy-start | bytes 1156
  6.9 20.9 %copy-start.15 = (f32[96]{0:T(128)S(1)}, f32[96]{0:T(128)}, u32[]{:S(2)}) copy-start(f32[96]{0:T(128)} %gain2_ref.1) | copy-start | bytes 1156
  89.9 1.5 %collective-permute-start.6 = (bf16[48,2048]{1,0:T(8,128)(2,1)S(1)}, bf16[48,2048]{1,0:T(8,128)(2,1)S(1)}, u32[]{:S(2)}, u32[]{:S(2)}) collective-permute-start(bf16[48,2048]{1,0:T(8,128)(2,1)S(1)} %get-tuple-element.50), channel_id=1, source_target_pairs={{0,1},{1,0},{2,3},{3,2},{4,5},{5,4},{6,7},{7,6},{8,9},{9,8},{10,11... | collective-permute-start | bytes 589832 | tf_op jit(solution)/shard_map/ppermute | solution.py:480
  91.5 5.0 %collective-permute-start.7 = (bf16[48,512]{1,0:T(8,128)(2,1)S(1)}, bf16[48,512]{1,0:T(8,128)(2,1)S(1)}, u32[]{:S(2)}, u32[]{:S(2)}) collective-permute-start(bf16[48,512]{1,0:T(8,128)(2,1)S(1)} %get-tuple-element.65), channel_id=1, source_target_pairs={{0,2},{2,0},{4,6},{6,4},{8,10},{10,8},{12,14},{14,12},{16,18},{18,... | collective-permute-start | bytes 147464 | tf_op jit(solution)/shard_map/ppermute | solution.py:488
  94.4 4.1 %collective-permute-start.8 = (bf16[48,512]{1,0:T(8,128)(2,1)S(1)}, bf16[48,512]{1,0:T(8,128)(2,1)S(1)}, u32[]{:S(2)}, u32[]{:S(2)}) collective-permute-start(bf16[48,512]{1,0:T(8,128)(2,1)S(1)} %get-tuple-element.66), channel_id=1, source_target_pairs={{0,4},{2,6},{4,0},{6,2},{8,12},{10,14},{12,8},{14,10},{16,20},{18,... | collective-permute-start | bytes 147464 | tf_op jit(solution)/shard_map/ppermute | solution.py:488
  96.0 5.1 %collective-permute-start.9 = (bf16[48,512]{1,0:T(8,128)(2,1)S(1)}, bf16[48,512]{1,0:T(8,128)(2,1)S(1)}, u32[]{:S(2)}, u32[]{:S(2)}) collective-permute-start(bf16[48,512]{1,0:T(8,128)(2,1)S(1)} %select_select_fusion.4), channel_id=1, source_target_pairs={{0,6},{2,4},{4,2},{6,0},{8,14},{10,12},{12,10},{14,8},{16,22},{18,... | collective-permute-start | bytes 147464 | tf_op jit(solution)/shard_map/ppermute | solution.py:488
  101.1 4.2 %collective-permute-start.10 = (bf16[48,512]{1,0:T(8,128)(2,1)S(1)}, bf16[48,512]{1,0:T(8,128)(2,1)S(1)}, u32[]{:S(2)}, u32[]{:S(2)}) collective-permute-start(bf16[48,512]{1,0:T(8,128)(2,1)S(1)} %add_convert_fusion.3), channel_id=1, source_target_pairs={{0,8},{2,10},{4,12},{6,14},{8,0},{10,2},{12,4},{14,6},{16,24},{18,... | collective-permute-start | bytes 147464 | tf_op jit(solution)/shard_map/ppermute | solution.py:488
  105.3 5.1 %collective-permute-start.11 = (bf16[48,512]{1,0:T(8,128)(2,1)S(1)}, bf16[48,512]{1,0:T(8,128)(2,1)S(1)}, u32[]{:S(2)}, u32[]{:S(2)}) collective-permute-start(bf16[48,512]{1,0:T(8,128)(2,1)S(1)} %add_convert_fusion.2), channel_id=1, source_target_pairs={{0,16},{2,18},{4,20},{6,22},{8,24},{10,26},{12,28},{14,30},{16,0},... | collective-permute-start | bytes 147464 | tf_op jit(solution)/shard_map/ppermute | solution.py:488
  110.3 4.2 %collective-permute-start.12 = (bf16[48,512]{1,0:T(8,128)(2,1)S(1)}, bf16[48,512]{1,0:T(8,128)(2,1)S(1)}, u32[]{:S(2)}, u32[]{:S(2)}) collective-permute-start(bf16[48,512]{1,0:T(8,128)(2,1)S(1)} %add_convert_fusion.1), channel_id=1, source_target_pairs={{0,2},{2,0},{4,6},{6,4},{8,10},{10,8},{12,14},{14,12},{16,18},{18,... | collective-permute-start | bytes 147464 | tf_op jit(solution)/shard_map/ppermute | solution.py:488
  110.9 4.1 %collective-permute-start.13 = (bf16[48,512]{1,0:T(8,128)(2,1)S(1)}, bf16[48,512]{1,0:T(8,128)(2,1)S(1)}, u32[]{:S(2)}, u32[]{:S(2)}) collective-permute-start(bf16[48,512]{1,0:T(8,128)(2,1)S(1)} %add_convert_fusion.1), channel_id=1, source_target_pairs={{0,4},{2,6},{4,0},{6,2},{8,12},{10,14},{12,8},{14,10},{16,20},{18,... | collective-permute-start | bytes 147464 | tf_op jit(solution)/shard_map/ppermute | solution.py:488
  111.2 5.0 %collective-permute-start.14 = (bf16[48,512]{1,0:T(8,128)(2,1)S(1)}, bf16[48,512]{1,0:T(8,128)(2,1)S(1)}, u32[]{:S(2)}, u32[]{:S(2)}) collective-permute-start(bf16[48,512]{1,0:T(8,128)(2,1)S(1)} %add_convert_fusion.1), channel_id=1, source_target_pairs={{0,6},{2,4},{4,2},{6,0},{8,14},{10,12},{12,10},{14,8},{16,22},{18,... | collective-permute-start | bytes 147464 | tf_op jit(solution)/shard_map/ppermute | solution.py:488
  116.3 1.5 %collective-permute-start.15 = (bf16[48,2048]{1,0:T(8,128)(2,1)S(1)}, bf16[48,2048]{1,0:T(8,128)(2,1)S(1)}, u32[]{:S(2)}, u32[]{:S(2)}) collective-permute-start(bf16[48,2048]{1,0:T(8,128)(2,1)S(1)} %pad_maximum_fusion.sent_ref), channel_id=1, source_target_pairs={{0,1},{1,0},{2,3},{3,2},{4,5},{5,4},{6,7},{7,6},{8,9},{9,8},{10,11... | collective-permute-start | bytes 589832 | tf_op jit(solution)/shard_map/ppermute | solution.py:480
